TPU v7x, 512 devices: a whole 4x4x16 slice. The times are simulated.
512 devices in a mesh: trip: 64 (over z, x), virt: 8 (over y, core).
Axes of the slice: x: 4, y: 4, z: 16, core: 2. Of those that a mesh axis runs over, the one named last changes fastest.
Arguments:
- virt_integrals: bfloat16 [64, 2048, 4096], P('trip', 'virt'), may hold values from -6 to 6
- pair_amps: bfloat16 [64, 3, 2, 64, 2048], P('trip', None, None, None, 'virt'), may hold values from -0.0048828125 to 0.0048828125
- hole_amps: bfloat16 [64, 304, 4096], P('trip', 'virt'), may hold values from -0.01171875 to 0.01171875
- coulomb_ints: bfloat16 [64, 3, 304, 64], P('trip', None, 'virt'), may hold values from -6 to 6
- exchange_ints: bfloat16 [64, 3, 4096], P('trip'), may hold values from -2.5 to 2.5
- singles: bfloat16 [64, 64], P('trip'), may hold values from -3 to 3
- occ_energy: bfloat16 [64], P('trip'), may hold values from -3 to -0.29882812
- virt_energy: float32 [64], replicated, may hold values from 0.5 to 4
- triples: int32 [128, 3], P('trip'), may hold values from -1 to 63, as said below
Outputs:
- triple_energy: float32 [128, 64], P('trip')
Inputs may be any that keep to these rules, and one draw needn't show every extreme that they name: Rows 2 * t to 2 * t + 1 belong to orbital t: the first of them hold distinct triples (i, j, t) with t < j < i <= t + 3, the others hold -1 in all three columns; some orbital has all 2 rows filled.
All inputs are finite; a program needn't handle non-finite values.
Results may differ from a plain program's by a relative error of at most 0.0025.
Values may be sent and summed in bfloat16 or wider, within the bound.
No kernel may reach another device: no remote copies, remote signals or barrier semaphores. Data moves between devices by JAX's collectives and lax.ppermute only.
A program may use at most 128 MiB of HBM per device.

v0:
```python
import jax
import jax.numpy as jnp
from jax import lax
from jax.sharding import PartitionSpec as P


def from_behind(block, axis, distance):
    devices = range(lax.axis_size(axis))
    route = [(i - distance, i) for i in devices if i - distance in devices]
    return lax.ppermute(block, axis, route)


def pair_pick(pair_table, first_orb, second_orb):
    lower_orb = jnp.minimum(first_orb, second_orb)
    return pair_table[
        lower_orb, jnp.abs(first_orb - second_orb) - 1, (first_orb > second_orb).astype(jnp.int32)
    ]


def local_terms(band_arrays, offsets):
    panels, pair_table, hole_table, coulomb_table = (
        band_arrays[0],
        band_arrays[1],
        band_arrays[2],
        band_arrays[3],
    )
    tile_width = pair_table.shape[3]
    orb_i, orb_j, orb_k = offsets
    groups = (
        (orb_k, (orb_i, orb_j, (0, 1, 2)), (orb_j, orb_i, (1, 0, 2))),
        (orb_j, (orb_i, orb_k, (0, 2, 1)), (orb_k, orb_i, (1, 2, 0))),
        (orb_i, (orb_k, orb_j, (2, 1, 0)), (orb_j, orb_k, (2, 0, 1))),
    )
    running = jnp.zeros((tile_width, tile_width, tile_width), jnp.float32)
    for third_orb, first_pair, second_pair in groups:
        stacked = jnp.concatenate(
            [
                pair_pick(pair_table, first_pair[0], first_pair[1]),
                pair_pick(pair_table, second_pair[0], second_pair[1]),
            ],
            axis=0,
        )
        products = jnp.dot(stacked, panels[third_orb], preferred_element_type=jnp.float32)
        products = products.reshape(2, tile_width, tile_width, tile_width)
        for member, (lead_orb, mid_orb, axes_order) in enumerate((first_pair, second_pair)):
            coulomb = coulomb_table[
                jnp.minimum(mid_orb, third_orb), jnp.abs(mid_orb - third_orb) - 1
            ]
            hole_term = lax.dot_general(
                hole_table[lead_orb],
                coulomb,
                (((0,), (0,)), ((), ())),
                preferred_element_type=jnp.float32,
            )
            hole_term = hole_term.reshape(tile_width, tile_width, tile_width)
            running = running + jnp.transpose(products[member] - hole_term, axes_order)
    return running


def triple_energy(summed, band_arrays, offsets, virt_energy):
    exchange_table, single_table, energy_table = (band_arrays[4], band_arrays[5], band_arrays[6])
    tile_width = virt_energy.shape[0]
    orb_i, orb_j, orb_k = offsets
    exch_kj = (
        exchange_table[orb_k, orb_j - orb_k - 1].astype(jnp.float32).reshape(tile_width, tile_width)
    )
    exch_ki = (
        exchange_table[orb_k, orb_i - orb_k - 1].astype(jnp.float32).reshape(tile_width, tile_width)
    )
    exch_ji = (
        exchange_table[orb_j, orb_i - orb_j - 1].astype(jnp.float32).reshape(tile_width, tile_width)
    )
    single_i = single_table[orb_i].astype(jnp.float32)
    single_j = single_table[orb_j].astype(jnp.float32)
    single_k = single_table[orb_k].astype(jnp.float32)
    full_v = (
        summed
        + single_i[:, None, None] * exch_kj.T[None, :, :]
        + single_j[None, :, None] * exch_ki.T[:, None, :]
        + single_k[None, None, :] * exch_ji.T[:, :, None]
    )
    cross = 4.0 * summed + jnp.transpose(summed, (2, 0, 1)) + jnp.transpose(summed, (1, 2, 0))
    occ_sum = (
        energy_table[orb_i].astype(jnp.float32)
        + energy_table[orb_j].astype(jnp.float32)
        + energy_table[orb_k].astype(jnp.float32)
    )
    denom = (
        occ_sum
        - virt_energy[:, None, None]
        - virt_energy[None, :, None]
        - virt_energy[None, None, :]
    )
    return jnp.sum(cross * (full_v - jnp.transpose(full_v, (2, 1, 0))) / denom, axis=(1, 2))


def local(
    virt_integrals,
    pair_amps,
    hole_amps,
    coulomb_ints,
    exchange_ints,
    singles,
    occ_energy,
    virt_energy,
    triples,
):
    owner_index = lax.axis_index("trip")
    slot_count = triples.shape[0]
    tile_width = virt_energy.shape[0]
    reach_span = pair_amps.shape[1]
    bundle = (
        virt_integrals,
        pair_amps,
        hole_amps,
        coulomb_ints,
        exchange_ints,
        singles,
        occ_energy,
    )
    pieces = [bundle]
    for distance in range(1, reach_span + 1):
        pieces.append(
            from_behind(
                (bundle[0], bundle[1], bundle[2], bundle[3], bundle[4], bundle[5], bundle[6]),
                "trip",
                -distance,
            )
        )
    band_arrays = tuple(
        (
            jnp.concatenate([parcel[member] for parcel in pieces], axis=0)
            for member in range(len(bundle))
        )
    )

    def one_triple(position, energy_rows):
        picked = triples[position]
        usable = picked[0] >= 0
        offsets = (
            jnp.where(usable, picked[0] - owner_index, 2),
            jnp.where(usable, picked[1] - owner_index, 1),
            jnp.where(usable, picked[2] - owner_index, 0),
        )
        partial_value = local_terms(band_arrays, offsets)
        summed = lax.psum(partial_value.astype(jnp.bfloat16), "virt").astype(jnp.float32)
        energy = triple_energy(summed, band_arrays, offsets, virt_energy)
        energy = jnp.where(usable, energy, jnp.zeros_like(energy))
        return energy_rows.at[position].set(energy)

    return lax.fori_loop(
        0, slot_count, one_triple, jnp.zeros((slot_count, tile_width), jnp.float32)
    )


def solution(mesh):
    placed = (
        P("trip", "virt", None),
        P("trip", None, None, None, "virt"),
        P("trip", "virt", None),
        P("trip", None, "virt", None),
        P("trip", None, None),
        P("trip", None),
        P("trip"),
        P(),
        P("trip", None),
    )
    return jax.shard_map(
        local, mesh=mesh, in_specs=placed, out_specs=P("trip", None), check_vma=False
    )
```

profile of v0, /device:TPU:2, one launch (start us, length us, event | category | flops | bytes accessed | tf_op | source)
XLA Modules:
  0.0 706.6 jit_solution(12541975350000002647)
XLA Ops:
  6.5 7.9 %collective-permute-start.3 = (bf16[1,256,4096]{2,1,0:T(8,128)(2,1)}, bf16[1,256,4096]{2,1,0:T(8,128)(2,1)S(1)}, u32[]{:S(2)}, u32[]{:S(2)}) collective-permute-start(bf16[1,256,4096]{2,1,0:T(8,128)(2,1)} %param.13), channel_id=1, source_target_pairs={{8,0},{16,8},{24,16},{32,24},{40,32},{48,40},{56,48},{64,56},{72,6... | collective-permute-start | bytes 6291464 | tf_op jit(solution)/shard_map/ppermute | solution.py:10
  20.3 78.7 %collective-permute-done.18 = bf16[1]{0:T(256)(128)(2,1)} collective-permute-done((bf16[1]{0:T(256)(128)(2,1)}, bf16[1]{0:T(256)(128)(2,1)}, u32[]{:S(2)}, u32[]{:S(2)}) %collective-permute-start.18) | collective-permute-done | bytes 34 | tf_op jit(solution)/shard_map/ppermute | solution.py:10
  100.3 133.3 %collective-permute-done.19 = bf16[1]{0:T(256)(128)(2,1)} collective-permute-done((bf16[1]{0:T(256)(128)(2,1)}, bf16[1]{0:T(256)(128)(2,1)}, u32[]{:S(2)}, u32[]{:S(2)}) %collective-permute-start.19) | collective-permute-done | bytes 34 | tf_op jit(solution)/shard_map/ppermute | solution.py:10
  234.8 5.1 collective-permute-done.20
  240.0 4.6 collective-permute-start.12
  247.2 8.4 %collective-permute-done.13 = bf16[1,64]{1,0:T(2,128)(2,1)S(1)} collective-permute-done((bf16[1,64]{1,0:T(2,128)(2,1)}, bf16[1,64]{1,0:T(2,128)(2,1)S(1)}, u32[]{:S(2)}, u32[]{:S(2)}) %collective-permute-start.13) | collective-permute-done | bytes 160 | tf_op jit(solution)/shard_map/ppermute | solution.py:10
  256.9 5.2 collective-permute-done.14
  262.1 4.6 collective-permute-start
  267.9 7.0 collective-permute-done.11
  276.9 4.1 collective-permute-done.9
  282.8 4.1 collective-permute-done.15
  288.2 7.6 %collective-permute-done.16 = bf16[1,3,4096]{2,1,0:T(4,128)(2,1)S(1)} collective-permute-done((bf16[1,3,4096]{2,1,0:T(4,128)(2,1)}, bf16[1,3,4096]{2,1,0:T(4,128)(2,1)S(1)}, u32[]{:S(2)}, u32[]{:S(2)}) %collective-permute-start.16) | collective-permute-done | bytes 24608 | tf_op jit(solution)/shard_map/ppermute | solution.py:10
  297.1 5.9 collective-permute-done.17
  305.0 4.3 collective-permute-start.6
  315.7 10.2 %collective-permute-done.2 = bf16[1,3,2,64,256]{4,3,2,1,0:T(8,128)(2,1)S(1)} collective-permute-done((bf16[1,3,2,64,256]{4,3,2,1,0:T(8,128)(2,1)}, bf16[1,3,2,64,256]{4,3,2,1,0:T(8,128)(2,1)S(1)}, u32[]{:S(2)}, u32[]{:S(2)}) %collective-permute-start.2) | collective-permute-done | bytes 196640 | tf_op jit(solution)/shard_map/ppermute | solution.py:10
  330.0 2.2 pad_maximum_fusion.2
  332.1 4.4 collective-permute-done.7
  339.7 6.2 pad_maximum_fusion
  345.9 353.3 %while.19 = (s32[]{:T(128)}, f32[2,64]{1,0:T(2,128)S(1)}, s32[2,3]{1,0:T(2,128)S(1)}, s32[]{:T(128)}, bf16[4,3,2,64,256]{4,3,2,1,0:T(8,128)(2,1)}, /*index=5*/bf...) while((s32[]{:T(128)}, f32[2,64]{1,0:T(2,128)S(1)}, ...), condition=%wide.region_4.5_spmd, body=%wide.region_0.4_spmd.sunk | while | flops 934429056 | bytes 105868432 | solution.py:151
  355.4 2.1 fusion.133
  357.5 2.3 copy.97
  359.7 3.1 fusion.129
  362.9 2.0 fusion.128
  365.7 2.0 fusion.126
  368.9 3.1 squeeze.445
  372.0 3.8 copy.91
  375.8 2.1 squeeze.446
  378.0 4.1 copy.93
  382.1 2.0 fusion.130
  385.3 3.1 squeeze.447
  388.5 2.9 copy.96
  393.3 2.0 fusion.124
  396.6 3.2 squeeze.444
  399.7 2.2 squeeze.448
  401.9 4.1 copy.94
  406.1 3.9 copy.92
  411.7 9.9 %fusion.134 = bf16[64,64,64]{2,1,0:T(8,128)(2,1)} fusion(f32[64,64,64]{2,0,1:T(8,128)S(1)} %fusion.123, f32[64,64,64]{2,1,0:T(8,128)} %squeeze.444, f32[64,64,64]{1,0,2:T(8,128)} %copy.91, f32[64,64,64]{1,0,2:T(8,128)} %copy.92, f32[64,64,64]{0,1,2:T(8,128)} %copy.93, f32[64,64,64]{0,1,2:T(8,128)} %copy.94, f32[64,64,64]{0,2,1:T(8,128)} %bitcast.203, ...), kind=kOutput, calls=%fused_computation.6.clone.1 | convolution fusion | flops 23068672 | bytes 15869960 | tf_op jit(solution)/shard_map/while/body/eval_jaxpr/dot_general | solution.py:49
  426.6 90.6 %all-reduce.2.cloned.1.call-done = bf16[64,64,64]{2,1,0:T(8,128)(2,1)} async-done(((bf16[64,64,64]{2,1,0:T(8,128)(2,1)}), bf16[64,64,64]{2,1,0:T(8,128)(2,1)}) %all-reduce.2.cloned.1.call-update) | async-done | bytes 524304 | tf_op jit(solution)/shard_map/while/body/eval_jaxpr/psum | solution.py:146
  519.1 3.0 copy.98
  522.1 2.3 copy.100
  524.4 2.2 copy.99
  526.6 4.3 fusion.136
  541.0 2.1 fusion.133
  543.1 2.3 copy.97
  545.4 3.1 fusion.129
  551.4 2.0 fusion.126
  554.6 3.1 squeeze.445
  557.7 3.8 copy.91
  561.5 2.1 squeeze.446
  563.6 4.1 copy.93
  567.8 2.0 fusion.130
  571.0 3.1 squeeze.447
  574.1 2.9 copy.96
  578.9 2.0 fusion.124
  582.2 3.2 squeeze.444
  585.4 2.2 squeeze.448
  587.6 4.1 copy.94
  591.7 3.9 copy.92
  597.3 9.9 %fusion.134 = bf16[64,64,64]{2,1,0:T(8,128)(2,1)} fusion(f32[64,64,64]{2,0,1:T(8,128)S(1)} %fusion.123, f32[64,64,64]{2,1,0:T(8,128)} %squeeze.444, f32[64,64,64]{1,0,2:T(8,128)} %copy.91, f32[64,64,64]{1,0,2:T(8,128)} %copy.92, f32[64,64,64]{0,1,2:T(8,128)} %copy.93, f32[64,64,64]{0,1,2:T(8,128)} %copy.94, f32[64,64,64]{0,2,1:T(8,128)} %bitcast.203, ...), kind=kOutput, calls=%fused_computation.6.clone.1 | convolution fusion | flops 23068672 | bytes 15869960 | tf_op jit(solution)/shard_map/while/body/eval_jaxpr/dot_general | solution.py:49
  612.2 72.4 %all-reduce.2.cloned.1.call-done = bf16[64,64,64]{2,1,0:T(8,128)(2,1)} async-done(((bf16[64,64,64]{2,1,0:T(8,128)(2,1)}), bf16[64,64,64]{2,1,0:T(8,128)(2,1)}) %all-reduce.2.cloned.1.call-update) | async-done | bytes 524304 | tf_op jit(solution)/shard_map/while/body/eval_jaxpr/psum | solution.py:146
  686.6 3.0 copy.98
  689.6 2.3 copy.100
  691.9 2.2 copy.99
  694.1 4.3 fusion.136
  (129 shorter events, 78.0 us)
Async XLA Ops:
  6.5 331.8 %copy-start.6 = (bf16[1,38,4096]{2,1,0:T(8,128)(2,1)S(1)}, bf16[1,38,4096]{2,1,0:T(8,128)(2,1)}, u32[]{:S(2)}) copy-start(bf16[1,38,4096]{2,1,0:T(8,128)(2,1)} %param.15) | copy-start | bytes 933892
  6.5 333.1 %collective-permute-start.3 = (bf16[1,256,4096]{2,1,0:T(8,128)(2,1)}, bf16[1,256,4096]{2,1,0:T(8,128)(2,1)S(1)}, u32[]{:S(2)}, u32[]{:S(2)}) collective-permute-start(bf16[1,256,4096]{2,1,0:T(8,128)(2,1)} %param.13), channel_id=1, source_target_pairs={{8,0},{16,8},{24,16},{32,24},{40,32},{48,40},{56,48},{64,56},{72,6... | collective-permute-start | bytes 6291464 | tf_op jit(solution)/shard_map/ppermute | solution.py:10
  14.5 325.1 %collective-permute-start.4 = (bf16[1,256,4096]{2,1,0:T(8,128)(2,1)}, bf16[1,256,4096]{2,1,0:T(8,128)(2,1)}, u32[]{:S(2)}, u32[]{:S(2)}) collective-permute-start(bf16[1,256,4096]{2,1,0:T(8,128)(2,1)} %param.13), channel_id=1, source_target_pairs={{16,0},{24,8},{32,16},{40,24},{48,32},{56,40},{64,48},{72,56},{80,... | collective-permute-start | bytes 6291464 | tf_op jit(solution)/shard_map/ppermute | solution.py:10
  15.8 323.9 %collective-permute-start.5 = (bf16[1,256,4096]{2,1,0:T(8,128)(2,1)}, bf16[1,256,4096]{2,1,0:T(8,128)(2,1)}, u32[]{:S(2)}, u32[]{:S(2)}) collective-permute-start(bf16[1,256,4096]{2,1,0:T(8,128)(2,1)} %param.13), channel_id=1, source_target_pairs={{24,0},{32,8},{40,16},{48,24},{56,32},{64,40},{72,48},{80,56},{88,... | collective-permute-start | bytes 6291464 | tf_op jit(solution)/shard_map/ppermute | solution.py:10
  17.1 249.6 %collective-permute-start.10 = (bf16[1,3,38,64]{3,2,1,0:T(8,128)(2,1)}, bf16[1,3,38,64]{3,2,1,0:T(8,128)(2,1)S(1)}, u32[]{:S(2)}, u32[]{:S(2)}) collective-permute-start(bf16[1,3,38,64]{3,2,1,0:T(8,128)(2,1)} %param.16), channel_id=1, source_target_pairs={{16,0},{24,8},{32,16},{40,24},{48,32},{56,40},{64,48},{72,56},{80,... | collective-permute-start | bytes 43784 | tf_op jit(solution)/shard_map/ppermute | solution.py:10
  18.4 80.6 %collective-permute-start.18 = (bf16[1]{0:T(256)(128)(2,1)}, bf16[1]{0:T(256)(128)(2,1)}, u32[]{:S(2)}, u32[]{:S(2)}) collective-permute-start(bf16[1]{0:T(256)(128)(2,1)} %param.19), channel_id=1, source_target_pairs={{8,0},{16,8},{24,16},{32,24},{40,32},{48,40},{56,48},{64,56},{72,6... | collective-permute-start | bytes 14 | tf_op jit(solution)/shard_map/ppermute | solution.py:10
  99.0 134.6 %collective-permute-start.19 = (bf16[1]{0:T(256)(128)(2,1)}, bf16[1]{0:T(256)(128)(2,1)}, u32[]{:S(2)}, u32[]{:S(2)}) collective-permute-start(bf16[1]{0:T(256)(128)(2,1)} %param.19), channel_id=1, source_target_pairs={{16,0},{24,8},{32,16},{40,24},{48,32},{56,40},{64,48},{72,56},{80,... | collective-permute-start | bytes 14 | tf_op jit(solution)/shard_map/ppermute | solution.py:10
  233.6 6.4 collective-permute-start.20
  240.0 6.0 collective-permute-start.12
  246.0 9.6 %collective-permute-start.13 = (bf16[1,64]{1,0:T(2,128)(2,1)}, bf16[1,64]{1,0:T(2,128)(2,1)S(1)}, u32[]{:S(2)}, u32[]{:S(2)}) collective-permute-start(bf16[1,64]{1,0:T(2,128)(2,1)} %param.18), channel_id=1, source_target_pairs={{16,0},{24,8},{32,16},{40,24},{48,32},{56,40},{64,48},{72,56},{80,... | collective-permute-start | bytes 392 | tf_op jit(solution)/shard_map/ppermute | solution.py:10
  255.6 6.5 collective-permute-start.14
  262.1 42.9 %collective-permute-start = (bf16[1,3,2,64,256]{4,3,2,1,0:T(8,128)(2,1)}, bf16[1,3,2,64,256]{4,3,2,1,0:T(8,128)(2,1)S(1)}, u32[]{:S(2)}, u32[]{:S(2)}) collective-permute-start(bf16[1,3,2,64,256]{4,3,2,1,0:T(8,128)(2,1)} %param.14), channel_id=1, source_target_pairs={{8,0},{16,8},{24,16},{32,24},{40,32},{48,40},{56,48},{64,56},{72,6... | collective-permute-start | bytes 589832 | tf_op jit(solution)/shard_map/ppermute | solution.py:10
  266.6 8.3 %collective-permute-start.11 = (bf16[1,3,38,64]{3,2,1,0:T(8,128)(2,1)}, bf16[1,3,38,64]{3,2,1,0:T(8,128)(2,1)S(1)}, u32[]{:S(2)}, u32[]{:S(2)}) collective-permute-start(bf16[1,3,38,64]{3,2,1,0:T(8,128)(2,1)} %param.16), channel_id=1, source_target_pairs={{24,0},{32,8},{40,16},{48,24},{56,32},{64,40},{72,48},{80,56},{88,... | collective-permute-start | bytes 43784 | tf_op jit(solution)/shard_map/ppermute | solution.py:10
  274.9 6.0 collective-permute-start.9
  280.9 6.0 collective-permute-start.15
  286.9 8.9 %collective-permute-start.16 = (bf16[1,3,4096]{2,1,0:T(4,128)(2,1)}, bf16[1,3,4096]{2,1,0:T(4,128)(2,1)S(1)}, u32[]{:S(2)}, u32[]{:S(2)}) collective-permute-start(bf16[1,3,4096]{2,1,0:T(4,128)(2,1)} %param.17), channel_id=1, source_target_pairs={{16,0},{24,8},{32,16},{40,24},{48,32},{56,40},{64,48},{72,56},{80,... | collective-permute-start | bytes 73736 | tf_op jit(solution)/shard_map/ppermute | solution.py:10
  295.8 7.2 %collective-permute-start.17 = (bf16[1,3,4096]{2,1,0:T(4,128)(2,1)}, bf16[1,3,4096]{2,1,0:T(4,128)(2,1)S(1)}, u32[]{:S(2)}, u32[]{:S(2)}) collective-permute-start(bf16[1,3,4096]{2,1,0:T(4,128)(2,1)} %param.17), channel_id=1, source_target_pairs={{24,0},{32,8},{40,16},{48,24},{56,32},{64,40},{72,48},{80,56},{88,... | collective-permute-start | bytes 73736 | tf_op jit(solution)/shard_map/ppermute | solution.py:10
  303.0 9.9 %collective-permute-start.1 = (bf16[1,3,2,64,256]{4,3,2,1,0:T(8,128)(2,1)}, bf16[1,3,2,64,256]{4,3,2,1,0:T(8,128)(2,1)S(1)}, u32[]{:S(2)}, u32[]{:S(2)}) collective-permute-start(bf16[1,3,2,64,256]{4,3,2,1,0:T(8,128)(2,1)} %param.14), channel_id=1, source_target_pairs={{16,0},{24,8},{32,16},{40,24},{48,32},{56,40},{64,48},{72,56},{80,... | collective-permute-start | bytes 589832 | tf_op jit(solution)/shard_map/ppermute | solution.py:10
  305.0 22.2 %collective-permute-start.6 = (bf16[1,38,4096]{2,1,0:T(8,128)(2,1)}, bf16[1,38,4096]{2,1,0:T(8,128)(2,1)S(1)}, u32[]{:S(2)}, u32[]{:S(2)}) collective-permute-start(bf16[1,38,4096]{2,1,0:T(8,128)(2,1)} %param.15), channel_id=1, source_target_pairs={{8,0},{16,8},{24,16},{32,24},{40,32},{48,40},{56,48},{64,56},{72,6... | collective-permute-start | bytes 933896 | tf_op jit(solution)/shard_map/ppermute | solution.py:10
  312.9 2.8 copy-start.7
  312.9 13.0 %collective-permute-start.2 = (bf16[1,3,2,64,256]{4,3,2,1,0:T(8,128)(2,1)}, bf16[1,3,2,64,256]{4,3,2,1,0:T(8,128)(2,1)S(1)}, u32[]{:S(2)}, u32[]{:S(2)}) collective-permute-start(bf16[1,3,2,64,256]{4,3,2,1,0:T(8,128)(2,1)} %param.14), channel_id=1, source_target_pairs={{24,0},{32,8},{40,16},{48,24},{56,32},{64,40},{72,48},{80,56},{88,... | collective-permute-start | bytes 589832 | tf_op jit(solution)/shard_map/ppermute | solution.py:10
  325.9 10.7 %collective-permute-start.7 = (bf16[1,38,4096]{2,1,0:T(8,128)(2,1)}, bf16[1,38,4096]{2,1,0:T(8,128)(2,1)S(1)}, u32[]{:S(2)}, u32[]{:S(2)}) collective-permute-start(bf16[1,38,4096]{2,1,0:T(8,128)(2,1)} %param.15), channel_id=1, source_target_pairs={{16,0},{24,8},{32,16},{40,24},{48,32},{56,40},{64,48},{72,56},{80,... | collective-permute-start | bytes 933896 | tf_op jit(solution)/shard_map/ppermute | solution.py:10
  327.2 11.2 %collective-permute-start.8 = (bf16[1,38,4096]{2,1,0:T(8,128)(2,1)}, bf16[1,38,4096]{2,1,0:T(8,128)(2,1)S(1)}, u32[]{:S(2)}, u32[]{:S(2)}) collective-permute-start(bf16[1,38,4096]{2,1,0:T(8,128)(2,1)} %param.15), channel_id=1, source_target_pairs={{24,0},{32,8},{40,16},{48,24},{56,32},{64,40},{72,48},{80,56},{88,... | collective-permute-start | bytes 933896 | tf_op jit(solution)/shard_map/ppermute | solution.py:10
  330.0 9.7 %copy-start.5 = (bf16[1,256,4096]{2,1,0:T(8,128)(2,1)S(1)}, bf16[1,256,4096]{2,1,0:T(8,128)(2,1)}, u32[]{:S(2)}) copy-start(bf16[1,256,4096]{2,1,0:T(8,128)(2,1)} %param.13) | copy-start | bytes 6291460
  339.6 6.3 copy-start.8
  339.6 6.3 copy-start.9
  339.6 6.3 copy-start.11
  346.1 171.1 %all-reduce.2.cloned.1.call-start = ((), (), s32[]{:S(2)}) async-start(), calls=%async_computation | async-start | bytes 2097152 | tf_op jit(solution)/shard_map/while/body/eval_jaxpr/psum | solution.py:146
  406.1 3.9 copy-start.4
  410.0 1.6 copy-start.1
  410.0 1.7 copy-start.3
  519.1 3.1 copy-start
  524.4 2.2 copy-start.2
  531.7 152.9 %all-reduce.2.cloned.1.call-start = ((), (), s32[]{:S(2)}) async-start(), calls=%async_computation | async-start | bytes 2097152 | tf_op jit(solution)/shard_map/while/body/eval_jaxpr/psum | solution.py:146
  591.7 3.9 copy-start.4
  595.6 1.6 copy-start.1
  595.6 1.7 copy-start.3
  686.6 3.1 copy-start
  691.9 2.2 copy-start.2
  699.2 0.6 copy-start.10
Sparse Core Ops, SparseCore 0:
  421.7 95.3 all-reduce.1
  607.4 77.2 all-reduce.1
where the time goes:
time: 709 us; the launch traced here: 707 us
  waiting for transfers between devices  442 us (62%)
  local copies, waits for them, and re-layouts  115 us (16%)
  matrix products  48.6 us (7%)
  starting transfers between devices  45.2 us (6%)
  other arithmetic  32.2 us (5%)
  between operations  14.3 us (2%)
  loops' own time  9.76 us (1%)
    ppermute x21, waiting for transfers between devices, from_behind(): return lax.ppermute(block, axis, route)  279 us
    psum x2, waiting for transfers between devices, one_triple(): lax.psum(partial_value.astype(jnp.bfloat16), 'virt').astype(jnp.float32)  163 us
    squeeze x16, local copies, waits for them, and re-layouts, local_terms(): running = running + jnp.transpose(products[member] - hole_term, axes_order)  49.1 us
    ppermute x21, starting transfers between devices, from_behind(): return lax.ppermute(block, axis, route)  45.1 us
    dot_general x12, matrix products, local_terms(): lax.dot_general(hole_table[lead_orb], coulomb, (((0,), (0,)), ((), ())),...  36.4 us
    dot_general x16, local copies, waits for them, and re-layouts, local_terms(): lax.dot_general(hole_table[lead_orb], coulomb, (((0,), (0,)), ((), ())),...  31.2 us
    concatenate x7, other arithmetic, local(): jnp.concatenate([parcel[member] for parcel in pieces], axis=0)  14.6 us
  transfers between devices with their start and end apart: 23, of which 17 were waited for; matrix products, arithmetic and copies ran while one was open for 2% of the time, Pallas kernels for 0%

commit v1 on v0

v1 whole, which is shorter than its diff:
```python
import jax
import jax.numpy as jnp
from jax import lax
from jax.experimental import pallas as pl
from jax.experimental.pallas import tpu as pltpu
from jax.sharding import PartitionSpec as P

T = 64
H = 32
F32 = jnp.float32
BF16 = jnp.bfloat16
CROWS = 16
BLOCK_ROWS = 2 * T + CROWS
VMEM_LIMIT = 48 * 1024 * 1024


def shift_route(size, distance):
    return [(i, i + distance) for i in range(size) if 0 <= i + distance < size]


def ring_route(step):
    return [(i, (i + 2 * step) % 8) for i in range(8)]


CORE_ROUTE = [(i, i ^ 1) for i in range(8)]


def lane_low(rows):
    return lax.broadcasted_iota(jnp.int32, (rows, 2 * T), 1) < T


def swap_halves(x):
    return jnp.concatenate([x[:, T:], x[:, :T]], axis=1)


def pack_rows(rows64):
    low = lane_low(H)
    top, bottom = rows64[:H], rows64[H:]
    first = jnp.where(low, top, swap_halves(bottom))
    second = jnp.where(low, swap_halves(top), bottom)
    return first, second


def terms_kernel(place, blocks, panels, holes, out):
    y = place[0]
    amps_lead, amps_dup, coul_lead, coul_dup = [], [], [], []
    for d in range(4):
        block = blocks[d]
        second = block[T : 2 * T]
        amps_lead.append(block[:T])
        amps_dup += [second, second]
        packed = block[2 * T :]
        coulomb = jnp.concatenate(
            [packed[:, g * T : (g + 1) * T] for g in range(4)], axis=0
        )
        coul_lead.append(coulomb)
        coul_dup += [coulomb, coulomb]
    amps_lead = jnp.concatenate(amps_lead, axis=0)
    amps_dup = jnp.concatenate(amps_dup, axis=0)
    coul_lead = jnp.concatenate(coul_lead, axis=0)
    coul_dup = jnp.concatenate(coul_dup, axis=0)
    low = lane_low(T)
    contract = (((1,), (1,)), ((), ()))

    def group(step, _):
        rows = pl.ds(pl.multiple_of(step * 8 * T, 8 * T), 8 * T)
        panel = panels[rows, :]
        hole = holes[rows, :]
        by_rows = lax.dot_general(panel, amps_dup, contract, preferred_element_type=F32)
        by_rows += lax.dot_general(hole, coul_dup, contract, preferred_element_type=F32)
        by_cols = lax.dot_general(amps_lead, panel, contract, preferred_element_type=F32)
        by_cols += lax.dot_general(coul_lead, hole, contract, preferred_element_type=F32)
        own = lax.rem(step // 2 - y + 4, 4)
        for pair in range(4):
            row = pair * 2 * T
            for d in range(4):
                col = d * 2 * T
                tile = jnp.where(
                    low,
                    by_rows[row : row + T, col : col + 2 * T],
                    by_rows[row + T : row + 2 * T, col : col + 2 * T],
                )
                tile += by_cols[d * T : (d + 1) * T, row : row + 2 * T]
                if d == 0:
                    at = pl.multiple_of((lax.rem(step, 2) * 4 + pair) * T, T)
                    out[own, 0, pl.ds(at, T), :] = tile.astype(BF16)
                else:
                    at = pl.multiple_of((step * 4 + pair) * 16, 16)
                    for quarter in range(4):
                        rows16 = jnp.concatenate(
                            [
                                tile[8 * quarter : 8 * quarter + 8],
                                tile[H + 8 * quarter : H + 8 * quarter + 8],
                            ],
                            axis=0,
                        )
                        out[lax.rem(quarter - y + 4, 4), d, pl.ds(at, 16), :] = rows16.astype(BF16)
        return 0

    lax.fori_loop(0, 8, group, 0)


def terms(place, blocks, panels, holes):
    vmem = pl.BlockSpec(memory_space=pltpu.VMEM)
    return pl.pallas_call(
        terms_kernel,
        out_shape=jax.ShapeDtypeStruct((4, 4, 512, 2 * T), BF16),
        in_specs=[pl.BlockSpec(memory_space=pltpu.SMEM), vmem, vmem, vmem],
        out_specs=vmem,
        compiler_params=pltpu.CompilerParams(vmem_limit_bytes=VMEM_LIMIT),
        cost_estimate=pl.CostEstimate(
            flops=2 * 4096 * 320 * 768, bytes_accessed=5 << 20, transcendentals=0
        ),
        name="terms",
    )(place, blocks, panels, holes)


def combine_kernel(role, own, one, two, three, out, scratch):
    for index, part in enumerate((one, two, three)):
        scratch[index * 512 : (index + 1) * 512, :] = part[...].astype(F32)
    mid_is_j = jnp.full((T, 2 * T), role[0], jnp.int32) == 1

    def as_rows(index, cp):
        low_rows = scratch[pl.ds(index * 512 + cp, H, stride=16), :]
        high_rows = scratch[pl.ds(index * 512 + 8 + cp, H, stride=16), :]
        low = lane_low(H)
        top = jnp.where(low, low_rows, swap_halves(high_rows))
        bottom = jnp.where(low, swap_halves(low_rows), high_rows)
        return jnp.concatenate([top, bottom], axis=0)

    def turned(x):
        flat = x.T
        return jnp.concatenate([flat[:T], flat[T:]], axis=1)

    for cp in range(8):
        total = own[cp * T : (cp + 1) * T, :].astype(F32)
        total += as_rows(0, cp)
        middle = as_rows(1, cp)
        total += jnp.where(mid_is_j, middle, turned(middle))
        total += turned(as_rows(2, cp))
        out[cp * T : (cp + 1) * T, :] = total.astype(BF16)


def combine(role, own, one, two, three):
    vmem = pl.BlockSpec(memory_space=pltpu.VMEM)
    return pl.pallas_call(
        combine_kernel,
        out_shape=jax.ShapeDtypeStruct((512, 2 * T), BF16),
        in_specs=[pl.BlockSpec(memory_space=pltpu.SMEM)] + [vmem] * 4,
        out_specs=vmem,
        scratch_shapes=[pltpu.VMEM((3 * 512, 2 * T), F32)],
        compiler_params=pltpu.CompilerParams(vmem_limit_bytes=VMEM_LIMIT),
        name="combine",
    )(role, own, one, two, three)


def energy_kernel(place, w0, w1, w2, w3, extra_a, extra_b, inverse, out, whole, flipped, acc, rows_b):
    y = place[0]
    for j, part in enumerate((w0, w1, w2, w3)):
        at = pl.multiple_of(lax.rem(y - j + 4, 4) * 512, 512)
        whole[pl.ds(at, 512), :] = part[...].astype(F32)

    def flip(b, _):
        across = whole[pl.ds(b, H, stride=T), :].T
        flipped[pl.ds(pl.multiple_of(b * H, H), H), :] = jnp.concatenate(
            [across[0:H], across[T : T + H], across[H:T], across[T + H :]], axis=1
        )
        return 0

    lax.fori_loop(0, T, flip, 0, unroll=4)
    acc[...] = jnp.zeros_like(acc)

    def pair(bp, _):
        from_flipped = pack_rows(flipped[pl.ds(bp, T, stride=H), :])
        from_whole = pack_rows(whole[pl.ds(pl.multiple_of(bp * T, T), T), :])
        for half in range(2):
            b = bp + H * half
            at = pl.ds(pl.multiple_of(b * H, H), H)
            plain = whole[pl.ds(b, H, stride=T), :]
            turned = flipped[at, :]
            inv = inverse[at, :]
            first = (4.0 * plain + from_flipped[half]) * (plain - turned + extra_a[at, :]) * inv
            second = plain * (from_flipped[half] - from_whole[half] + extra_b[at, :]) * inv
            acc[...] += first
            rows_b[pl.ds(b, 1), :] = jnp.sum(second, axis=0, keepdims=True)
        return 0

    lax.fori_loop(0, H, pair, 0, unroll=2)
    by_a = jnp.sum(acc[...], axis=0, keepdims=True)
    by_a = by_a[:, :T] + by_a[:, T:]
    by_b = jnp.sum(rows_b[...].T, axis=0, keepdims=True)
    out[...] = jnp.broadcast_to(by_a + by_b, (8, T))


def energy_of(place, parts, extra_a, extra_b, inverse):
    vmem = pl.BlockSpec(memory_space=pltpu.VMEM)
    return pl.pallas_call(
        energy_kernel,
        out_shape=jax.ShapeDtypeStruct((8, T), F32),
        in_specs=[pl.BlockSpec(memory_space=pltpu.SMEM)] + [vmem] * 7,
        out_specs=vmem,
        scratch_shapes=[
            pltpu.VMEM((H * T, 2 * T), F32),
            pltpu.VMEM((H * T, 2 * T), F32),
            pltpu.VMEM((H, 2 * T), F32),
            pltpu.VMEM((T, 2 * T), F32),
        ],
        compiler_params=pltpu.CompilerParams(vmem_limit_bytes=VMEM_LIMIT),
        name="energy",
    )(place, *parts, extra_a, extra_b, inverse)


def pair_blocks(pair_amps, coulomb_ints):
    amps = pair_amps[0].reshape(3, 2 * T, 256)
    coulomb = -jnp.swapaxes(coulomb_ints[0], 1, 2)
    coulomb = jnp.pad(coulomb, ((0, 0), (0, 0), (0, T - coulomb.shape[2])))
    coulomb = coulomb.reshape(3, 4, CROWS, T).transpose(0, 2, 1, 3).reshape(3, CROWS, 4 * T)
    return jnp.concatenate([amps, coulomb], axis=1)


def energy_tables(offset_i, offset_j, usable, exch_kj, exch_ki, exch_ji, singles, occ, virt_energy):
    def pick(table, offset):
        return jnp.sum(
            jnp.where((jnp.arange(4) == offset).reshape((4,) + (1,) * (table.ndim - 1)), table, 0),
            axis=0,
        )

    s_i, s_j, s_k = pick(singles, offset_i), pick(singles, offset_j), singles[0]
    occ_sum = pick(occ, offset_i) + pick(occ, offset_j) + occ[0]
    lanes = 2 * T

    def over_a(v):
        return jnp.tile(v, 2)[None, None, :]

    def over_b(v):
        return v[:, None, None]

    def over_c(v):
        return jnp.concatenate(
            [jnp.broadcast_to(v[:H, None], (H, T)), jnp.broadcast_to(v[H:, None], (H, T))], axis=1
        )[None]

    def over_ca(m):
        return jnp.concatenate([m[:H], m[H:]], axis=1)[None]

    def over_ba(m):
        return jnp.tile(m, (1, 2))[:, None, :]

    def over_bc(m):
        low = jnp.broadcast_to(m[:, :H, None], (T, H, T))
        high = jnp.broadcast_to(m[:, H:, None], (T, H, T))
        return jnp.concatenate([low, high], axis=2)

    extra_a = (
        over_a(s_i) * over_bc(exch_kj.T)
        - over_c(s_i) * over_ba(exch_kj.T)
        + over_b(s_j) * over_ca(exch_ki - exch_ki.T)
        + over_c(s_k) * over_ba(exch_ji)
        - over_a(s_k) * over_bc(exch_ji)
    )
    extra_b = (
        over_b(s_i) * over_ca(exch_kj.T)
        - over_a(s_i) * over_bc(exch_kj)
        + over_c(s_j) * (over_ba(exch_ki.T) - over_ba(exch_ki))
        + over_a(s_k) * over_bc(exch_ji.T)
        - over_b(s_k) * over_ca(exch_ji)
    )
    denom = occ_sum - over_a(virt_energy) - over_b(virt_energy) - over_c(virt_energy)
    inverse = 1.0 / denom
    shape = (H * T, lanes)
    return extra_a.reshape(shape), extra_b.reshape(shape), inverse.reshape(shape)


def local(
    virt_integrals,
    pair_amps,
    hole_amps,
    coulomb_ints,
    exchange_ints,
    singles,
    occ_energy,
    virt_energy,
    triples,
):
    owner = lax.axis_index("trip")
    virt = lax.axis_index("virt")
    n_trip = lax.axis_size("trip")
    y, core = virt // 2, virt % 2
    place = jnp.stack([y, core]).astype(jnp.int32)

    usable = triples[:, 0] >= 0
    off_i = jnp.where(usable, triples[:, 0] - owner, 2)
    off_j = jnp.where(usable, triples[:, 1] - owner, 1)

    def by_core(pairs):
        return jnp.where(core == 0, pairs, pairs[::-1])

    usable, off_i, off_j = by_core(usable), by_core(off_i), by_core(off_j)

    blocks = pair_blocks(pair_amps, coulomb_ints)
    zero = jnp.zeros((), BF16)

    def choose(options, index, live):
        result = jnp.zeros_like(options[0])
        for at, option in enumerate(options):
            result = jnp.where(live & (index == at), option, result)
        return result

    outgoing = []
    for d in (1, 2, 3):
        rows = []
        for s in range(2):
            takes_part = usable[s] & ((off_i[s] == d) | (off_j[s] == d))
            other = off_i[s] + off_j[s] - d
            rows.append(choose([blocks[0], blocks[1], blocks[2]], other - 1, takes_part))
        outgoing.append(jnp.stack(rows))
    exchange = exchange_ints[0].reshape(3, 16, 256)
    small = jnp.concatenate(
        [singles[0], occ_energy, jnp.zeros((16 * 256 - T - 1,), BF16)]
    ).reshape(16, 256)
    from_one = jnp.concatenate([blocks[0], blocks[1], exchange[0], exchange[1], small], axis=0)
    from_two = jnp.concatenate([blocks[0], exchange[0], small], axis=0)

    incoming = [
        lax.ppermute(outgoing[d - 1], "trip", shift_route(n_trip, d)) for d in (1, 2, 3)
    ]
    got_one = lax.ppermute(from_one, "trip", shift_route(n_trip, -1))
    got_two = lax.ppermute(from_two, "trip", shift_route(n_trip, -2))
    got_three = lax.ppermute(small, "trip", shift_route(n_trip, -3))

    panels = virt_integrals[0].reshape(256, T, 2, H).transpose(3, 2, 1, 0).reshape(T * T, 256)
    holes = hole_amps[0].reshape(-1, 2, H, T).transpose(2, 1, 3, 0).reshape(T * T, -1)
    holes = jnp.pad(holes, ((0, 0), (0, T - holes.shape[1])))

    own_options = [got_one[:BLOCK_ROWS], got_one[BLOCK_ROWS : 2 * BLOCK_ROWS], got_two[:BLOCK_ROWS]]

    def own_block(s):
        return choose(own_options, off_i[s] + off_j[s] - 3, usable[s])

    def slots(s):
        return jnp.stack([own_block(s)] + [incoming[d][s] for d in range(3)])

    send = terms(place, slots(1), panels, holes)
    got = lax.ppermute(send, "virt", CORE_ROUTE)
    keep = terms(place, slots(0), panels, holes)
    sums = [(keep[j].astype(F32) + got[j].astype(F32)) for j in range(4)]

    arrived = [
        lax.ppermute(sums[j].astype(BF16), "virt", ring_route(j)) for j in (1, 2, 3)
    ]
    total = sums[0] + arrived[0].astype(F32) + arrived[1].astype(F32) + arrived[2].astype(F32)

    shares = [
        lax.ppermute(total[d].astype(BF16), "trip", shift_route(n_trip, -d)) for d in (1, 2, 3)
    ]
    role = (off_j[0] == 2).astype(jnp.int32).reshape(1)
    chunk = combine(role, total[0], shares[0], shares[1], shares[2])
    parts = [chunk] + [lax.ppermute(chunk, "virt", ring_route(j)) for j in (1, 2, 3)]

    exch_own = exchange_ints[0].astype(F32).reshape(3, T, T)

    def matrix(rows):
        return rows.astype(F32).reshape(T, T)

    first_exch = 2 * BLOCK_ROWS
    exch_ji = choose(
        [
            matrix(got_one[first_exch : first_exch + 16]),
            matrix(got_one[first_exch + 16 : first_exch + 32]),
            matrix(got_two[BLOCK_ROWS : BLOCK_ROWS + 16]),
        ],
        off_i[0] + off_j[0] - 3,
        usable[0],
    )
    exch_kj = choose([exch_own[0], exch_own[1]], off_j[0] - 1, usable[0])
    exch_ki = choose([exch_own[1], exch_own[2]], off_i[0] - 2, usable[0])
    smalls = [small, got_one[first_exch + 32 :], got_two[BLOCK_ROWS + 16 :], got_three]
    singles_by = jnp.stack([x[0, :T].astype(F32) for x in smalls])
    occ_by = jnp.stack([x[0, T].astype(F32) for x in smalls])
    extra_a, extra_b, inverse = energy_tables(
        off_i[0], off_j[0], usable[0], exch_kj, exch_ki, exch_ji, singles_by, occ_by, virt_energy
    )

    mine = energy_of(place, parts, extra_a, extra_b, inverse)[0]
    mine = jnp.where(usable[0], mine, jnp.zeros_like(mine))
    other = lax.ppermute(mine, "virt", CORE_ROUTE)
    return jnp.where(core == 0, jnp.stack([mine, other]), jnp.stack([other, mine]))


def solution(mesh):
    placed = (
        P("trip", "virt", None),
        P("trip", None, None, None, "virt"),
        P("trip", "virt", None),
        P("trip", None, "virt", None),
        P("trip", None, None),
        P("trip", None),
        P("trip"),
        P(),
        P("trip", None),
    )
    return jax.shard_map(
        local, mesh=mesh, in_specs=placed, out_specs=P("trip", None), check_vma=False
    )
```

time: 709 us -> 200 us (0.28)
  the two profiles are of different devices: /device:TPU:2 before, /device:TPU:359 now
where the time goes in v1:
time: 200 us; the launch traced here: 198 us
  starting transfers between devices  60.7 us (30%)
  local copies, waits for them, and re-layouts  34.9 us (17%)
  other arithmetic  30 us (15%)
  between operations  27.1 us (14%)
  waiting for transfers between devices  24 us (12%)
  Pallas kernels  21.5 us (11%)
    ppermute x3, waiting for transfers between devices, local(): lax.ppermute(sums[j].astype(BF16), 'virt', ring_route(j))  13.3 us
    pallas_call x2, Pallas kernels, terms(): pl.pallas_call(terms_kernel, out_shape=jax.ShapeDtypeStruct((4, 4, 512, 2...  12.2 us
    ppermute x3, starting transfers between devices, local(): lax.ppermute(outgoing[d - 1], 'trip', shift_route(n_trip, d))  11 us
    ppermute x3, starting transfers between devices, local(): lax.ppermute(chunk, 'virt', ring_route(j))  10.9 us
    ppermute x3, starting transfers between devices, local(): lax.ppermute(sums[j].astype(BF16), 'virt', ring_route(j))  10.7 us
    ppermute x3, starting transfers between devices, local(): lax.ppermute(total[d].astype(BF16), 'trip', shift_route(n_trip, -d))  10.3 us
    ppermute x3, waiting for transfers between devices, local(): lax.ppermute(total[d].astype(BF16), 'trip', shift_route(n_trip, -d))  7.07 us
    pallas_call x1, Pallas kernels, energy_of(): pl.pallas_call(energy_kernel, out_shape=jax.ShapeDtypeStruct((8, T), F32)...  6.8 us
  transfers between devices with their start and end apart: 17, of which 7 were waited for; matrix products, arithmetic and copies ran while one was open for 27% of the time, Pallas kernels for 3%

profile of v1, /device:TPU:359, one launch (start us, length us, event | category | flops | bytes accessed | tf_op | source)
XLA Modules:
  0.0 198.1 jit_solution(12043172576511925249)
XLA Ops:
  0.7 0.8 concatenate.50
  1.5 2.1 %collective-permute-start.15 = (bf16[16,256]{1,0:T(8,128)(2,1)S(1)}, bf16[16,256]{1,0:T(8,128)(2,1)S(1)}, u32[]{:S(2)}, u32[]{:S(2)}) collective-permute-start(bf16[16,256]{1,0:T(8,128)(2,1)S(1)} %reshape.335), channel_id=1, source_target_pairs={{24,0},{32,8},{40,16},{48,24},{56,32},{64,40},{72,48},{80,56},{88,... | collective-permute-start | bytes 24584 | tf_op jit(solution)/shard_map/ppermute | solution.py:329
  3.6 0.9 copy.36
  4.6 1.5 constant_dynamic-update-slice_fusion.3
  6.1 1.5 bitcast_dynamic-update-slice_fusion
  7.6 0.9 slice_reduce_fusion
  10.3 3.6 %collective-permute-start.1 = (bf16[336,256]{1,0:T(8,128)(2,1)}, bf16[336,256]{1,0:T(8,128)(2,1)}, u32[]{:S(2)}, u32[]{:S(2)}) collective-permute-start(bf16[336,256]{1,0:T(8,128)(2,1)} %constant_dynamic-update-slice_fusion), channel_id=1, source_target_pairs={{8,0},{16,8},{24,16},{32,24},{40,32},{48,40},{56,48},{64,56},{72,6... | collective-permute-start | bytes 516104 | tf_op jit(solution)/shard_map/ppermute | solution.py:327
  14.6 3.0 %collective-permute-start = (bf16[176,256]{1,0:T(8,128)(2,1)}, bf16[176,256]{1,0:T(8,128)(2,1)}, u32[]{:S(2)}, u32[]{:S(2)}) collective-permute-start(bf16[176,256]{1,0:T(8,128)(2,1)} %pad_maximum_fusion.5), channel_id=1, source_target_pairs={{16,0},{24,8},{32,16},{40,24},{48,32},{56,40},{64,48},{72,56},{80,... | collective-permute-start | bytes 270344 | tf_op jit(solution)/shard_map/ppermute | solution.py:328
  17.6 0.8 compare_reduce_fusion
  18.4 1.0 subtract_reduce_fusion
  35.3 0.9 select_select_fusion.5
  36.3 5.8 %collective-permute-start.2 = (bf16[2,144,256]{2,1,0:T(8,128)(2,1)S(1)}, bf16[2,144,256]{2,1,0:T(8,128)(2,1)}, u32[]{:S(2)}, u32[]{:S(2)}) collective-permute-start(bf16[2,144,256]{2,1,0:T(8,128)(2,1)S(1)} %pad_maximum_fusion.2), channel_id=1, source_target_pairs={{0,8},{8,16},{16,24},{24,32},{32,40},{40,48},{48,56},{56,64},{64,7... | collective-permute-start | bytes 442376 | tf_op jit(solution)/shard_map/ppermute | solution.py:325
  42.8 2.3 %collective-permute-start.3 = (bf16[2,144,256]{2,1,0:T(8,128)(2,1)}, bf16[2,144,256]{2,1,0:T(8,128)(2,1)S(1)}, u32[]{:S(2)}, u32[]{:S(2)}) collective-permute-start(bf16[2,144,256]{2,1,0:T(8,128)(2,1)} %pad_maximum_fusion.3), channel_id=1, source_target_pairs={{0,16},{8,24},{16,32},{24,40},{32,48},{40,56},{48,64},{56,72},{64,... | collective-permute-start | bytes 442376 | tf_op jit(solution)/shard_map/ppermute | solution.py:325
  45.1 1.2 iota_compare_fusion
  46.3 1.1 iota_compare_fusion.1
  52.4 0.7 pad_maximum_fusion.9
  53.1 0.7 pad_maximum_fusion.8
  53.8 0.7 pad_maximum_fusion.10
  55.2 0.7 pad_maximum_fusion.13
  60.7 0.7 sub.150
  61.4 0.7 tile.22
  62.2 0.7 broadcast_in_dim.87
  63.0 0.7 broadcast_in_dim.165
  65.1 0.7 mul.180
  66.4 2.5 %copy.38 = bf16[1,256,4096]{1,2,0:T(8,128)(2,1)} copy(bf16[1,256,4096]{2,1,0:T(8,128)(2,1)S(1)} %copy-done.1) | data formatting | bytes 4194304 | tf_op args[0]
  68.8 2.8 %copy.39 = bf16[32,2,64,256]{3,2,1,0:T(8,128)(2,1)S(1)} copy(bf16[32,2,64,256]{3,0,1,2:T(8,128)(2,1)} %bitcast.108) | data formatting | bytes 4194304 | tf_op jit(solution)/shard_map/transpose | solution.py:331
  72.3 1.8 copy.40
  74.1 1.5 pad.9.holes
  76.3 2.9 %collective-permute-start.4 = (bf16[2,144,256]{2,1,0:T(8,128)(2,1)S(1)}, bf16[2,144,256]{2,1,0:T(8,128)(2,1)S(1)}, u32[]{:S(2)}, u32[]{:S(2)}) collective-permute-start(bf16[2,144,256]{2,1,0:T(8,128)(2,1)S(1)} %copy-done.4), channel_id=1, source_target_pairs={{0,24},{8,32},{16,40},{24,48},{32,56},{40,64},{48,72},{56,80},{64,... | collective-permute-start | bytes 442376 | tf_op jit(solution)/shard_map/ppermute | solution.py:325
  81.1 1.3 slice.430
  83.1 1.2 slice_convert_fusion.1
  84.3 0.9 fusion.22
  86.5 0.7 select_select_fusion.6
  88.6 0.7 copy.47
  89.3 1.0 select_bitcast_fusion.1
  90.3 1.0 pad_maximum_fusion.1.blocks
  91.3 6.8 %terms.3 = bf16[4,4,512,128]{3,2,1,0:T(8,128)(2,1)} custom-call(s32[2]{0:T(128)S(1)} %pad_add_fusion.place, bf16[4,144,256]{2,1,0:T(8,128)(2,1)S(1)} %pad_maximum_fusion.1.blocks, bf16[4096,256]{1,0:T(8,128)(2,1)S(1)} %bitcast.106, bf16[4096,64]{1,0:T(8,128)(2,1)S(1)} %pad.9.holes), custom_call_target="tpu_custom_call" | custom-call | flops 2013265920 | bytes 5242880 | tf_op jit(solution)/shard_map/terms/pallas_call | solution.py:105
  98.1 4.3 %collective-permute-start.5 = (bf16[4,4,512,128]{3,2,1,0:T(8,128)(2,1)}, bf16[4,4,512,128]{3,2,1,0:T(8,128)(2,1)}, u32[]{:S(2)}, u32[]{:S(2)}) collective-permute-start(bf16[4,4,512,128]{3,2,1,0:T(8,128)(2,1)} %terms.3), channel_id=1, source_target_pairs={{0,1},{1,0},{2,3},{3,2},{4,5},{5,4},{6,7},{7,6},{8,9},{9,8},{10,11... | collective-permute-start | bytes 6291464 | tf_op jit(solution)/shard_map/ppermute | solution.py:344
  102.4 1.2 slice.429
  104.2 1.9 select_reduce_fusion.2
  108.7 5.4 %terms.2 = bf16[4,4,512,128]{3,2,1,0:T(8,128)(2,1)S(1)} custom-call(s32[2]{0:T(128)S(1)} %pad_add_fusion.place, bf16[4,144,256]{2,1,0:T(8,128)(2,1)S(1)} %pad_maximum_fusion.blocks, bf16[4096,256]{1,0:T(8,128)(2,1)S(1)} %bitcast.107, bf16[4096,64]{1,0:T(8,128)(2,1)S(1)} %pad.9.holes), custom_call_target="tpu_custom_call" | custom-call | flops 2013265920 | bytes 5242880 | tf_op jit(solution)/shard_map/terms/pallas_call | solution.py:105
  114.7 2.8 %fusion.10 = (bf16[4,512,128]{2,1,0:T(8,128)(2,1)}, bf16[4,512,128]{2,1,0:T(8,128)(2,1)S(1)}, bf16[4,512,128]{2,1,0:T(8,128)(2,1)S(1)}) fusion(bf16[4,4,512,128]{3,2,1,0:T(8,128)(2,1)} %collective-permute-done.5, bf16[4,4,512,128]{3,2,1,0:T(8,128)(2,1)S(1)} %terms.2), kind=kLoop, calls=%fused_computation.22 | loop fusion | flops 3145728 | bytes 4718592 | tf_op jit(solution)/shard_map/convert_element_type | solution.py:349
  117.5 3.2 %collective-permute-start.6 = (bf16[4,512,128]{2,1,0:T(8,128)(2,1)}, bf16[4,512,128]{2,1,0:T(8,128)(2,1)}, u32[]{:S(2)}, u32[]{:S(2)}) collective-permute-start(bf16[4,512,128]{2,1,0:T(8,128)(2,1)} %get-tuple-element.23), channel_id=1, source_target_pairs={{0,2},{1,3},{2,4},{3,5},{4,6},{5,7},{6,0},{7,1},{8,10},{9,11},{10,... | collective-permute-start | bytes 1572872 | tf_op jit(solution)/shard_map/ppermute | solution.py:349
  120.7 4.5 %collective-permute-start.7 = (bf16[4,512,128]{2,1,0:T(8,128)(2,1)S(1)}, bf16[4,512,128]{2,1,0:T(8,128)(2,1)}, u32[]{:S(2)}, u32[]{:S(2)}) collective-permute-start(bf16[4,512,128]{2,1,0:T(8,128)(2,1)S(1)} %get-tuple-element.25), channel_id=1, source_target_pairs={{0,4},{1,5},{2,6},{3,7},{4,0},{5,1},{6,2},{7,3},{8,12},{9,13},{10,... | collective-permute-start | bytes 1572872 | tf_op jit(solution)/shard_map/ppermute | solution.py:349
  125.2 3.0 %collective-permute-start.8 = (bf16[4,512,128]{2,1,0:T(8,128)(2,1)S(1)}, bf16[4,512,128]{2,1,0:T(8,128)(2,1)}, u32[]{:S(2)}, u32[]{:S(2)}) collective-permute-start(bf16[4,512,128]{2,1,0:T(8,128)(2,1)S(1)} %get-tuple-element.24), channel_id=1, source_target_pairs={{0,6},{1,7},{2,0},{3,1},{4,2},{5,3},{6,4},{7,5},{8,14},{9,15},{10,... | collective-permute-start | bytes 1572872 | tf_op jit(solution)/shard_map/ppermute | solution.py:349
  132.2 2.3 %fusion.7 = (f32[2048,128]{1,0:T(8,128)S(1)}, f32[2048,128]{1,0:T(8,128)S(1)}) fusion(f32[2048,64]{1,0:T(8,128)S(1)} %broadcast_in_dim.179, f32[2048,64]{1,0:T(8,128)S(1)} %broadcast_in_dim.177, f32[2048,64]{1,0:T(8,128)S(1)} %broadcast_in_dim.185, f32[2048,64]{1,0:T(8,128)S(1)} %broadcast_in_dim.183, f32[64,32,128]{2,1,0:T(8,128)S(1)} %broadcast_multiply_fusion, ...), kind=kLoop, calls=%fused_computation.10 | loop fusion | flops 4980736 | bytes 9511936 | tf_op jit(solution)/shard_map/sub | solution.py:262
  134.6 12.3 %collective-permute-done.7 = bf16[4,512,128]{2,1,0:T(8,128)(2,1)} collective-permute-done((bf16[4,512,128]{2,1,0:T(8,128)(2,1)S(1)}, bf16[4,512,128]{2,1,0:T(8,128)(2,1)}, u32[]{:S(2)}, u32[]{:S(2)}) %collective-permute-start.7) | collective-permute-done | bytes 524320 | tf_op jit(solution)/shard_map/ppermute | solution.py:349
  146.9 0.9 collective-permute-done.8
  147.8 2.0 %fusion.18 = (bf16[4,512,128]{2,1,0:T(8,128)(2,1)S(1)}, f32[4,512,128]{2,1,0:T(8,128)S(1)}) fusion(bf16[4,512,128]{2,1,0:T(8,128)(2,1)} %collective-permute-done.8, bf16[4,512,128]{2,1,0:T(8,128)(2,1)} %collective-permute-done.7, bf16[4,512,128]{2,1,0:T(8,128)(2,1)} %collective-permute-done.6, bf16[4,4,512,128]{3,2,1,0:T(8,128)(2,1)} %collective-permute-done.5, ...), kind=kLoop, calls=%fused_computation.105 | loop fusion | flops 2621440 | bytes 4194304 | tf_op jit(solution)/shard_map/convert.6
  149.9 3.3 %collective-permute-start.10 = (bf16[512,128]{1,0:T(8,128)(2,1)S(1)}, bf16[512,128]{1,0:T(8,128)(2,1)S(1)}, u32[]{:S(2)}, u32[]{:S(2)}) collective-permute-start(bf16[512,128]{1,0:T(8,128)(2,1)S(1)} %get-tuple-element.27), channel_id=1, source_target_pairs={{16,0},{24,8},{32,16},{40,24},{48,32},{56,40},{64,48},{72,56},{80,... | collective-permute-start | bytes 393224 | tf_op jit(solution)/shard_map/ppermute | solution.py:354
  153.3 5.1 %collective-permute-start.11 = (bf16[512,128]{1,0:T(8,128)(2,1)S(1)}, bf16[512,128]{1,0:T(8,128)(2,1)S(1)}, u32[]{:S(2)}, u32[]{:S(2)}) collective-permute-start(bf16[512,128]{1,0:T(8,128)(2,1)S(1)} %get-tuple-element.26), channel_id=1, source_target_pairs={{24,0},{32,8},{40,16},{48,24},{56,32},{64,40},{72,48},{80,56},{88,... | collective-permute-start | bytes 393224 | tf_op jit(solution)/shard_map/ppermute | solution.py:354
  158.3 1.9 collective-permute-start.9
  160.3 0.8 collective-permute-done.11.three
  161.1 6.3 %collective-permute-done.9.one = bf16[512,128]{1,0:T(8,128)(2,1)S(1)} collective-permute-done((bf16[512,128]{1,0:T(8,128)(2,1)S(1)}, bf16[512,128]{1,0:T(8,128)(2,1)S(1)}, u32[]{:S(2)}, u32[]{:S(2)}) %collective-permute-start.9) | collective-permute-done | bytes 131104 | tf_op jit(solution)/shard_map/ppermute | solution.py:354
  167.4 2.4 %combine.1.w0 = bf16[512,128]{1,0:T(8,128)(2,1)S(1)} custom-call(s32[1]{0:T(128)} %bitcast.4.role, f32[512,128]{1,0:T(8,128)S(1)} %slice_bitcast_fusion.own, bf16[512,128]{1,0:T(8,128)(2,1)S(1)} %collective-permute-done.9.one, bf16[512,128]{1,0:T(8,128)(2,1)S(1)} %collective-permute-done.10.two, bf16[512,128]{1,0:T(8,128)(2,1)S(1)} %collective-permute-done.11.three), custom_call_target="tpu_custom_call" | custom-call | tf_op jit(solution)/shard_map/combine/pallas_call | solution.py:146
  169.8 4.7 %collective-permute-start.12 = (bf16[512,128]{1,0:T(8,128)(2,1)S(1)}, bf16[512,128]{1,0:T(8,128)(2,1)S(1)}, u32[]{:S(2)}, u32[]{:S(2)}) collective-permute-start(bf16[512,128]{1,0:T(8,128)(2,1)S(1)} %combine.1.w0), channel_id=1, source_target_pairs={{0,2},{1,3},{2,4},{3,5},{4,6},{5,7},{6,0},{7,1},{8,10},{9,11},{10,... | collective-permute-start | bytes 393224 | tf_op jit(solution)/shard_map/ppermute | solution.py:358
  174.5 3.2 %collective-permute-start.13 = (bf16[512,128]{1,0:T(8,128)(2,1)S(1)}, bf16[512,128]{1,0:T(8,128)(2,1)S(1)}, u32[]{:S(2)}, u32[]{:S(2)}) collective-permute-start(bf16[512,128]{1,0:T(8,128)(2,1)S(1)} %combine.1.w0), channel_id=1, source_target_pairs={{0,4},{1,5},{2,6},{3,7},{4,0},{5,1},{6,2},{7,3},{8,12},{9,13},{10,... | collective-permute-start | bytes 393224 | tf_op jit(solution)/shard_map/ppermute | solution.py:358
  177.7 3.0 %collective-permute-start.14 = (bf16[512,128]{1,0:T(8,128)(2,1)S(1)}, bf16[512,128]{1,0:T(8,128)(2,1)S(1)}, u32[]{:S(2)}, u32[]{:S(2)}) collective-permute-start(bf16[512,128]{1,0:T(8,128)(2,1)S(1)} %combine.1.w0), channel_id=1, source_target_pairs={{0,6},{1,7},{2,0},{3,1},{4,2},{5,3},{6,4},{7,5},{8,14},{9,15},{10,... | collective-permute-start | bytes 393224 | tf_op jit(solution)/shard_map/ppermute | solution.py:358
  180.9 1.3 collective-permute-done.13.w2
  182.2 2.2 %collective-permute-done.14.w3 = bf16[512,128]{1,0:T(8,128)(2,1)S(1)} collective-permute-done((bf16[512,128]{1,0:T(8,128)(2,1)S(1)}, bf16[512,128]{1,0:T(8,128)(2,1)S(1)}, u32[]{:S(2)}, u32[]{:S(2)}) %collective-permute-start.14) | collective-permute-done | bytes 131104 | tf_op jit(solution)/shard_map/ppermute | solution.py:358
  184.4 6.8 %energy.1 = f32[8,64]{1,0:T(8,128)S(1)} custom-call(s32[2]{0:T(128)S(1)} %pad_add_fusion.place, bf16[512,128]{1,0:T(8,128)(2,1)S(1)} %combine.1.w0, bf16[512,128]{1,0:T(8,128)(2,1)S(1)} %collective-permute-done.12.w1, bf16[512,128]{1,0:T(8,128)(2,1)S(1)} %collective-permute-done.13.w2, bf16[512,128]{1,0:T(8,128)(2,1)S(1)} %collective-permute-done.14.w3, ...), custom_call_target="tpu_custom_call" | custom-call | tf_op jit(solution)/shard_map/energy/pallas_call | solution.py:197
  191.2 0.7 fusion.38
  191.9 4.8 %collective-permute-start.16 = (f32[64]{0:T(128)S(1)}, f32[64]{0:T(128)S(1)}, u32[]{:S(2)}, u32[]{:S(2)}) collective-permute-start(f32[64]{0:T(128)S(1)} %fusion.38), channel_id=1, source_target_pairs={{0,1},{1,0},{2,3},{3,2},{4,5},{5,4},{6,7},{7,6},{8,9},{9,8},{10,11... | collective-permute-start | bytes 776 | tf_op jit(solution)/shard_map/ppermute | solution.py:386
  196.8 0.7 broadcast_select_fusion.4
  (175 shorter events, 21.4 us)
Async XLA Ops:
  0.0 48.7 %copy-start.7 = (bf16[1,3,4096]{2,1,0:T(4,128)(2,1)S(1)}, bf16[1,3,4096]{2,1,0:T(4,128)(2,1)}, u32[]{:S(2)}) copy-start(bf16[1,3,4096]{2,1,0:T(4,128)(2,1)} %param.13) | copy-start | bytes 73732
  1.5 74.8 %collective-permute-start.15 = (bf16[16,256]{1,0:T(8,128)(2,1)S(1)}, bf16[16,256]{1,0:T(8,128)(2,1)S(1)}, u32[]{:S(2)}, u32[]{:S(2)}) collective-permute-start(bf16[16,256]{1,0:T(8,128)(2,1)S(1)} %reshape.335), channel_id=1, source_target_pairs={{24,0},{32,8},{40,16},{48,24},{56,32},{64,40},{72,48},{80,56},{88,... | collective-permute-start | bytes 24584 | tf_op jit(solution)/shard_map/ppermute | solution.py:329
  4.5 47.7 %copy-start.19 = (f32[64]{0:T(128)S(1)}, f32[64]{0:T(128)}, u32[]{:S(2)}) copy-start(f32[64]{0:T(128)} %param.16) | copy-start | bytes 772
  10.3 76.2 %collective-permute-start.1 = (bf16[336,256]{1,0:T(8,128)(2,1)}, bf16[336,256]{1,0:T(8,128)(2,1)}, u32[]{:S(2)}, u32[]{:S(2)}) collective-permute-start(bf16[336,256]{1,0:T(8,128)(2,1)} %constant_dynamic-update-slice_fusion), channel_id=1, source_target_pairs={{8,0},{16,8},{24,16},{32,24},{40,32},{48,40},{56,48},{64,56},{72,6... | collective-permute-start | bytes 516104 | tf_op jit(solution)/shard_map/ppermute | solution.py:327
  14.6 66.5 %collective-permute-start = (bf16[176,256]{1,0:T(8,128)(2,1)}, bf16[176,256]{1,0:T(8,128)(2,1)}, u32[]{:S(2)}, u32[]{:S(2)}) collective-permute-start(bf16[176,256]{1,0:T(8,128)(2,1)} %pad_maximum_fusion.5), channel_id=1, source_target_pairs={{16,0},{24,8},{32,16},{40,24},{48,32},{56,40},{64,48},{72,56},{80,... | collective-permute-start | bytes 270344 | tf_op jit(solution)/shard_map/ppermute | solution.py:328
  33.2 33.2 %copy-start.1 = (bf16[1,256,4096]{2,1,0:T(8,128)(2,1)S(1)}, bf16[1,256,4096]{2,1,0:T(8,128)(2,1)}, u32[]{:S(2)}) copy-start(bf16[1,256,4096]{2,1,0:T(8,128)(2,1)} %param.9) | copy-start | bytes 6291460
  36.3 48.0 %collective-permute-start.2 = (bf16[2,144,256]{2,1,0:T(8,128)(2,1)S(1)}, bf16[2,144,256]{2,1,0:T(8,128)(2,1)}, u32[]{:S(2)}, u32[]{:S(2)}) collective-permute-start(bf16[2,144,256]{2,1,0:T(8,128)(2,1)S(1)} %pad_maximum_fusion.2), channel_id=1, source_target_pairs={{0,8},{8,16},{16,24},{24,32},{32,40},{40,48},{48,56},{56,64},{64,7... | collective-permute-start | bytes 442376 | tf_op jit(solution)/shard_map/ppermute | solution.py:325
  42.8 42.4 %collective-permute-start.3 = (bf16[2,144,256]{2,1,0:T(8,128)(2,1)}, bf16[2,144,256]{2,1,0:T(8,128)(2,1)S(1)}, u32[]{:S(2)}, u32[]{:S(2)}) collective-permute-start(bf16[2,144,256]{2,1,0:T(8,128)(2,1)} %pad_maximum_fusion.3), channel_id=1, source_target_pairs={{0,16},{8,24},{16,32},{24,40},{32,48},{40,56},{48,64},{56,72},{64,... | collective-permute-start | bytes 442376 | tf_op jit(solution)/shard_map/ppermute | solution.py:325
  47.5 21.4 %copy-start.20 = (f32[1,64]{1,0:T(1,128)}, f32[1,64]{1,0:T(1,128)S(1)}, u32[]{:S(2)}) copy-start(f32[1,64]{1,0:T(1,128)S(1)} %get-tuple-element.59) | copy-start | bytes 772
  68.8 2.8 %copy-start.2 = (bf16[1,38,4096]{2,1,0:T(8,128)(2,1)S(1)}, bf16[1,38,4096]{2,1,0:T(8,128)(2,1)}, u32[]{:S(2)}) copy-start(bf16[1,38,4096]{2,1,0:T(8,128)(2,1)} %param.11) | copy-start | bytes 933892
  74.1 2.2 %copy-start.4 = (bf16[2,144,256]{2,1,0:T(8,128)(2,1)S(1)}, bf16[2,144,256]{2,1,0:T(8,128)(2,1)}, u32[]{:S(2)}) copy-start(bf16[2,144,256]{2,1,0:T(8,128)(2,1)} %pad_maximum_fusion.4) | copy-start | bytes 442372
  76.3 9.6 %collective-permute-start.4 = (bf16[2,144,256]{2,1,0:T(8,128)(2,1)S(1)}, bf16[2,144,256]{2,1,0:T(8,128)(2,1)S(1)}, u32[]{:S(2)}, u32[]{:S(2)}) collective-permute-start(bf16[2,144,256]{2,1,0:T(8,128)(2,1)S(1)} %copy-done.4), channel_id=1, source_target_pairs={{0,24},{8,32},{16,40},{24,48},{32,56},{40,64},{48,72},{56,80},{64,... | collective-permute-start | bytes 442376 | tf_op jit(solution)/shard_map/ppermute | solution.py:325
  91.3 16.7 %copy-start.21 = (f32[1,64]{1,0:T(1,128)S(1)}, f32[1,64]{1,0:T(1,128)}, u32[]{:S(2)}) copy-start(f32[1,64]{1,0:T(1,128)} %copy-done.20) | copy-start | bytes 772
  91.3 16.7 %copy-start.23 = (pred[4]{0:T(512)(128)(4,1)S(1)}, pred[4]{0:T(512)(128)(4,1)}, u32[]{:S(2)}) copy-start(pred[4]{0:T(512)(128)(4,1)} %iota_compare_fusion) | copy-start | bytes 16
  91.3 16.6 %copy-start.24 = (pred[4]{0:T(512)(128)(4,1)S(1)}, pred[4]{0:T(512)(128)(4,1)}, u32[]{:S(2)}) copy-start(pred[4]{0:T(512)(128)(4,1)} %iota_compare_fusion.1) | copy-start | bytes 16
  91.3 16.6 %copy-start.25 = (f32[1,64]{1,0:T(1,128)S(1)}, f32[1,64]{1,0:T(1,128)}, u32[]{:S(2)}) copy-start(f32[1,64]{1,0:T(1,128)} %slice_convert_fusion) | copy-start | bytes 772
  91.3 16.6 %copy-start.26 = (f32[1,64]{1,0:T(1,128)S(1)}, f32[1,64]{1,0:T(1,128)}, u32[]{:S(2)}) copy-start(f32[1,64]{1,0:T(1,128)} %slice_convert_fusion.1) | copy-start | bytes 772
  98.1 16.5 %collective-permute-start.5 = (bf16[4,4,512,128]{3,2,1,0:T(8,128)(2,1)}, bf16[4,4,512,128]{3,2,1,0:T(8,128)(2,1)}, u32[]{:S(2)}, u32[]{:S(2)}) collective-permute-start(bf16[4,4,512,128]{3,2,1,0:T(8,128)(2,1)} %terms.3), channel_id=1, source_target_pairs={{0,1},{1,0},{2,3},{3,2},{4,5},{5,4},{6,7},{7,6},{8,9},{9,8},{10,11... | collective-permute-start | bytes 6291464 | tf_op jit(solution)/shard_map/ppermute | solution.py:344
  108.7 5.6 %copy-start.3 = (f32[64,64]{0,1:T(8,128)S(1)}, f32[64,64]{0,1:T(8,128)}, u32[]{:S(2)}) copy-start(f32[64,64]{0,1:T(8,128)} %copy.47) | copy-start | bytes 49156
  108.7 5.6 %copy-start.5 = (f32[64,128]{1,0:T(8,128)S(1)}, f32[64,128]{1,0:T(8,128)}, u32[]{:S(2)}) copy-start(f32[64,128]{1,0:T(8,128)} %sub.150) | copy-start | bytes 98308
  108.7 5.8 %copy-start.6 = (f32[64,128]{1,0:T(8,128)S(1)}, f32[64,128]{1,0:T(8,128)}, u32[]{:S(2)}) copy-start(f32[64,128]{1,0:T(8,128)} %tile.22) | copy-start | bytes 98308
  114.2 3.3 %copy-start = (bf16[4,4,512,128]{3,2,1,0:T(8,128)(2,1)}, bf16[4,4,512,128]{3,2,1,0:T(8,128)(2,1)S(1)}, u32[]{:S(2)}) copy-start(bf16[4,4,512,128]{3,2,1,0:T(8,128)(2,1)S(1)} %terms.2) | copy-start | bytes 6291460
  114.6 13.6 %copy-start.12 = (f32[32,64]{1,0:T(8,128)S(1)}, f32[32,64]{1,0:T(8,128)}, u32[]{:S(2)}) copy-start(f32[32,64]{1,0:T(8,128)} %slice.369) | copy-start | bytes 24580
  114.6 13.6 %copy-start.13 = (f32[32,64]{1,0:T(8,128)S(1)}, f32[32,64]{1,0:T(8,128)}, u32[]{:S(2)}) copy-start(f32[32,64]{1,0:T(8,128)} %slice.371) | copy-start | bytes 24580
  114.6 14.6 %copy-start.11 = (f32[32,128]{1,0:T(8,128)S(1)}, f32[32,128]{1,0:T(8,128)}, u32[]{:S(2)}) copy-start(f32[32,128]{1,0:T(8,128)} %pad_maximum_fusion.9) | copy-start | bytes 49156
  117.5 17.1 %collective-permute-start.6 = (bf16[4,512,128]{2,1,0:T(8,128)(2,1)}, bf16[4,512,128]{2,1,0:T(8,128)(2,1)}, u32[]{:S(2)}, u32[]{:S(2)}) collective-permute-start(bf16[4,512,128]{2,1,0:T(8,128)(2,1)} %get-tuple-element.23), channel_id=1, source_target_pairs={{0,2},{1,3},{2,4},{3,5},{4,6},{5,7},{6,0},{7,1},{8,10},{9,11},{10,... | collective-permute-start | bytes 1572872 | tf_op jit(solution)/shard_map/ppermute | solution.py:349
  120.7 26.2 %collective-permute-start.7 = (bf16[4,512,128]{2,1,0:T(8,128)(2,1)S(1)}, bf16[4,512,128]{2,1,0:T(8,128)(2,1)}, u32[]{:S(2)}, u32[]{:S(2)}) collective-permute-start(bf16[4,512,128]{2,1,0:T(8,128)(2,1)S(1)} %get-tuple-element.25), channel_id=1, source_target_pairs={{0,4},{1,5},{2,6},{3,7},{4,0},{5,1},{6,2},{7,3},{8,12},{9,13},{10,... | collective-permute-start | bytes 1572872 | tf_op jit(solution)/shard_map/ppermute | solution.py:349
  125.2 22.6 %collective-permute-start.8 = (bf16[4,512,128]{2,1,0:T(8,128)(2,1)S(1)}, bf16[4,512,128]{2,1,0:T(8,128)(2,1)}, u32[]{:S(2)}, u32[]{:S(2)}) collective-permute-start(bf16[4,512,128]{2,1,0:T(8,128)(2,1)S(1)} %get-tuple-element.24), channel_id=1, source_target_pairs={{0,6},{1,7},{2,0},{3,1},{4,2},{5,3},{6,4},{7,5},{8,14},{9,15},{10,... | collective-permute-start | bytes 1572872 | tf_op jit(solution)/shard_map/ppermute | solution.py:349
  129.4 1.4 copy-start.14
  129.7 1.4 copy-start.16
  130.1 1.4 copy-start.17
  130.4 1.4 copy-start.18
  130.7 1.4 copy-start.9
  130.8 1.4 copy-start.10
  130.8 1.4 copy-start.15
  130.8 1.4 copy-start.22
  149.9 30.8 %copy-start.8 = (f32[32,128]{1,0:T(8,128)S(1)}, f32[32,128]{1,0:T(8,128)}, u32[]{:S(2)}) copy-start(f32[32,128]{1,0:T(8,128)} %pad_maximum_fusion.13) | copy-start | bytes 49156
  149.9 10.4 %collective-permute-start.10 = (bf16[512,128]{1,0:T(8,128)(2,1)S(1)}, bf16[512,128]{1,0:T(8,128)(2,1)S(1)}, u32[]{:S(2)}, u32[]{:S(2)}) collective-permute-start(bf16[512,128]{1,0:T(8,128)(2,1)S(1)} %get-tuple-element.27), channel_id=1, source_target_pairs={{16,0},{24,8},{32,16},{40,24},{48,32},{56,40},{64,48},{72,56},{80,... | collective-permute-start | bytes 393224 | tf_op jit(solution)/shard_map/ppermute | solution.py:354
  153.3 7.8 %collective-permute-start.11 = (bf16[512,128]{1,0:T(8,128)(2,1)S(1)}, bf16[512,128]{1,0:T(8,128)(2,1)S(1)}, u32[]{:S(2)}, u32[]{:S(2)}) collective-permute-start(bf16[512,128]{1,0:T(8,128)(2,1)S(1)} %get-tuple-element.26), channel_id=1, source_target_pairs={{24,0},{32,8},{40,16},{48,24},{56,32},{64,40},{72,48},{80,56},{88,... | collective-permute-start | bytes 393224 | tf_op jit(solution)/shard_map/ppermute | solution.py:354
  158.3 9.0 %collective-permute-start.9 = (bf16[512,128]{1,0:T(8,128)(2,1)S(1)}, bf16[512,128]{1,0:T(8,128)(2,1)S(1)}, u32[]{:S(2)}, u32[]{:S(2)}) collective-permute-start(bf16[512,128]{1,0:T(8,128)(2,1)S(1)} %get-tuple-element.28), channel_id=1, source_target_pairs={{8,0},{16,8},{24,16},{32,24},{40,32},{48,40},{56,48},{64,56},{72,6... | collective-permute-start | bytes 393224 | tf_op jit(solution)/shard_map/ppermute | solution.py:354
  169.8 11.1 %collective-permute-start.12 = (bf16[512,128]{1,0:T(8,128)(2,1)S(1)}, bf16[512,128]{1,0:T(8,128)(2,1)S(1)}, u32[]{:S(2)}, u32[]{:S(2)}) collective-permute-start(bf16[512,128]{1,0:T(8,128)(2,1)S(1)} %combine.1.w0), channel_id=1, source_target_pairs={{0,2},{1,3},{2,4},{3,5},{4,6},{5,7},{6,0},{7,1},{8,10},{9,11},{10,... | collective-permute-start | bytes 393224 | tf_op jit(solution)/shard_map/ppermute | solution.py:358
  174.5 7.7 %collective-permute-start.13 = (bf16[512,128]{1,0:T(8,128)(2,1)S(1)}, bf16[512,128]{1,0:T(8,128)(2,1)S(1)}, u32[]{:S(2)}, u32[]{:S(2)}) collective-permute-start(bf16[512,128]{1,0:T(8,128)(2,1)S(1)} %combine.1.w0), channel_id=1, source_target_pairs={{0,4},{1,5},{2,6},{3,7},{4,0},{5,1},{6,2},{7,3},{8,12},{9,13},{10,... | collective-permute-start | bytes 393224 | tf_op jit(solution)/shard_map/ppermute | solution.py:358
  177.7 6.7 %collective-permute-start.14 = (bf16[512,128]{1,0:T(8,128)(2,1)S(1)}, bf16[512,128]{1,0:T(8,128)(2,1)S(1)}, u32[]{:S(2)}, u32[]{:S(2)}) collective-permute-start(bf16[512,128]{1,0:T(8,128)(2,1)S(1)} %combine.1.w0), channel_id=1, source_target_pairs={{0,6},{1,7},{2,0},{3,1},{4,2},{5,3},{6,4},{7,5},{8,14},{9,15},{10,... | collective-permute-start | bytes 393224 | tf_op jit(solution)/shard_map/ppermute | solution.py:358
  191.9 5.6 %collective-permute-start.16 = (f32[64]{0:T(128)S(1)}, f32[64]{0:T(128)S(1)}, u32[]{:S(2)}, u32[]{:S(2)}) collective-permute-start(f32[64]{0:T(128)S(1)} %fusion.38), channel_id=1, source_target_pairs={{0,1},{1,0},{2,3},{3,2},{4,5},{5,4},{6,7},{7,6},{8,9},{9,8},{10,11... | collective-permute-start | bytes 776 | tf_op jit(solution)/shard_map/ppermute | solution.py:386

commit v2 on v1

v2 whole, which is shorter than its diff:
```python
import functools

import jax
import jax.numpy as jnp
from jax import lax
from jax.experimental import pallas as pl
from jax.experimental.pallas import tpu as pltpu
from jax.sharding import PartitionSpec as P

T = 64
H = 32
F32 = jnp.float32
BF16 = jnp.bfloat16
CROWS = 16
BLOCK_ROWS = 2 * T + CROWS
VMEM_LIMIT = 48 * 1024 * 1024


def shift_route(size, distance):
    return [(i, i + distance) for i in range(size) if 0 <= i + distance < size]


def ring_route(step):
    return [(i, (i + 2 * step) % 8) for i in range(8)]


CORE_ROUTE = [(i, i ^ 1) for i in range(8)]


def lane_low(rows):
    return lax.broadcasted_iota(jnp.int32, (rows, 2 * T), 1) < T


def swap_halves(x):
    return jnp.concatenate([x[:, T:], x[:, :T]], axis=1)


def pack_rows(rows64):
    low = lane_low(H)
    top, bottom = rows64[:H], rows64[H:]
    first = jnp.where(low, top, swap_halves(bottom))
    second = jnp.where(low, swap_halves(top), bottom)
    return first, second


def row_of(triples, owner, core, rel):
    s = jnp.where(core == 0, rel, 1 - rel)
    live = triples[s, 0] >= 0
    off_i = jnp.where(live, triples[s, 0] - owner, 2)
    off_j = jnp.where(live, triples[s, 1] - owner, 1)
    return off_i, off_j, live


def prep_kernel(triples, amps, coulomb, out1, out2, out3, up1, up2, blocks):
    owner, core = lax.axis_index("trip"), lax.rem(lax.axis_index("virt"), 2)
    occ_rows = coulomb.shape[1]
    for s in range(3):
        blocks[s, : 2 * T, :] = amps[s]
        turned = jnp.concatenate(
            [coulomb[s].astype(F32), jnp.zeros((T - occ_rows, T), F32)], axis=0
        ).T
        packed = jnp.concatenate([-turned[g * CROWS : (g + 1) * CROWS] for g in range(4)], axis=1)
        blocks[s, 2 * T :, :] = packed.astype(BF16)
    up1[...] = blocks[0:2]
    up2[...] = blocks[0]
    for rel in range(2):
        off_i, off_j, live = row_of(triples, owner, core, rel)
        for d, out in ((1, out1), (2, out2), (3, out3)):
            takes_part = live & ((off_i == d) | (off_j == d))
            other = jnp.clip(off_i + off_j - d - 1, 0, 2)

            @pl.when(takes_part)
            def _():
                out[rel] = blocks[other]

            @pl.when(jnp.logical_not(takes_part))
            def _():
                out[rel] = jnp.zeros((BLOCK_ROWS, 4 * T), BF16)


def prep(triples, amps, coulomb):
    vmem = pl.BlockSpec(memory_space=pltpu.VMEM)
    two = jax.ShapeDtypeStruct((2, BLOCK_ROWS, 4 * T), BF16)
    one = jax.ShapeDtypeStruct((BLOCK_ROWS, 4 * T), BF16)
    return pl.pallas_call(
        prep_kernel,
        out_shape=(two, two, two, two, one),
        in_specs=[pl.BlockSpec(memory_space=pltpu.SMEM), vmem, vmem],
        out_specs=[vmem] * 5,
        scratch_shapes=[pltpu.VMEM((3, BLOCK_ROWS, 4 * T), BF16)],
        compiler_params=pltpu.CompilerParams(vmem_limit_bytes=VMEM_LIMIT),
        name="prep",
    )(triples, amps, coulomb)


def panels_kernel(integrals, holes, panels_out, holes_out, spread_a, spread_b):
    occ_rows = holes.shape[0]

    def one_chunk(chunk, _):
        columns = pl.ds(pl.multiple_of(chunk * 2 * T, 2 * T), 2 * T)
        turned = integrals[:, columns].astype(F32).T
        hole = holes[:, columns].astype(F32)
        hole = jnp.concatenate([hole, jnp.zeros((T - occ_rows, 2 * T), F32)], axis=0)
        hole = jnp.concatenate([hole, hole], axis=0).T
        for part in range(4):
            at = pl.ds((part % 2) * T + chunk * 2 + part // 2, H, stride=2 * T)
            spread_a[at, :] = turned[part * H : (part + 1) * H, : 2 * T]
            spread_b[at, :] = turned[part * H : (part + 1) * H, 2 * T :]
        for w in range(2):
            third = chunk * 2 + w
            at = lax.rem(third, H) * 2 * T + (third // H) * T
            holes_out[pl.ds(pl.multiple_of(at, T), T), :] = hole[w * T : (w + 1) * T].astype(BF16)
        return 0

    lax.fori_loop(0, H, one_chunk, 0, unroll=2)

    def settle(step, _):
        rows = pl.ds(pl.multiple_of(step * 2 * T, 2 * T), 2 * T)
        panels_out[rows, : 2 * T] = spread_a[rows, :].astype(BF16)
        panels_out[rows, 2 * T :] = spread_b[rows, :].astype(BF16)
        return 0

    lax.fori_loop(0, H, settle, 0, unroll=2)


def panels_of(integrals, holes):
    vmem = pl.BlockSpec(memory_space=pltpu.VMEM)
    return pl.pallas_call(
        panels_kernel,
        out_shape=(
            jax.ShapeDtypeStruct((T * T, 4 * T), BF16),
            jax.ShapeDtypeStruct((T * T, 2 * T), BF16),
        ),
        in_specs=[vmem, vmem],
        out_specs=[vmem, vmem],
        scratch_shapes=[pltpu.VMEM((T * T, 2 * T), F32)] * 2,
        compiler_params=pltpu.CompilerParams(vmem_limit_bytes=VMEM_LIMIT),
        cost_estimate=pl.CostEstimate(flops=1 << 28, bytes_accessed=5 << 20, transcendentals=0),
        name="panels",
    )(integrals, holes)


def terms_kernel(rel, triples, got_one, got_two, in1, in2, in3, panels, holes, out, chosen):
    virt = lax.axis_index("virt")
    y, core = virt // 2, lax.rem(virt, 2)
    off_i, off_j, live = row_of(triples, lax.axis_index("trip"), core, rel)
    which = jnp.where(live, off_i + off_j - 3, 3)
    for at, option in enumerate((got_one.at[0], got_one.at[1], got_two)):

        @pl.when(which == at)
        def _():
            chosen[...] = option[...]

    @pl.when(which == 3)
    def _():
        chosen[...] = jnp.zeros_like(chosen)

    blocks = (chosen, in1.at[rel], in2.at[rel], in3.at[rel])
    amps_lead, amps_dup, coul_lead, coul_dup = [], [], [], []
    for d in range(4):
        block = blocks[d][...]
        second = block[T : 2 * T]
        amps_lead.append(block[:T])
        amps_dup += [second, second]
        packed = block[2 * T :]
        coulomb = jnp.concatenate(
            [packed[:, g * T : (g + 1) * T] for g in range(4)], axis=0
        )
        coul_lead.append(coulomb)
        coul_dup += [coulomb, coulomb]
    amps_lead = jnp.concatenate(amps_lead, axis=0)
    amps_dup = jnp.concatenate(amps_dup, axis=0)
    coul_lead = jnp.concatenate(coul_lead, axis=0)
    coul_dup = jnp.concatenate(coul_dup, axis=0)
    low = lane_low(T)
    contract = (((1,), (1,)), ((), ()))

    def group(step, _):
        rows = pl.ds(pl.multiple_of(step * 8 * T, 8 * T), 8 * T)
        panel = panels[rows, :]
        hole = holes[rows, :T]
        by_rows = lax.dot_general(panel, amps_dup, contract, preferred_element_type=F32)
        by_rows += lax.dot_general(hole, coul_dup, contract, preferred_element_type=F32)
        by_cols = lax.dot_general(amps_lead, panel, contract, preferred_element_type=F32)
        by_cols += lax.dot_general(coul_lead, hole, contract, preferred_element_type=F32)
        own = lax.rem(step // 2 - y + 4, 4)
        for pair in range(4):
            row = pair * 2 * T
            for d in range(4):
                col = d * 2 * T
                tile = jnp.where(
                    low,
                    by_rows[row : row + T, col : col + 2 * T],
                    by_rows[row + T : row + 2 * T, col : col + 2 * T],
                )
                tile += by_cols[d * T : (d + 1) * T, row : row + 2 * T]
                if d == 0:
                    at = pl.multiple_of((lax.rem(step, 2) * 4 + pair) * T, T)
                    out[own, 0, pl.ds(at, T), :] = tile.astype(BF16)
                else:
                    at = pl.multiple_of((step * 4 + pair) * 16, 16)
                    for quarter in range(4):
                        rows16 = jnp.concatenate(
                            [
                                tile[8 * quarter : 8 * quarter + 8],
                                tile[H + 8 * quarter : H + 8 * quarter + 8],
                            ],
                            axis=0,
                        )
                        out[lax.rem(quarter - y + 4, 4), d, pl.ds(at, 16), :] = rows16.astype(BF16)
        return 0

    lax.fori_loop(0, 8, group, 0)


def terms(rel, triples, blocks, panels, holes):
    vmem = pl.BlockSpec(memory_space=pltpu.VMEM)
    return pl.pallas_call(
        functools.partial(terms_kernel, rel),
        out_shape=jax.ShapeDtypeStruct((4, 4, 512, 2 * T), BF16),
        in_specs=[pl.BlockSpec(memory_space=pltpu.SMEM)] + [vmem] * 7,
        out_specs=vmem,
        scratch_shapes=[pltpu.VMEM((BLOCK_ROWS, 4 * T), BF16)],
        compiler_params=pltpu.CompilerParams(vmem_limit_bytes=VMEM_LIMIT),
        cost_estimate=pl.CostEstimate(
            flops=2 * 4096 * 320 * 768, bytes_accessed=5 << 20, transcendentals=0
        ),
        name="terms",
    )(triples, *blocks, panels, holes)


def combine_kernel(triples, own, one, two, three, out, scratch):
    core = lax.rem(lax.axis_index("virt"), 2)
    _, off_j, _ = row_of(triples, lax.axis_index("trip"), core, 0)
    for index, part in enumerate((one, two, three)):
        scratch[index * 512 : (index + 1) * 512, :] = part[...].astype(F32)
    mid_is_j = jnp.full((T, 2 * T), off_j, jnp.int32) == 2

    def as_rows(index, cp):
        low_rows = scratch[pl.ds(index * 512 + cp, H, stride=16), :]
        high_rows = scratch[pl.ds(index * 512 + 8 + cp, H, stride=16), :]
        low = lane_low(H)
        top = jnp.where(low, low_rows, swap_halves(high_rows))
        bottom = jnp.where(low, swap_halves(low_rows), high_rows)
        return jnp.concatenate([top, bottom], axis=0)

    def turned(x):
        flat = x.T
        return jnp.concatenate([flat[:T], flat[T:]], axis=1)

    for cp in range(8):
        total = own[cp * T : (cp + 1) * T, :].astype(F32)
        total += as_rows(0, cp)
        middle = as_rows(1, cp)
        total += jnp.where(mid_is_j, middle, turned(middle))
        total += turned(as_rows(2, cp))
        out[cp * T : (cp + 1) * T, :] = total.astype(BF16)


def combine(triples, own, one, two, three):
    vmem = pl.BlockSpec(memory_space=pltpu.VMEM)
    return pl.pallas_call(
        combine_kernel,
        out_shape=jax.ShapeDtypeStruct((512, 2 * T), BF16),
        in_specs=[pl.BlockSpec(memory_space=pltpu.SMEM)] + [vmem] * 4,
        out_specs=vmem,
        scratch_shapes=[pltpu.VMEM((3 * 512, 2 * T), F32)],
        compiler_params=pltpu.CompilerParams(vmem_limit_bytes=VMEM_LIMIT),
        name="combine",
    )(triples, own, one, two, three)


def energy_kernel(triples, w0, w1, w2, w3, extra_a, extra_b, inverse, out, whole, flipped, acc, rows_b):
    virt = lax.axis_index("virt")
    y, core = virt // 2, lax.rem(virt, 2)
    _, _, live = row_of(triples, lax.axis_index("trip"), core, 0)
    for j, part in enumerate((w0, w1, w2, w3)):
        at = pl.multiple_of(lax.rem(y - j + 4, 4) * 512, 512)
        whole[pl.ds(at, 512), :] = part[...].astype(F32)

    def flip(b, _):
        across = whole[pl.ds(b, H, stride=T), :].T
        flipped[pl.ds(pl.multiple_of(b * H, H), H), :] = jnp.concatenate(
            [across[0:H], across[T : T + H], across[H:T], across[T + H :]], axis=1
        )
        return 0

    lax.fori_loop(0, T, flip, 0, unroll=4)
    acc[...] = jnp.zeros_like(acc)

    def pair(bp, _):
        from_flipped = pack_rows(flipped[pl.ds(bp, T, stride=H), :])
        from_whole = pack_rows(whole[pl.ds(pl.multiple_of(bp * T, T), T), :])
        for half in range(2):
            b = bp + H * half
            at = pl.ds(pl.multiple_of(b * H, H), H)
            plain = whole[pl.ds(b, H, stride=T), :]
            turned = flipped[at, :]
            inv = inverse[at, :]
            first = (4.0 * plain + from_flipped[half]) * (plain - turned + extra_a[at, :]) * inv
            second = plain * (from_flipped[half] - from_whole[half] + extra_b[at, :]) * inv
            acc[...] += first
            rows_b[pl.ds(b, 1), :] = jnp.sum(second, axis=0, keepdims=True)
        return 0

    lax.fori_loop(0, H, pair, 0, unroll=2)
    by_a = jnp.sum(acc[...], axis=0, keepdims=True)
    by_a = by_a[:, :T] + by_a[:, T:]
    by_b = jnp.sum(rows_b[...].T, axis=0, keepdims=True)
    out[...] = jnp.where(live, by_a + by_b, 0.0)


def energy_of(triples, parts, extra_a, extra_b, inverse):
    vmem = pl.BlockSpec(memory_space=pltpu.VMEM)
    return pl.pallas_call(
        energy_kernel,
        out_shape=jax.ShapeDtypeStruct((1, T), F32),
        in_specs=[pl.BlockSpec(memory_space=pltpu.SMEM)] + [vmem] * 7,
        out_specs=vmem,
        scratch_shapes=[
            pltpu.VMEM((H * T, 2 * T), F32),
            pltpu.VMEM((H * T, 2 * T), F32),
            pltpu.VMEM((H, 2 * T), F32),
            pltpu.VMEM((T, 2 * T), F32),
        ],
        compiler_params=pltpu.CompilerParams(vmem_limit_bytes=VMEM_LIMIT),
        name="energy",
    )(triples, *parts, extra_a, extra_b, inverse)


def tables_kernel(
    triples, own, one, two, three, virt_energy, extra_a, extra_b, inverse, columns, rows, scalars
):
    core = lax.rem(lax.axis_index("virt"), 2)
    off_i, off_j, _ = row_of(triples, lax.axis_index("trip"), core, 0)
    low = lane_low(H)

    def exch(table, index):
        return table[index * T : (index + 1) * T, :].astype(F32)

    def pick(options, index):
        result = options[-1]
        for at in range(len(options) - 1):
            result = jnp.where(index == at, options[at], result)
        return result

    kj = pick([exch(own, 0), exch(own, 1)], off_j - 1)
    ki = pick([exch(own, 1), exch(own, 2)], off_i - 2)
    ji = pick([exch(one, 0), exch(one, 1), exch(two, 0)], off_i + off_j - 3)
    kj_t, ki_t, ji_t = kj.T, ki.T, ji.T
    heads = [x[3 * T : 3 * T + 8, :].astype(F32) for x in (own, one, two, three)]
    head_i = pick([heads[2], heads[3]], off_i - 2)
    head_j = pick([heads[1], heads[2]], off_j - 1)
    head_k = heads[0]
    occ = head_i[1:2] + head_j[1:2] + head_k[1:2]
    occ = jnp.concatenate([occ, occ], axis=1)

    def dup(m):
        return jnp.concatenate([m, m], axis=1)

    def by_row(v):
        return jnp.broadcast_to(v, (2 * T, T)).T

    def by_c(column):
        return jnp.where(low, column[:H], column[H:])

    def packed(m):
        return jnp.concatenate([m[:H], m[H:]], axis=1)

    s_i, s_j, s_k, e_v = head_i[0:1], head_j[0:1], head_k[0:1], virt_energy[...]
    for at, v in enumerate((s_i, s_j, s_k, e_v)):
        scalars[at * T : (at + 1) * T, :] = by_row(v)
    si_a, sk_a, e_a = dup(s_i), dup(s_k), dup(e_v)
    si_c, sj_c, sk_c, e_c = (by_c(scalars[at * T : (at + 1) * T, :]) for at in range(4))
    for at, m in enumerate((kj, ji_t, kj_t, ji)):
        columns[at * H : (at + 1) * H, :] = packed(m).astype(BF16)
    for at, m in enumerate((kj_t, ji, ki_t - ki)):
        rows[at * T : (at + 1) * T, :] = dup(m)
    ki_diff = packed(ki - ki_t)
    kj_ac = packed(kj_t)
    ji_ca = packed(ji)
    base = occ - e_a - e_c
    source = lax.broadcasted_iota(jnp.int32, (2 * T, 2 * T), 0)
    target = lax.broadcasted_iota(jnp.int32, (2 * T, 2 * T), 1)
    same_half = (source >= T) == (target >= T)

    def one_b(b, _):
        at = pl.ds(pl.multiple_of(b * H, H), H)
        spread = jnp.where(same_half & (jnp.bitwise_and(source, T - 1) == b), 1.0, 0.0).astype(BF16)
        over_c = jnp.dot(columns[...], spread, preferred_element_type=F32)
        kj_cb, ji_bc, kj_bc, ji_cb = (over_c[g * H : (g + 1) * H] for g in range(4))
        kj_ab, ji_ba, ki_ab = (rows[pl.ds(g * T + b, 1), :] for g in range(3))
        si_b, sj_b, sk_b, e_b = (scalars[pl.ds(g * T + b, 1), :] for g in range(4))
        extra_a[at, :] = (
            si_a * kj_cb - si_c * kj_ab + sj_b * ki_diff + sk_c * ji_ba - sk_a * ji_bc
        )
        extra_b[at, :] = (
            si_b * kj_ac - si_a * kj_bc + sj_c * ki_ab + sk_a * ji_cb - sk_b * ji_ca
        )
        inverse[at, :] = 1.0 / (base - e_b)
        return 0

    lax.fori_loop(0, T, one_b, 0, unroll=2)


def tables(triples, small, virt_energy):
    vmem = pl.BlockSpec(memory_space=pltpu.VMEM)
    table = jax.ShapeDtypeStruct((H * T, 2 * T), F32)
    return pl.pallas_call(
        tables_kernel,
        out_shape=(table, table, table),
        in_specs=[pl.BlockSpec(memory_space=pltpu.SMEM)] + [vmem] * 5,
        out_specs=[vmem] * 3,
        scratch_shapes=[
            pltpu.VMEM((4 * H, 2 * T), BF16),
            pltpu.VMEM((3 * T, 2 * T), F32),
            pltpu.VMEM((4 * T, 2 * T), F32),
        ],
        compiler_params=pltpu.CompilerParams(vmem_limit_bytes=VMEM_LIMIT),
        cost_estimate=pl.CostEstimate(flops=1 << 28, bytes_accessed=3 << 20, transcendentals=0),
        name="tables",
    )(triples, *small, virt_energy)


def local(
    virt_integrals,
    pair_amps,
    hole_amps,
    coulomb_ints,
    exchange_ints,
    singles,
    occ_energy,
    virt_energy,
    triples,
):
    n_trip = lax.axis_size("trip")

    out1, out2, out3, up1, up2 = prep(
        triples, pair_amps.reshape(3, 2 * T, 4 * T), coulomb_ints.reshape(coulomb_ints.shape[1:])
    )
    got_two = lax.ppermute(up2, "trip", shift_route(n_trip, -2))
    in2 = lax.ppermute(out2, "trip", shift_route(n_trip, 2))
    got_one = lax.ppermute(up1, "trip", shift_route(n_trip, -1))
    in1 = lax.ppermute(out1, "trip", shift_route(n_trip, 1))
    in3 = lax.ppermute(out3, "trip", shift_route(n_trip, 3))
    blocks = (got_one, got_two, in1, in2, in3)

    panels, holes = panels_of(
        virt_integrals.reshape(4 * T, T * T), hole_amps.reshape(hole_amps.shape[1:])
    )

    send = terms(1, triples, blocks, panels, holes)
    got = lax.ppermute(send, "virt", CORE_ROUTE)
    keep = terms(0, triples, blocks, panels, holes)
    sums = [(keep[j].astype(F32) + got[j].astype(F32)) for j in range(4)]

    arrived = [lax.ppermute(sums[j].astype(BF16), "virt", ring_route(j)) for j in (1, 2, 3)]

    small = jnp.concatenate(
        [
            exchange_ints.reshape(3 * T, T),
            singles,
            jnp.broadcast_to(occ_energy[:, None], (1, T)),
            jnp.zeros((14, T), BF16),
        ],
        axis=0,
    )
    small, _ = lax.optimization_barrier((small, keep))
    smalls = [small] + [
        lax.ppermute(small, "trip", shift_route(n_trip, -d)) for d in (1, 2, 3)
    ]
    extra_a, extra_b, inverse = tables(triples, smalls, virt_energy.reshape(1, T))

    (extra_a, extra_b, inverse), arrived = lax.optimization_barrier(
        ((extra_a, extra_b, inverse), arrived)
    )
    total = sums[0] + arrived[0].astype(F32) + arrived[1].astype(F32) + arrived[2].astype(F32)
    shares = [
        lax.ppermute(total[d].astype(BF16), "trip", shift_route(n_trip, -d)) for d in (1, 2, 3)
    ]
    chunk = combine(triples, total[0], shares[0], shares[1], shares[2])
    parts = [chunk] + [lax.ppermute(chunk, "virt", ring_route(j)) for j in (1, 2, 3)]

    mine = energy_of(triples, parts, extra_a, extra_b, inverse)
    other = lax.ppermute(mine, "virt", CORE_ROUTE)
    first = lax.rem(lax.axis_index("virt"), 2) == 0
    return jnp.where(
        first, jnp.concatenate([mine, other], axis=0), jnp.concatenate([other, mine], axis=0)
    )


def solution(mesh):
    placed = (
        P("trip", "virt", None),
        P("trip", None, None, None, "virt"),
        P("trip", "virt", None),
        P("trip", None, "virt", None),
        P("trip", None, None),
        P("trip", None),
        P("trip"),
        P(),
        P("trip", None),
    )
    return jax.shard_map(
        local, mesh=mesh, in_specs=placed, out_specs=P("trip", None), check_vma=False
    )
```

time: 200 us -> 131 us (0.66)
  the two profiles are of different devices: /device:TPU:359 before, /device:TPU:417 now
where the time goes in v2:
time: 131 us; the launch traced here: 130 us
  starting transfers between devices  70.1 us (54%)
  Pallas kernels  33.7 us (26%)
  waiting for transfers between devices  15.1 us (12%)
  local copies, waits for them, and re-layouts  5.79 us (4%)
  other arithmetic  3.95 us (3%)
    pallas_call x2, Pallas kernels, terms(): pl.pallas_call(functools.partial(terms_kernel, rel), out_shape=jax.ShapeD...  10.9 us
    ppermute x3, starting transfers between devices, local(): lax.ppermute(total[d].astype(BF16), 'trip', shift_route(n_trip, -d))  10.7 us
    ppermute x3, starting transfers between devices, local(): lax.ppermute(small, 'trip', shift_route(n_trip, -d))  10.5 us
    ppermute x3, starting transfers between devices, local(): lax.ppermute(sums[j].astype(BF16), 'virt', ring_route(j))  9.49 us
    ppermute x3, starting transfers between devices, local(): lax.ppermute(chunk, 'virt', ring_route(j))  8.74 us
    ppermute x1, starting transfers between devices, local(): other = lax.ppermute(mine, 'virt', CORE_ROUTE)  7.85 us
    pallas_call x1, Pallas kernels, energy_of(): pl.pallas_call(energy_kernel, out_shape=jax.ShapeDtypeStruct((1, T), F32)...  7.24 us
    pallas_call x1, Pallas kernels, tables(): pl.pallas_call(tables_kernel, out_shape=(table, table, table), in_specs=[...  6.04 us
  transfers between devices with their start and end apart: 19, of which 6 were waited for; matrix products, arithmetic and copies ran while one was open for 0% of the time, Pallas kernels for 13%

profile of v2, /device:TPU:417, one launch (start us, length us, event | category | flops | bytes accessed | tf_op | source)
XLA Modules:
  0.0 129.8 jit_solution(11734335415245118185)
XLA Ops:
  0.0 0.9 copy-done.6
  0.9 0.8 copy-done.7
  1.7 0.7 copy-done.8
  2.4 0.8 prep.1
  3.2 4.8 %collective-permute-start = (bf16[2,144,256]{2,1,0:T(8,128)(2,1)S(1)}, bf16[2,144,256]{2,1,0:T(8,128)(2,1)S(1)}, u32[]{:S(2)}, u32[]{:S(2)}) collective-permute-start(bf16[2,144,256]{2,1,0:T(8,128)(2,1)S(1)} %get-tuple-element.22), channel_id=1, source_target_pairs={{8,0},{16,8},{24,16},{32,24},{40,32},{48,40},{56,48},{64,56},{72,6... | collective-permute-start | bytes 442376 | tf_op jit(solution)/shard_map/ppermute | solution.py:443
  8.0 1.9 %collective-permute-start.2 = (bf16[2,144,256]{2,1,0:T(8,128)(2,1)S(1)}, bf16[2,144,256]{2,1,0:T(8,128)(2,1)S(1)}, u32[]{:S(2)}, u32[]{:S(2)}) collective-permute-start(bf16[2,144,256]{2,1,0:T(8,128)(2,1)S(1)} %get-tuple-element.24), channel_id=1, source_target_pairs={{0,8},{8,16},{16,24},{24,32},{32,40},{40,48},{48,56},{56,64},{64,7... | collective-permute-start | bytes 442376 | tf_op jit(solution)/shard_map/ppermute | solution.py:444
  9.9 3.2 %collective-permute-start.3 = (bf16[2,144,256]{2,1,0:T(8,128)(2,1)S(1)}, bf16[2,144,256]{2,1,0:T(8,128)(2,1)S(1)}, u32[]{:S(2)}, u32[]{:S(2)}) collective-permute-start(bf16[2,144,256]{2,1,0:T(8,128)(2,1)S(1)} %get-tuple-element.25), channel_id=1, source_target_pairs={{0,16},{8,24},{16,32},{24,40},{32,48},{40,56},{48,64},{56,72},{64,... | collective-permute-start | bytes 442376 | tf_op jit(solution)/shard_map/ppermute | solution.py:442
  13.1 3.8 %collective-permute-start.4 = (bf16[2,144,256]{2,1,0:T(8,128)(2,1)S(1)}, bf16[2,144,256]{2,1,0:T(8,128)(2,1)S(1)}, u32[]{:S(2)}, u32[]{:S(2)}) collective-permute-start(bf16[2,144,256]{2,1,0:T(8,128)(2,1)S(1)} %get-tuple-element.26), channel_id=1, source_target_pairs={{0,24},{8,32},{16,40},{24,48},{32,56},{40,64},{48,72},{56,80},{64,... | collective-permute-start | bytes 442376 | tf_op jit(solution)/shard_map/ppermute | solution.py:445
  16.9 5.2 %collective-permute-start.1 = (bf16[144,256]{1,0:T(8,128)(2,1)S(1)}, bf16[144,256]{1,0:T(8,128)(2,1)S(1)}, u32[]{:S(2)}, u32[]{:S(2)}) collective-permute-start(bf16[144,256]{1,0:T(8,128)(2,1)S(1)} %get-tuple-element.23), channel_id=1, source_target_pairs={{16,0},{24,8},{32,16},{40,24},{48,32},{56,40},{64,48},{72,56},{80,... | collective-permute-start | bytes 221192 | tf_op jit(solution)/shard_map/ppermute | solution.py:441
  22.1 0.0 copy-start
  22.1 1.6 %copy-done = bf16[1,256,4096]{2,1,0:T(8,128)(2,1)S(1)} copy-done((bf16[1,256,4096]{2,1,0:T(8,128)(2,1)S(1)}, bf16[1,256,4096]{2,1,0:T(8,128)(2,1)}, u32[]{:S(2)}) %copy-start) | copy-done | bytes 2097176
  23.7 1.0 copy-done.5
  24.6 5.7 %panels.1 = (bf16[4096,256]{1,0:T(8,128)(2,1)S(1)}, bf16[4096,128]{1,0:T(8,128)(2,1)S(1)}) custom-call(bf16[256,4096]{1,0:T(8,128)(2,1)S(1)} %bitcast.27, bf16[38,4096]{1,0:T(8,128)(2,1)S(1)} %bitcast.28), custom_call_target="tpu_custom_call" | custom-call | flops 268435456 | bytes 5242880 | tf_op jit(solution)/shard_map/panels/pallas_call | solution.py:128
  30.3 0.0 collective-permute-done.1.got_two
  30.4 0.0 collective-permute-done.got_one
  30.4 0.0 collective-permute-done.2.in1
  30.4 0.0 collective-permute-done.3.in2
  30.4 0.0 collective-permute-done.4.in3
  30.4 0.0 copy-done.9
  30.4 5.5 %terms.3 = bf16[4,4,512,128]{3,2,1,0:T(8,128)(2,1)S(1)} custom-call(s32[2,3]{1,0:T(2,128)S(1)} %copy-done.9, bf16[2,144,256]{2,1,0:T(8,128)(2,1)S(1)} %collective-permute-done.got_one, bf16[144,256]{1,0:T(8,128)(2,1)S(1)} %collective-permute-done.1.got_two, bf16[2,144,256]{2,1,0:T(8,128)(2,1)S(1)} %collective-permute-done.2.in1, ...), custom_call_target="tpu_custom_call" | custom-call | flops 2013265920 | bytes 5242880 | tf_op jit(solution)/shard_map/terms/pallas_call | solution.py:218
  35.9 4.0 %collective-permute-start.5 = (bf16[4,4,512,128]{3,2,1,0:T(8,128)(2,1)S(1)}, bf16[4,4,512,128]{3,2,1,0:T(8,128)(2,1)S(1)}, u32[]{:S(2)}, u32[]{:S(2)}) collective-permute-start(bf16[4,4,512,128]{3,2,1,0:T(8,128)(2,1)S(1)} %terms.3), channel_id=1, source_target_pairs={{0,1},{1,0},{2,3},{3,2},{4,5},{5,4},{6,7},{7,6},{8,9},{9,8},{10,11... | collective-permute-start | bytes 6291464 | tf_op jit(solution)/shard_map/ppermute | solution.py:453
  39.9 5.5 %terms.2 = bf16[4,4,512,128]{3,2,1,0:T(8,128)(2,1)S(1)} custom-call(s32[2,3]{1,0:T(2,128)S(1)} %copy-done.9, bf16[2,144,256]{2,1,0:T(8,128)(2,1)S(1)} %collective-permute-done.got_one, bf16[144,256]{1,0:T(8,128)(2,1)S(1)} %collective-permute-done.1.got_two, bf16[2,144,256]{2,1,0:T(8,128)(2,1)S(1)} %collective-permute-done.2.in1, ...), custom_call_target="tpu_custom_call" | custom-call | flops 2013265920 | bytes 5242880 | tf_op jit(solution)/shard_map/terms/pallas_call | solution.py:218
  45.3 0.0 copy-start.12
  45.4 0.0 copy-start.13
  45.4 0.0 copy-start.10
  45.4 0.0 collective-permute-done.5
  45.4 1.4 %fusion.4 = (bf16[4,512,128]{2,1,0:T(8,128)(2,1)}, bf16[4,512,128]{2,1,0:T(8,128)(2,1)}, bf16[4,512,128]{2,1,0:T(8,128)(2,1)}) fusion(bf16[4,4,512,128]{3,2,1,0:T(8,128)(2,1)S(1)} %collective-permute-done.5, bf16[4,4,512,128]{3,2,1,0:T(8,128)(2,1)S(1)} %terms.2), kind=kLoop, calls=%fused_computation.8 | loop fusion | flops 3145728 | bytes 4718592 | tf_op jit(solution)/shard_map/convert_element_type | solution.py:457
  46.8 0.5 copy-done.11
  47.3 4.6 %collective-permute-start.11 = (bf16[4,512,128]{2,1,0:T(8,128)(2,1)}, bf16[4,512,128]{2,1,0:T(8,128)(2,1)}, u32[]{:S(2)}, u32[]{:S(2)}) collective-permute-start(bf16[4,512,128]{2,1,0:T(8,128)(2,1)} %get-tuple-element.41), channel_id=1, source_target_pairs={{0,6},{1,7},{2,0},{3,1},{4,2},{5,3},{6,4},{7,5},{8,14},{9,15},{10,... | collective-permute-start | bytes 1572872 | tf_op jit(solution)/shard_map/ppermute | solution.py:457
  51.9 2.3 %collective-permute-start.10 = (bf16[4,512,128]{2,1,0:T(8,128)(2,1)}, bf16[4,512,128]{2,1,0:T(8,128)(2,1)}, u32[]{:S(2)}, u32[]{:S(2)}) collective-permute-start(bf16[4,512,128]{2,1,0:T(8,128)(2,1)} %get-tuple-element.42), channel_id=1, source_target_pairs={{0,4},{1,5},{2,6},{3,7},{4,0},{5,1},{6,2},{7,3},{8,12},{9,13},{10,... | collective-permute-start | bytes 1572872 | tf_op jit(solution)/shard_map/ppermute | solution.py:457
  54.2 2.6 %collective-permute-start.9 = (bf16[4,512,128]{2,1,0:T(8,128)(2,1)}, bf16[4,512,128]{2,1,0:T(8,128)(2,1)}, u32[]{:S(2)}, u32[]{:S(2)}) collective-permute-start(bf16[4,512,128]{2,1,0:T(8,128)(2,1)} %get-tuple-element.43), channel_id=1, source_target_pairs={{0,2},{1,3},{2,4},{3,5},{4,6},{5,7},{6,0},{7,1},{8,10},{9,11},{10,... | collective-permute-start | bytes 1572872 | tf_op jit(solution)/shard_map/ppermute | solution.py:457
  57.4 0.1 pad.6.clone
  57.5 0.1 pad.7.clone
  57.6 0.1 reshape.43
  57.7 0.1 maximum_maximum_fusion.own
  57.8 2.1 %collective-permute-start.8 = (bf16[208,64]{1,0:T(8,128)(2,1)S(1)}, bf16[208,64]{1,0:T(8,128)(2,1)S(1)}, u32[]{:S(2)}, u32[]{:S(2)}) collective-permute-start(bf16[208,64]{1,0:T(8,128)(2,1)S(1)} %maximum_maximum_fusion.own), channel_id=1, source_target_pairs={{24,0},{32,8},{40,16},{48,24},{56,32},{64,40},{72,48},{80,56},{88,... | collective-permute-start | bytes 79880 | tf_op jit(solution)/shard_map/ppermute | solution.py:470
  59.9 5.7 %collective-permute-start.7 = (bf16[208,64]{1,0:T(8,128)(2,1)S(1)}, bf16[208,64]{1,0:T(8,128)(2,1)S(1)}, u32[]{:S(2)}, u32[]{:S(2)}) collective-permute-start(bf16[208,64]{1,0:T(8,128)(2,1)S(1)} %maximum_maximum_fusion.own), channel_id=1, source_target_pairs={{16,0},{24,8},{32,16},{40,24},{48,32},{56,40},{64,48},{72,56},{80,... | collective-permute-start | bytes 79880 | tf_op jit(solution)/shard_map/ppermute | solution.py:470
  65.6 0.0 collective-permute-done.8.three
  65.6 2.8 %collective-permute-start.6 = (bf16[208,64]{1,0:T(8,128)(2,1)S(1)}, bf16[208,64]{1,0:T(8,128)(2,1)S(1)}, u32[]{:S(2)}, u32[]{:S(2)}) collective-permute-start(bf16[208,64]{1,0:T(8,128)(2,1)S(1)} %maximum_maximum_fusion.own), channel_id=1, source_target_pairs={{8,0},{16,8},{24,16},{32,24},{40,32},{48,40},{56,48},{64,56},{72,6... | collective-permute-start | bytes 79880 | tf_op jit(solution)/shard_map/ppermute | solution.py:470
  68.4 0.0 collective-permute-done.7.two
  68.4 2.5 %collective-permute-done.6.one = bf16[208,64]{1,0:T(8,128)(2,1)S(1)} collective-permute-done((bf16[208,64]{1,0:T(8,128)(2,1)S(1)}, bf16[208,64]{1,0:T(8,128)(2,1)S(1)}, u32[]{:S(2)}, u32[]{:S(2)}) %collective-permute-start.6) | collective-permute-done | bytes 26656 | tf_op jit(solution)/shard_map/ppermute | solution.py:470
  70.9 6.0 %tables.1 = (f32[2048,128]{1,0:T(8,128)S(1)}, f32[2048,128]{1,0:T(8,128)S(1)}, f32[2048,128]{1,0:T(8,128)S(1)}) custom-call(s32[2,3]{1,0:T(2,128)S(1)} %copy-done.9, bf16[208,64]{1,0:T(8,128)(2,1)S(1)} %maximum_maximum_fusion.own, bf16[208,64]{1,0:T(8,128)(2,1)S(1)} %collective-permute-done.6.one, bf16[208,64]{1,0:T(8,128)(2,1)S(1)} %collective-permute-done.7.two, ...), custom_call_target="tpu_custom_call" | custom-call | flops 268435456 | bytes 3145728 | tf_op jit(solution)/shard_map/tables/pallas_call | solution.py:409
  77.0 0.0 collective-permute-done.11
  77.0 0.0 collective-permute-done.10
  77.0 3.7 %collective-permute-done.9 = bf16[4,512,128]{2,1,0:T(8,128)(2,1)} collective-permute-done((bf16[4,512,128]{2,1,0:T(8,128)(2,1)}, bf16[4,512,128]{2,1,0:T(8,128)(2,1)}, u32[]{:S(2)}, u32[]{:S(2)}) %collective-permute-start.9) | collective-permute-done | bytes 524320 | tf_op jit(solution)/shard_map/ppermute | solution.py:457
  80.7 1.9 %fusion.5 = (bf16[4,512,128]{2,1,0:T(8,128)(2,1)S(1)}, f32[4,512,128]{2,1,0:T(8,128)S(1)}) fusion(bf16[4,512,128]{2,1,0:T(8,128)(2,1)} %collective-permute-done.11, bf16[4,512,128]{2,1,0:T(8,128)(2,1)} %collective-permute-done.10, bf16[4,512,128]{2,1,0:T(8,128)(2,1)} %collective-permute-done.9, bf16[4,4,512,128]{3,2,1,0:T(8,128)(2,1)} %copy-done.11, ...), kind=kLoop, calls=%fused_computation.15 | loop fusion | flops 2621440 | bytes 4194304 | tf_op jit(solution)/shard_map/convert.2
  82.7 2.2 %collective-permute-start.14 = (bf16[512,128]{1,0:T(8,128)(2,1)S(1)}, bf16[512,128]{1,0:T(8,128)(2,1)S(1)}, u32[]{:S(2)}, u32[]{:S(2)}) collective-permute-start(bf16[512,128]{1,0:T(8,128)(2,1)S(1)} %get-tuple-element.44), channel_id=1, source_target_pairs={{24,0},{32,8},{40,16},{48,24},{56,32},{64,40},{72,48},{80,56},{88,... | collective-permute-start | bytes 393224 | tf_op jit(solution)/shard_map/ppermute | solution.py:479
  84.9 5.7 %collective-permute-start.13 = (bf16[512,128]{1,0:T(8,128)(2,1)S(1)}, bf16[512,128]{1,0:T(8,128)(2,1)S(1)}, u32[]{:S(2)}, u32[]{:S(2)}) collective-permute-start(bf16[512,128]{1,0:T(8,128)(2,1)S(1)} %get-tuple-element.45), channel_id=1, source_target_pairs={{16,0},{24,8},{32,16},{40,24},{48,32},{56,40},{64,48},{72,56},{80,... | collective-permute-start | bytes 393224 | tf_op jit(solution)/shard_map/ppermute | solution.py:479
  90.6 2.8 %collective-permute-start.12 = (bf16[512,128]{1,0:T(8,128)(2,1)S(1)}, bf16[512,128]{1,0:T(8,128)(2,1)S(1)}, u32[]{:S(2)}, u32[]{:S(2)}) collective-permute-start(bf16[512,128]{1,0:T(8,128)(2,1)S(1)} %get-tuple-element.46), channel_id=1, source_target_pairs={{8,0},{16,8},{24,16},{32,24},{40,32},{48,40},{56,48},{64,56},{72,6... | collective-permute-start | bytes 393224 | tf_op jit(solution)/shard_map/ppermute | solution.py:479
  93.4 0.0 collective-permute-done.14.three
  93.4 0.0 collective-permute-done.13.two
  93.4 3.0 %collective-permute-done.12.one = bf16[512,128]{1,0:T(8,128)(2,1)S(1)} collective-permute-done((bf16[512,128]{1,0:T(8,128)(2,1)S(1)}, bf16[512,128]{1,0:T(8,128)(2,1)S(1)}, u32[]{:S(2)}, u32[]{:S(2)}) %collective-permute-start.12) | collective-permute-done | bytes 131104 | tf_op jit(solution)/shard_map/ppermute | solution.py:479
  96.5 3.0 %combine.1.w0 = bf16[512,128]{1,0:T(8,128)(2,1)S(1)} custom-call(s32[2,3]{1,0:T(2,128)S(1)} %copy-done.9, f32[512,128]{1,0:T(8,128)S(1)} %slice_bitcast_fusion.own, bf16[512,128]{1,0:T(8,128)(2,1)S(1)} %collective-permute-done.12.one, bf16[512,128]{1,0:T(8,128)(2,1)S(1)} %collective-permute-done.13.two, bf16[512,128]{1,0:T(8,128)(2,1)S(1)} %collective-permute-done.14.three), custom_call_target="tpu_custom_call" | custom-call | tf_op jit(solution)/shard_map/combine/pallas_call | solution.py:262
  99.4 3.5 %collective-permute-start.17 = (bf16[512,128]{1,0:T(8,128)(2,1)S(1)}, bf16[512,128]{1,0:T(8,128)(2,1)S(1)}, u32[]{:S(2)}, u32[]{:S(2)}) collective-permute-start(bf16[512,128]{1,0:T(8,128)(2,1)S(1)} %combine.1.w0), channel_id=1, source_target_pairs={{0,6},{1,7},{2,0},{3,1},{4,2},{5,3},{6,4},{7,5},{8,14},{9,15},{10,... | collective-permute-start | bytes 393224 | tf_op jit(solution)/shard_map/ppermute | solution.py:482
  102.9 3.3 %collective-permute-start.16 = (bf16[512,128]{1,0:T(8,128)(2,1)S(1)}, bf16[512,128]{1,0:T(8,128)(2,1)S(1)}, u32[]{:S(2)}, u32[]{:S(2)}) collective-permute-start(bf16[512,128]{1,0:T(8,128)(2,1)S(1)} %combine.1.w0), channel_id=1, source_target_pairs={{0,4},{1,5},{2,6},{3,7},{4,0},{5,1},{6,2},{7,3},{8,12},{9,13},{10,... | collective-permute-start | bytes 393224 | tf_op jit(solution)/shard_map/ppermute | solution.py:482
  106.3 1.9 %collective-permute-start.15 = (bf16[512,128]{1,0:T(8,128)(2,1)S(1)}, bf16[512,128]{1,0:T(8,128)(2,1)}, u32[]{:S(2)}, u32[]{:S(2)}) collective-permute-start(bf16[512,128]{1,0:T(8,128)(2,1)S(1)} %combine.1.w0), channel_id=1, source_target_pairs={{0,2},{1,3},{2,4},{3,5},{4,6},{5,7},{6,0},{7,1},{8,10},{9,11},{10,... | collective-permute-start | bytes 393224 | tf_op jit(solution)/shard_map/ppermute | solution.py:482
  108.2 0.0 collective-permute-done.17.w3
  108.2 1.9 %collective-permute-done.16.w2 = bf16[512,128]{1,0:T(8,128)(2,1)S(1)} collective-permute-done((bf16[512,128]{1,0:T(8,128)(2,1)S(1)}, bf16[512,128]{1,0:T(8,128)(2,1)S(1)}, u32[]{:S(2)}, u32[]{:S(2)}) %collective-permute-start.16) | collective-permute-done | bytes 131104 | tf_op jit(solution)/shard_map/ppermute | solution.py:482
  110.2 3.1 %collective-permute-done.15.w1 = bf16[512,128]{1,0:T(8,128)(2,1)} collective-permute-done((bf16[512,128]{1,0:T(8,128)(2,1)S(1)}, bf16[512,128]{1,0:T(8,128)(2,1)}, u32[]{:S(2)}, u32[]{:S(2)}) %collective-permute-start.15) | collective-permute-done | bytes 131104 | tf_op jit(solution)/shard_map/ppermute | solution.py:482
  113.3 0.0 copy-done.4
  113.3 7.2 %energy.1 = f32[1,64]{1,0:T(1,128)S(1)} custom-call(s32[2,3]{1,0:T(2,128)S(1)} %copy-done.9, bf16[512,128]{1,0:T(8,128)(2,1)S(1)} %combine.1.w0, bf16[512,128]{1,0:T(8,128)(2,1)} %collective-permute-done.15.w1, bf16[512,128]{1,0:T(8,128)(2,1)S(1)} %collective-permute-done.16.w2, bf16[512,128]{1,0:T(8,128)(2,1)S(1)} %collective-permute-done.17.w3, ...), custom_call_target="tpu_custom_call" | custom-call | tf_op jit(solution)/shard_map/energy/pallas_call | solution.py:315
  120.6 7.8 %collective-permute-start.18 = (f32[1,64]{1,0:T(1,128)S(1)}, f32[1,64]{1,0:T(1,128)S(1)}, u32[]{:S(2)}, u32[]{:S(2)}) collective-permute-start(f32[1,64]{1,0:T(1,128)S(1)} %energy.1), channel_id=1, source_target_pairs={{0,1},{1,0},{2,3},{3,2},{4,5},{5,4},{6,7},{7,6},{8,9},{9,8},{10,11... | collective-permute-start | bytes 776 | tf_op jit(solution)/shard_map/ppermute | solution.py:485
  128.4 0.8 collective-permute-done.18
  129.2 0.6 maximum_select_fusion
  (19 shorter events, 0.1 us)
Async XLA Ops:
  0.0 30.4 %copy-start.9 = (s32[2,3]{1,0:T(2,128)S(1)}, s32[2,3]{1,0:T(2,128)}, u32[]{:S(2)}) copy-start(s32[2,3]{1,0:T(2,128)} %triples.11) | copy-start | bytes 76
  0.0 0.9 copy-start.6
  0.9 0.8 copy-start.7
  1.7 0.7 copy-start.8
  3.2 27.2 %collective-permute-start = (bf16[2,144,256]{2,1,0:T(8,128)(2,1)S(1)}, bf16[2,144,256]{2,1,0:T(8,128)(2,1)S(1)}, u32[]{:S(2)}, u32[]{:S(2)}) collective-permute-start(bf16[2,144,256]{2,1,0:T(8,128)(2,1)S(1)} %get-tuple-element.22), channel_id=1, source_target_pairs={{8,0},{16,8},{24,16},{32,24},{40,32},{48,40},{56,48},{64,56},{72,6... | collective-permute-start | bytes 442376 | tf_op jit(solution)/shard_map/ppermute | solution.py:443
  8.0 22.4 %collective-permute-start.2 = (bf16[2,144,256]{2,1,0:T(8,128)(2,1)S(1)}, bf16[2,144,256]{2,1,0:T(8,128)(2,1)S(1)}, u32[]{:S(2)}, u32[]{:S(2)}) collective-permute-start(bf16[2,144,256]{2,1,0:T(8,128)(2,1)S(1)} %get-tuple-element.24), channel_id=1, source_target_pairs={{0,8},{8,16},{16,24},{24,32},{32,40},{40,48},{48,56},{56,64},{64,7... | collective-permute-start | bytes 442376 | tf_op jit(solution)/shard_map/ppermute | solution.py:444
  9.9 20.4 %collective-permute-start.3 = (bf16[2,144,256]{2,1,0:T(8,128)(2,1)S(1)}, bf16[2,144,256]{2,1,0:T(8,128)(2,1)S(1)}, u32[]{:S(2)}, u32[]{:S(2)}) collective-permute-start(bf16[2,144,256]{2,1,0:T(8,128)(2,1)S(1)} %get-tuple-element.25), channel_id=1, source_target_pairs={{0,16},{8,24},{16,32},{24,40},{32,48},{40,56},{48,64},{56,72},{64,... | collective-permute-start | bytes 442376 | tf_op jit(solution)/shard_map/ppermute | solution.py:442
  13.1 17.3 %collective-permute-start.4 = (bf16[2,144,256]{2,1,0:T(8,128)(2,1)S(1)}, bf16[2,144,256]{2,1,0:T(8,128)(2,1)S(1)}, u32[]{:S(2)}, u32[]{:S(2)}) collective-permute-start(bf16[2,144,256]{2,1,0:T(8,128)(2,1)S(1)} %get-tuple-element.26), channel_id=1, source_target_pairs={{0,24},{8,32},{16,40},{24,48},{32,56},{40,64},{48,72},{56,80},{64,... | collective-permute-start | bytes 442376 | tf_op jit(solution)/shard_map/ppermute | solution.py:445
  16.9 13.4 %collective-permute-start.1 = (bf16[144,256]{1,0:T(8,128)(2,1)S(1)}, bf16[144,256]{1,0:T(8,128)(2,1)S(1)}, u32[]{:S(2)}, u32[]{:S(2)}) collective-permute-start(bf16[144,256]{1,0:T(8,128)(2,1)S(1)} %get-tuple-element.23), channel_id=1, source_target_pairs={{16,0},{24,8},{32,16},{40,24},{48,32},{56,40},{64,48},{72,56},{80,... | collective-permute-start | bytes 221192 | tf_op jit(solution)/shard_map/ppermute | solution.py:441
  22.1 1.6 %copy-start = (bf16[1,256,4096]{2,1,0:T(8,128)(2,1)S(1)}, bf16[1,256,4096]{2,1,0:T(8,128)(2,1)}, u32[]{:S(2)}) copy-start(bf16[1,256,4096]{2,1,0:T(8,128)(2,1)} %param.9) | copy-start | bytes 6291460
  23.7 1.0 copy-start.5
  35.9 9.5 %collective-permute-start.5 = (bf16[4,4,512,128]{3,2,1,0:T(8,128)(2,1)S(1)}, bf16[4,4,512,128]{3,2,1,0:T(8,128)(2,1)S(1)}, u32[]{:S(2)}, u32[]{:S(2)}) collective-permute-start(bf16[4,4,512,128]{3,2,1,0:T(8,128)(2,1)S(1)} %terms.3), channel_id=1, source_target_pairs={{0,1},{1,0},{2,3},{3,2},{4,5},{5,4},{6,7},{7,6},{8,9},{9,8},{10,11... | collective-permute-start | bytes 6291464 | tf_op jit(solution)/shard_map/ppermute | solution.py:453
  45.3 12.3 %copy-start.12 = (bf16[1,3,4096]{2,1,0:T(4,128)(2,1)S(1)}, bf16[1,3,4096]{2,1,0:T(4,128)(2,1)}, u32[]{:S(2)}) copy-start(bf16[1,3,4096]{2,1,0:T(4,128)(2,1)} %param.13) | copy-start | bytes 73732
  45.4 12.4 %copy-start.13 = (bf16[1,64]{1,0:T(2,128)(2,1)S(1)}, bf16[1,64]{1,0:T(2,128)(2,1)}, u32[]{:S(2)}) copy-start(bf16[1,64]{1,0:T(2,128)(2,1)} %param.14) | copy-start | bytes 388
  45.4 25.5 %copy-start.10 = (f32[64]{0:T(128)S(1)}, f32[64]{0:T(128)}, u32[]{:S(2)}) copy-start(f32[64]{0:T(128)} %param.16) | copy-start | bytes 772
  45.4 1.9 %copy-start.11 = (bf16[4,4,512,128]{3,2,1,0:T(8,128)(2,1)}, bf16[4,4,512,128]{3,2,1,0:T(8,128)(2,1)S(1)}, u32[]{:S(2)}) copy-start(bf16[4,4,512,128]{3,2,1,0:T(8,128)(2,1)S(1)} %collective-permute-done.5) | copy-start | bytes 6291460
  47.3 29.7 %collective-permute-start.11 = (bf16[4,512,128]{2,1,0:T(8,128)(2,1)}, bf16[4,512,128]{2,1,0:T(8,128)(2,1)}, u32[]{:S(2)}, u32[]{:S(2)}) collective-permute-start(bf16[4,512,128]{2,1,0:T(8,128)(2,1)} %get-tuple-element.41), channel_id=1, source_target_pairs={{0,6},{1,7},{2,0},{3,1},{4,2},{5,3},{6,4},{7,5},{8,14},{9,15},{10,... | collective-permute-start | bytes 1572872 | tf_op jit(solution)/shard_map/ppermute | solution.py:457
  51.9 25.1 %collective-permute-start.10 = (bf16[4,512,128]{2,1,0:T(8,128)(2,1)}, bf16[4,512,128]{2,1,0:T(8,128)(2,1)}, u32[]{:S(2)}, u32[]{:S(2)}) collective-permute-start(bf16[4,512,128]{2,1,0:T(8,128)(2,1)} %get-tuple-element.42), channel_id=1, source_target_pairs={{0,4},{1,5},{2,6},{3,7},{4,0},{5,1},{6,2},{7,3},{8,12},{9,13},{10,... | collective-permute-start | bytes 1572872 | tf_op jit(solution)/shard_map/ppermute | solution.py:457
  54.2 26.5 %collective-permute-start.9 = (bf16[4,512,128]{2,1,0:T(8,128)(2,1)}, bf16[4,512,128]{2,1,0:T(8,128)(2,1)}, u32[]{:S(2)}, u32[]{:S(2)}) collective-permute-start(bf16[4,512,128]{2,1,0:T(8,128)(2,1)} %get-tuple-element.43), channel_id=1, source_target_pairs={{0,2},{1,3},{2,4},{3,5},{4,6},{5,7},{6,0},{7,1},{8,10},{9,11},{10,... | collective-permute-start | bytes 1572872 | tf_op jit(solution)/shard_map/ppermute | solution.py:457
  57.8 7.8 %collective-permute-start.8 = (bf16[208,64]{1,0:T(8,128)(2,1)S(1)}, bf16[208,64]{1,0:T(8,128)(2,1)S(1)}, u32[]{:S(2)}, u32[]{:S(2)}) collective-permute-start(bf16[208,64]{1,0:T(8,128)(2,1)S(1)} %maximum_maximum_fusion.own), channel_id=1, source_target_pairs={{24,0},{32,8},{40,16},{48,24},{56,32},{64,40},{72,48},{80,56},{88,... | collective-permute-start | bytes 79880 | tf_op jit(solution)/shard_map/ppermute | solution.py:470
  59.9 8.5 %collective-permute-start.7 = (bf16[208,64]{1,0:T(8,128)(2,1)S(1)}, bf16[208,64]{1,0:T(8,128)(2,1)S(1)}, u32[]{:S(2)}, u32[]{:S(2)}) collective-permute-start(bf16[208,64]{1,0:T(8,128)(2,1)S(1)} %maximum_maximum_fusion.own), channel_id=1, source_target_pairs={{16,0},{24,8},{32,16},{40,24},{48,32},{56,40},{64,48},{72,56},{80,... | collective-permute-start | bytes 79880 | tf_op jit(solution)/shard_map/ppermute | solution.py:470
  65.6 5.3 %collective-permute-start.6 = (bf16[208,64]{1,0:T(8,128)(2,1)S(1)}, bf16[208,64]{1,0:T(8,128)(2,1)S(1)}, u32[]{:S(2)}, u32[]{:S(2)}) collective-permute-start(bf16[208,64]{1,0:T(8,128)(2,1)S(1)} %maximum_maximum_fusion.own), channel_id=1, source_target_pairs={{8,0},{16,8},{24,16},{32,24},{40,32},{48,40},{56,48},{64,56},{72,6... | collective-permute-start | bytes 79880 | tf_op jit(solution)/shard_map/ppermute | solution.py:470
  77.0 5.7 %copy-start.1 = (f32[2048,128]{1,0:T(8,128)}, f32[2048,128]{1,0:T(8,128)S(1)}, u32[]{:S(2)}) copy-start(f32[2048,128]{1,0:T(8,128)S(1)} %get-tuple-element.37.extra_b) | copy-start | bytes 3145732
  77.0 5.7 %copy-start.3 = (f32[2048,128]{1,0:T(8,128)}, f32[2048,128]{1,0:T(8,128)S(1)}, u32[]{:S(2)}) copy-start(f32[2048,128]{1,0:T(8,128)S(1)} %get-tuple-element.38.inverse) | copy-start | bytes 3145732
  82.6 30.7 %copy-start.2 = (f32[2048,128]{1,0:T(8,128)S(1)}, f32[2048,128]{1,0:T(8,128)}, u32[]{:S(2)}) copy-start(f32[2048,128]{1,0:T(8,128)} %copy-done.1) | copy-start | bytes 3145732
  82.6 30.7 %copy-start.4 = (f32[2048,128]{1,0:T(8,128)S(1)}, f32[2048,128]{1,0:T(8,128)}, u32[]{:S(2)}) copy-start(f32[2048,128]{1,0:T(8,128)} %copy-done.3) | copy-start | bytes 3145732
  82.7 10.7 %collective-permute-start.14 = (bf16[512,128]{1,0:T(8,128)(2,1)S(1)}, bf16[512,128]{1,0:T(8,128)(2,1)S(1)}, u32[]{:S(2)}, u32[]{:S(2)}) collective-permute-start(bf16[512,128]{1,0:T(8,128)(2,1)S(1)} %get-tuple-element.44), channel_id=1, source_target_pairs={{24,0},{32,8},{40,16},{48,24},{56,32},{64,40},{72,48},{80,56},{88,... | collective-permute-start | bytes 393224 | tf_op jit(solution)/shard_map/ppermute | solution.py:479
  84.9 8.5 %collective-permute-start.13 = (bf16[512,128]{1,0:T(8,128)(2,1)S(1)}, bf16[512,128]{1,0:T(8,128)(2,1)S(1)}, u32[]{:S(2)}, u32[]{:S(2)}) collective-permute-start(bf16[512,128]{1,0:T(8,128)(2,1)S(1)} %get-tuple-element.45), channel_id=1, source_target_pairs={{16,0},{24,8},{32,16},{40,24},{48,32},{56,40},{64,48},{72,56},{80,... | collective-permute-start | bytes 393224 | tf_op jit(solution)/shard_map/ppermute | solution.py:479
  90.6 5.9 %collective-permute-start.12 = (bf16[512,128]{1,0:T(8,128)(2,1)S(1)}, bf16[512,128]{1,0:T(8,128)(2,1)S(1)}, u32[]{:S(2)}, u32[]{:S(2)}) collective-permute-start(bf16[512,128]{1,0:T(8,128)(2,1)S(1)} %get-tuple-element.46), channel_id=1, source_target_pairs={{8,0},{16,8},{24,16},{32,24},{40,32},{48,40},{56,48},{64,56},{72,6... | collective-permute-start | bytes 393224 | tf_op jit(solution)/shard_map/ppermute | solution.py:479
  99.4 8.8 %collective-permute-start.17 = (bf16[512,128]{1,0:T(8,128)(2,1)S(1)}, bf16[512,128]{1,0:T(8,128)(2,1)S(1)}, u32[]{:S(2)}, u32[]{:S(2)}) collective-permute-start(bf16[512,128]{1,0:T(8,128)(2,1)S(1)} %combine.1.w0), channel_id=1, source_target_pairs={{0,6},{1,7},{2,0},{3,1},{4,2},{5,3},{6,4},{7,5},{8,14},{9,15},{10,... | collective-permute-start | bytes 393224 | tf_op jit(solution)/shard_map/ppermute | solution.py:482
  102.9 7.2 %collective-permute-start.16 = (bf16[512,128]{1,0:T(8,128)(2,1)S(1)}, bf16[512,128]{1,0:T(8,128)(2,1)S(1)}, u32[]{:S(2)}, u32[]{:S(2)}) collective-permute-start(bf16[512,128]{1,0:T(8,128)(2,1)S(1)} %combine.1.w0), channel_id=1, source_target_pairs={{0,4},{1,5},{2,6},{3,7},{4,0},{5,1},{6,2},{7,3},{8,12},{9,13},{10,... | collective-permute-start | bytes 393224 | tf_op jit(solution)/shard_map/ppermute | solution.py:482
  106.3 7.0 %collective-permute-start.15 = (bf16[512,128]{1,0:T(8,128)(2,1)S(1)}, bf16[512,128]{1,0:T(8,128)(2,1)}, u32[]{:S(2)}, u32[]{:S(2)}) collective-permute-start(bf16[512,128]{1,0:T(8,128)(2,1)S(1)} %combine.1.w0), channel_id=1, source_target_pairs={{0,2},{1,3},{2,4},{3,5},{4,6},{5,7},{6,0},{7,1},{8,10},{9,11},{10,... | collective-permute-start | bytes 393224 | tf_op jit(solution)/shard_map/ppermute | solution.py:482
  120.6 8.7 %collective-permute-start.18 = (f32[1,64]{1,0:T(1,128)S(1)}, f32[1,64]{1,0:T(1,128)S(1)}, u32[]{:S(2)}, u32[]{:S(2)}) collective-permute-start(f32[1,64]{1,0:T(1,128)S(1)} %energy.1), channel_id=1, source_target_pairs={{0,1},{1,0},{2,3},{3,2},{4,5},{5,4},{6,7},{7,6},{8,9},{9,8},{10,11... | collective-permute-start | bytes 776 | tf_op jit(solution)/shard_map/ppermute | solution.py:485

commit v3 on v2

v3 whole, which is shorter than its diff:
```python
import functools

import jax
import jax.numpy as jnp
from jax import lax
from jax.experimental import pallas as pl
from jax.experimental.pallas import tpu as pltpu
from jax.sharding import PartitionSpec as P

T = 64
H = 32
F32 = jnp.float32
BF16 = jnp.bfloat16
CROWS = 16
BLOCK_ROWS = 2 * T + CROWS
SMALL_ROWS = 3 * H + 16
VMEM_LIMIT = 20 * 1024 * 1024


def shift_route(size, distance):
    return [(i, i + distance) for i in range(size) if 0 <= i + distance < size]


CORE_ROUTE = [(i, i ^ 1) for i in range(8)]


def lane_low(rows):
    return lax.broadcasted_iota(jnp.int32, (rows, 2 * T), 1) < T


def swap_halves(x):
    return pltpu.roll(x, T, 1)


def pack_rows(rows64):
    low = lane_low(H)
    top, bottom = rows64[:H], rows64[H:]
    first = jnp.where(low, top, swap_halves(bottom))
    second = jnp.where(low, swap_halves(top), bottom)
    return first, second


def row_of(triples, owner, core, rel):
    s = jnp.where(core == 0, rel, 1 - rel)
    live = triples[s, 0] >= 0
    off_i = jnp.where(live, triples[s, 0] - owner, 2)
    off_j = jnp.where(live, triples[s, 1] - owner, 1)
    return off_i, off_j, live


def prep_kernel(triples, amps_in, coulomb_in, out1, out2, out3, up1, up2, blocks, amps, coulomb, sems):
    copies = [
        pltpu.make_async_copy(amps_in, amps, sems.at[0]),
        pltpu.make_async_copy(coulomb_in, coulomb, sems.at[1]),
    ]
    for copy in copies:
        copy.start()
    for copy in copies:
        copy.wait()
    owner, core = lax.axis_index("trip"), lax.rem(lax.axis_index("virt"), 2)
    occ_rows = coulomb.shape[1]
    for s in range(3):
        blocks[s, : 2 * T, :] = amps[s]
        turned = jnp.concatenate(
            [coulomb[s].astype(F32), jnp.zeros((T - occ_rows, T), F32)], axis=0
        ).T
        packed = jnp.concatenate([-turned[g * CROWS : (g + 1) * CROWS] for g in range(4)], axis=1)
        blocks[s, 2 * T :, :] = packed.astype(BF16)
    up1[...] = blocks[0:2]
    up2[...] = blocks[0]
    for rel in range(2):
        off_i, off_j, live = row_of(triples, owner, core, rel)
        for d, out in ((1, out1), (2, out2), (3, out3)):
            takes_part = live & ((off_i == d) | (off_j == d))
            other = jnp.clip(off_i + off_j - d - 1, 0, 2)

            @pl.when(takes_part)
            def _():
                out[rel] = blocks[other]

            @pl.when(jnp.logical_not(takes_part))
            def _():
                out[rel] = jnp.zeros((BLOCK_ROWS, 4 * T), BF16)


def prep(triples, amps, coulomb):
    vmem = pl.BlockSpec(memory_space=pltpu.VMEM)
    two = jax.ShapeDtypeStruct((2, BLOCK_ROWS, 4 * T), BF16)
    one = jax.ShapeDtypeStruct((BLOCK_ROWS, 4 * T), BF16)
    return pl.pallas_call(
        prep_kernel,
        out_shape=(two, two, two, two, one),
        in_specs=[
            pl.BlockSpec(memory_space=pltpu.SMEM),
            pl.BlockSpec(memory_space=pltpu.HBM),
            pl.BlockSpec(memory_space=pltpu.HBM),
        ],
        out_specs=[vmem] * 5,
        scratch_shapes=[
            pltpu.VMEM((3, BLOCK_ROWS, 4 * T), BF16),
            pltpu.VMEM(amps.shape, BF16),
            pltpu.VMEM(coulomb.shape, BF16),
            pltpu.SemaphoreType.DMA((2,)),
        ],
        compiler_params=pltpu.CompilerParams(vmem_limit_bytes=VMEM_LIMIT),
        name="prep",
    )(triples, amps, coulomb)


STEPS = 8
DEPTH = 6 * T


def panels_kernel(integrals, holes, out, spread_a, spread_b):
    occ_rows = holes.shape[0]
    step = pl.program_id(0)
    per_step = H // STEPS

    for inner in range(per_step):
        chunk = step * per_step + inner
        columns = slice(inner * 2 * T, (inner + 1) * 2 * T)
        turned = integrals[:, columns].astype(F32).T
        hole = holes[:, columns].astype(F32)
        hole = jnp.concatenate([hole, jnp.zeros((2 * T - occ_rows, 2 * T), F32)], axis=0).T
        for part in range(4):
            at = pl.ds((part % 2) * T + chunk * 2 + part // 2, H, stride=2 * T)
            spread_a[at, :] = turned[part * H : (part + 1) * H, : 2 * T]
            spread_b[at, :] = turned[part * H : (part + 1) * H, 2 * T :]
        for w in range(2):
            third = chunk * 2 + w
            at = lax.rem(third, H) * 2 * T + (third // H) * T
            rows = pl.ds(pl.multiple_of(at, T), T)
            out[rows, 4 * T :] = hole[w * T : (w + 1) * T].astype(BF16)

    @pl.when(step == STEPS - 1)
    def _():
        def settle(step, _):
            rows = pl.ds(pl.multiple_of(step * 2 * T, 2 * T), 2 * T)
            out[rows, : 2 * T] = spread_a[rows, :].astype(BF16)
            out[rows, 2 * T : 4 * T] = spread_b[rows, :].astype(BF16)
            return 0

        lax.fori_loop(0, H, settle, 0, unroll=2)


def panels_of(integrals, holes):
    vmem = pl.BlockSpec(memory_space=pltpu.VMEM)
    columns = T * T // STEPS
    return pl.pallas_call(
        panels_kernel,
        grid=(STEPS,),
        out_shape=jax.ShapeDtypeStruct((T * T, DEPTH), BF16),
        in_specs=[
            pl.BlockSpec((4 * T, columns), lambda step: (0, step)),
            pl.BlockSpec((holes.shape[0], columns), lambda step: (0, step)),
        ],
        out_specs=vmem,
        scratch_shapes=[pltpu.VMEM((T * T, 2 * T), F32)] * 2,
        compiler_params=pltpu.CompilerParams(vmem_limit_bytes=VMEM_LIMIT),
        cost_estimate=pl.CostEstimate(flops=1 << 28, bytes_accessed=5 << 20, transcendentals=0),
        name="panels",
    )(integrals, holes)


def terms_kernel(rel, triples, got_one, got_two, in1, in2, in3, panels, out, chosen):
    core = lax.rem(lax.axis_index("virt"), 2)
    off_i, off_j, live = row_of(triples, lax.axis_index("trip"), core, rel)
    which = jnp.where(live, off_i + off_j - 3, 3)
    for at, option in enumerate((got_one.at[0], got_one.at[1], got_two)):

        @pl.when(which == at)
        def _():
            chosen[...] = option[...]

    @pl.when(which == 3)
    def _():
        chosen[...] = jnp.zeros_like(chosen)

    blocks = (chosen, in1.at[rel], in2.at[rel], in3.at[rel])
    lead, second = [], []
    for d in range(4):
        block = blocks[d][...]
        packed = block[2 * T :]
        coulomb = jnp.concatenate(
            [packed[:, g * T : (g + 1) * T] for g in range(4)], axis=0
        )
        coulomb = jnp.concatenate([coulomb, jnp.zeros_like(coulomb)], axis=1)
        lead.append(jnp.concatenate([block[:T], coulomb], axis=1))
        second.append(jnp.concatenate([block[T : 2 * T], coulomb], axis=1))
    lead = jnp.concatenate(lead, axis=0)
    second = jnp.concatenate(second, axis=0)
    low = lane_low(T)
    contract = (((1,), (1,)), ((), ()))

    def group(step, _):
        panel = panels[pl.ds(pl.multiple_of(step * 8 * T, 8 * T), 8 * T), :]
        by_rows = lax.dot_general(panel, second, contract, preferred_element_type=F32)
        by_cols = lax.dot_general(lead, panel, contract, preferred_element_type=F32)

        def tiles_of(pair, duo):
            row = pair * 2 * T
            lanes = slice(duo * 2 * T, (duo + 1) * 2 * T)
            upper, lower = by_rows[row : row + T, lanes], by_rows[row + T : row + 2 * T, lanes]
            first = jnp.where(low, upper, swap_halves(lower))
            other = jnp.where(low, swap_halves(upper), lower)
            at = 2 * duo * T
            return (
                first + by_cols[at : at + T, row : row + 2 * T],
                other + by_cols[at + T : at + 2 * T, row : row + 2 * T],
            )

        for two in range(2):
            evens = tiles_of(2 * two, 0) + tiles_of(2 * two, 1)
            odds = tiles_of(2 * two + 1, 0) + tiles_of(2 * two + 1, 1)
            for d, (even, odd) in enumerate(zip(evens, odds)):
                if d == 0:
                    quarter = step // 2
                    at = pl.ds(pl.multiple_of((lax.rem(step, 2) * 2 + two) * T, T), T)
                    out[0, quarter * 4, at, :] = jnp.where(low, even, swap_halves(odd)).astype(BF16)
                    out[1, quarter, at, :] = jnp.where(low, swap_halves(even), odd).astype(BF16)
                else:
                    at = pl.ds(pl.multiple_of((step * 4 + 2 * two) * 8, 16), 16)
                    for quarter in range(4):
                        for half in range(2):
                            c = slice(half * H + quarter * 8, half * H + quarter * 8 + 8)
                            rows16 = jnp.concatenate([even[c], odd[c]], axis=0).astype(BF16)
                            index = quarter * 4 + d if half == 0 else d * 4 + quarter
                            out[half, index, at, :] = rows16
        return 0

    lax.fori_loop(0, 8, group, 0)


def terms(rel, triples, blocks, panels):
    vmem = pl.BlockSpec(memory_space=pltpu.VMEM)
    return pl.pallas_call(
        functools.partial(terms_kernel, rel),
        out_shape=jax.ShapeDtypeStruct((2, 16, 256, 2 * T), BF16),
        in_specs=[pl.BlockSpec(memory_space=pltpu.SMEM)] + [vmem] * 6,
        out_specs=vmem,
        scratch_shapes=[pltpu.VMEM((BLOCK_ROWS, 4 * T), BF16)],
        compiler_params=pltpu.CompilerParams(vmem_limit_bytes=VMEM_LIMIT),
        cost_estimate=pl.CostEstimate(flops=1 << 31, bytes_accessed=5 << 20, transcendentals=0),
        name="terms",
    )(triples, *blocks, panels)


def add_kernel(keep, got, first, *second):
    for half, outs in ((0, [first]), (1, second)):
        per_out = 16 // len(outs)
        for at, out in enumerate(outs):

            def one(index, _):
                source = at * per_out + index
                total = keep[half, source].astype(F32) + got[half, source].astype(F32)
                out[index] = total.astype(BF16)
                return 0

            lax.fori_loop(0, per_out, one, 0)


def add(keep, got):
    vmem = pl.BlockSpec(memory_space=pltpu.VMEM)
    first = jax.ShapeDtypeStruct((16, 256, 2 * T), BF16)
    second = jax.ShapeDtypeStruct((4, 256, 2 * T), BF16)
    return pl.pallas_call(
        add_kernel,
        out_shape=(first,) + (second,) * 4,
        in_specs=[vmem] * 2,
        out_specs=[vmem] * 5,
        compiler_params=pltpu.CompilerParams(vmem_limit_bytes=VMEM_LIMIT),
        name="add",
    )(keep, got)


def gather_terms(mid_is_j, one, two, three, by_j, by_i):
    middle = two.astype(F32)
    by_j[...] = one.astype(F32) + jnp.where(mid_is_j, middle, 0.0)
    by_i[...] = three.astype(F32) + jnp.where(mid_is_j, 0.0, middle)


def turned_sum(own, by_j, by_i, base, q):
    low = lane_low(H)

    def as_rows(table):
        even = table[pl.ds(base + 2 * q, H, stride=8), :]
        odd = table[pl.ds(base + 2 * q + 1, H, stride=8), :]
        top = jnp.where(low, even, swap_halves(odd))
        bottom = jnp.where(low, swap_halves(even), odd)
        return jnp.concatenate([top, bottom], axis=0)

    flat = as_rows(by_i).T
    return own + as_rows(by_j) + jnp.concatenate([flat[:T], flat[T:]], axis=1)


def middle_is_j(triples):
    core = lax.rem(lax.axis_index("virt"), 2)
    _, off_j, _ = row_of(triples, lax.axis_index("trip"), core, 0)
    return off_j == 2


def combine_kernel(triples, own, one, two, three, out, by_j, by_i):
    mid_is_j = middle_is_j(triples)
    for quarter in range(4):
        rows = pl.ds(quarter * 256, 256)
        gather_terms(
            mid_is_j, one[quarter], two[quarter], three[quarter], by_j.at[rows], by_i.at[rows]
        )
    for quarter in range(4):
        for q in range(4):
            at = slice(q * T, (q + 1) * T)
            total = turned_sum(own[quarter, at, :].astype(F32), by_j, by_i, quarter * 256, q)
            out[quarter, at, :] = total.astype(BF16)


def combine(triples, own, one, two, three):
    vmem = pl.BlockSpec(memory_space=pltpu.VMEM)
    return pl.pallas_call(
        combine_kernel,
        out_shape=jax.ShapeDtypeStruct((4, 256, 2 * T), BF16),
        in_specs=[pl.BlockSpec(memory_space=pltpu.SMEM)] + [vmem] * 4,
        out_specs=vmem,
        scratch_shapes=[pltpu.VMEM((1024, 2 * T), F32)] * 2,
        compiler_params=pltpu.CompilerParams(vmem_limit_bytes=VMEM_LIMIT),
        name="combine",
    )(triples, own, one, two, three)


def finish_kernel(triples, own, one, two, three, others, out, by_j, by_i):
    gather_terms(middle_is_j(triples), one[:256], two[:256], three[:256], by_j, by_i)
    for q in range(4):
        at = slice(q * T, (q + 1) * T)
        total = turned_sum(own[at, :], by_j, by_i, 0, q).astype(BF16)
        second = sum(others[source, at, :].astype(F32) for source in range(4)).astype(BF16)
        for copy in range(4):
            out[copy, at, :] = total
            out[copy, 256 + q * T : 256 + (q + 1) * T, :] = second


def finish(triples, own, shares, others):
    vmem = pl.BlockSpec(memory_space=pltpu.VMEM)
    return pl.pallas_call(
        finish_kernel,
        out_shape=jax.ShapeDtypeStruct((4, 512, 2 * T), BF16),
        in_specs=[pl.BlockSpec(memory_space=pltpu.SMEM)] + [vmem] * 5,
        out_specs=vmem,
        scratch_shapes=[pltpu.VMEM((256, 2 * T), F32)] * 2,
        compiler_params=pltpu.CompilerParams(vmem_limit_bytes=VMEM_LIMIT),
        name="finish",
    )(triples, own, *shares, others)


def energy_kernel(triples, parts, extra_a, extra_b, inverse, out, whole, flipped, acc, rows_b):
    core = lax.rem(lax.axis_index("virt"), 2)
    _, _, live = row_of(triples, lax.axis_index("trip"), core, 0)
    low = lane_low(T)
    for quarter in range(4):
        for q in range(4):
            first = parts[quarter, q * T : (q + 1) * T, :].astype(F32)
            second = parts[quarter, 256 + q * T : 256 + (q + 1) * T, :].astype(F32)
            at = (quarter * 8 + 2 * q) * T
            whole[at : at + T, :] = jnp.where(low, first, swap_halves(second))
            whole[at + T : at + 2 * T, :] = jnp.where(low, swap_halves(first), second)

    low32 = lax.broadcasted_iota(jnp.int32, (H, 2 * T), 1) % T < H
    low_half = lane_low(H)

    def flip(step, _):
        b = step * 4
        across = jnp.concatenate(
            [whole[pl.ds(b + at, H, stride=T), :] for at in range(4)], axis=0
        ).T
        first = [across[at * H : (at + 1) * H] for at in (0, 2, 1, 3)]
        mid = [None] * 4
        for at in range(2):
            x, z = first[at], first[at + 2]
            mid[at] = jnp.where(low_half, x, swap_halves(z))
            mid[at + 2] = jnp.where(low_half, swap_halves(x), z)
        for at in (0, 2):
            x, z = mid[at], mid[at + 1]
            for inner, value in (
                (0, jnp.where(low32, x, pltpu.roll(z, H, 1))),
                (1, jnp.where(low32, pltpu.roll(x, 3 * H, 1), z)),
            ):
                rows = pl.ds(pl.multiple_of((b + at + inner) * H, H), H)
                flipped[rows, :] = value
        return 0

    lax.fori_loop(0, T // 4, flip, 0, unroll=2)
    acc[...] = jnp.zeros_like(acc)

    def pair(bp, _):
        from_flipped = pack_rows(flipped[pl.ds(bp, T, stride=H), :])
        from_whole = pack_rows(whole[pl.ds(pl.multiple_of(bp * T, T), T), :])
        for half in range(2):
            b = bp + H * half
            at = pl.ds(pl.multiple_of(b * H, H), H)
            plain = whole[pl.ds(b, H, stride=T), :]
            turned = flipped[at, :]
            inv = inverse[at, :]
            first = (4.0 * plain + from_flipped[half]) * (plain - turned + extra_a[at, :]) * inv
            second = plain * (from_flipped[half] - from_whole[half] + extra_b[at, :]) * inv
            acc[...] += first
            rows_b[pl.ds(b, 1), :] = jnp.sum(second, axis=0, keepdims=True)
        return 0

    lax.fori_loop(0, H, pair, 0, unroll=2)
    by_a = jnp.sum(acc[...], axis=0, keepdims=True)
    by_a = by_a[:, :T] + by_a[:, T:]
    by_b = jnp.sum(rows_b[...].T, axis=0, keepdims=True)
    out[...] = jnp.where(live, by_a + by_b, 0.0)


def energy_of(triples, parts, extra_a, extra_b, inverse):
    vmem = pl.BlockSpec(memory_space=pltpu.VMEM)
    return pl.pallas_call(
        energy_kernel,
        out_shape=jax.ShapeDtypeStruct((1, T), F32),
        in_specs=[pl.BlockSpec(memory_space=pltpu.SMEM)] + [vmem] * 4,
        out_specs=vmem,
        scratch_shapes=[
            pltpu.VMEM((H * T, 2 * T), F32),
            pltpu.VMEM((H * T, 2 * T), F32),
            pltpu.VMEM((H, 2 * T), F32),
            pltpu.VMEM((T, 2 * T), F32),
        ],
        compiler_params=pltpu.CompilerParams(vmem_limit_bytes=VMEM_LIMIT),
        name="energy",
    )(triples, parts, extra_a, extra_b, inverse)


def tables_kernel(
    triples, own, one, two, three, virt_energy, extra_a, extra_b, inverse, columns, rows, scalars
):
    core = lax.rem(lax.axis_index("virt"), 2)
    off_i, off_j, _ = row_of(triples, lax.axis_index("trip"), core, 0)
    low = lane_low(H)

    def small_of(table):
        return table[table.shape[0] - SMALL_ROWS :, :]

    def exch(table, index):
        flat = small_of(table)[index * H : (index + 1) * H, :].astype(F32)
        return jnp.concatenate([flat[:, :T], flat[:, T:]], axis=0)

    def pick(options, index):
        result = options[-1]
        for at in range(len(options) - 1):
            result = jnp.where(index == at, options[at], result)
        return result

    kj = pick([exch(own, 0), exch(own, 1)], off_j - 1)
    ki = pick([exch(own, 1), exch(own, 2)], off_i - 2)
    ji = pick([exch(one, 0), exch(one, 1), exch(two, 0)], off_i + off_j - 3)
    kj_t, ki_t, ji_t = kj.T, ki.T, ji.T
    heads = [small_of(x)[3 * H :, :].astype(F32) for x in (own, one, two, three)]
    head_i = pick([heads[2], heads[3]], off_i - 2)
    head_j = pick([heads[1], heads[2]], off_j - 1)
    head_k = heads[0]
    occ = head_i[0:1, T:] + head_j[0:1, T:] + head_k[0:1, T:]
    occ = jnp.concatenate([occ, occ], axis=1)

    def dup(m):
        return jnp.concatenate([m, m], axis=1)

    def by_row(v):
        return jnp.broadcast_to(v, (2 * T, T)).T

    def by_c(column):
        return jnp.where(low, column[:H], column[H:])

    def packed(m):
        return jnp.concatenate([m[:H], m[H:]], axis=1)

    s_i, s_j, s_k, e_v = (*(x[0:1, :T] for x in (head_i, head_j, head_k)), virt_energy[...])
    for at, v in enumerate((s_i, s_j, s_k, e_v)):
        scalars[at * T : (at + 1) * T, :] = by_row(v)
    si_a, sk_a, e_a = dup(s_i), dup(s_k), dup(e_v)
    si_c, sj_c, sk_c, e_c = (by_c(scalars[at * T : (at + 1) * T, :]) for at in range(4))
    for at, m in enumerate((kj, ji_t, kj_t, ji)):
        columns[at * H : (at + 1) * H, :] = packed(m).astype(BF16)
    for at, m in enumerate((kj_t, ji, ki_t - ki)):
        rows[at * T : (at + 1) * T, :] = dup(m)
    ki_diff = packed(ki - ki_t)
    kj_ac = packed(kj_t)
    ji_ca = packed(ji)
    base = occ - e_a - e_c
    source = lax.broadcasted_iota(jnp.int32, (2 * T, 2 * T), 0)
    target = lax.broadcasted_iota(jnp.int32, (2 * T, 2 * T), 1)
    same_half = (source >= T) == (target >= T)

    def one_b(b, _):
        at = pl.ds(pl.multiple_of(b * H, H), H)
        spread = jnp.where(same_half & (jnp.bitwise_and(source, T - 1) == b), 1.0, 0.0).astype(BF16)
        over_c = jnp.dot(columns[...], spread, preferred_element_type=F32)
        kj_cb, ji_bc, kj_bc, ji_cb = (over_c[g * H : (g + 1) * H] for g in range(4))
        kj_ab, ji_ba, ki_ab = (rows[pl.ds(g * T + b, 1), :] for g in range(3))
        si_b, sj_b, sk_b, e_b = (scalars[pl.ds(g * T + b, 1), :] for g in range(4))
        extra_a[at, :] = (
            si_a * kj_cb - si_c * kj_ab + sj_b * ki_diff + sk_c * ji_ba - sk_a * ji_bc
        )
        extra_b[at, :] = (
            si_b * kj_ac - si_a * kj_bc + sj_c * ki_ab + sk_a * ji_cb - sk_b * ji_ca
        )
        inverse[at, :] = 1.0 / (base - e_b)
        return 0

    lax.fori_loop(0, T, one_b, 0, unroll=2)


def tables(triples, small, virt_energy):
    vmem = pl.BlockSpec(memory_space=pltpu.VMEM)
    table = jax.ShapeDtypeStruct((H * T, 2 * T), F32)
    return pl.pallas_call(
        tables_kernel,
        out_shape=(table, table, table),
        in_specs=[pl.BlockSpec(memory_space=pltpu.SMEM)] + [vmem] * 5,
        out_specs=[vmem] * 3,
        scratch_shapes=[
            pltpu.VMEM((4 * H, 2 * T), BF16),
            pltpu.VMEM((3 * T, 2 * T), F32),
            pltpu.VMEM((4 * T, 2 * T), F32),
        ],
        compiler_params=pltpu.CompilerParams(vmem_limit_bytes=VMEM_LIMIT),
        cost_estimate=pl.CostEstimate(flops=1 << 28, bytes_accessed=3 << 20, transcendentals=0),
        name="tables",
    )(triples, *small, virt_energy)


def local(
    virt_integrals,
    pair_amps,
    hole_amps,
    coulomb_ints,
    exchange_ints,
    singles,
    occ_energy,
    virt_energy,
    triples,
):
    n_trip = lax.axis_size("trip")

    out1, out2, out3, up1, up2 = prep(
        triples, pair_amps.reshape(3, 2 * T, 4 * T), coulomb_ints.reshape(coulomb_ints.shape[1:])
    )
    got_two = lax.ppermute(up2, "trip", shift_route(n_trip, -2))
    in2 = lax.ppermute(out2, "trip", shift_route(n_trip, 2))
    got_one = lax.ppermute(up1, "trip", shift_route(n_trip, -1))
    in1 = lax.ppermute(out1, "trip", shift_route(n_trip, 1))
    in3 = lax.ppermute(out3, "trip", shift_route(n_trip, 3))
    blocks = (got_one, got_two, in1, in2, in3)

    panels = panels_of(
        virt_integrals.reshape(4 * T, T * T), hole_amps.reshape(hole_amps.shape[1:])
    )

    send = terms(1, triples, blocks, panels)
    got = lax.ppermute(send, "virt", CORE_ROUTE)
    keep = terms(0, triples, blocks, panels)
    first_half, *second_half = add(keep, got)
    over_y = functools.partial(
        lax.all_to_all,
        axis_name="virt",
        split_axis=0,
        concat_axis=0,
        axis_index_groups=[[0, 2, 4, 6], [1, 3, 5, 7]],
        tiled=True,
    )
    by_y = over_y(first_half)
    by_owner = [
        lax.ppermute(second_half[d], "trip", shift_route(n_trip, -d)) for d in (1, 2, 3)
    ]

    exchange = exchange_ints.reshape(3, 2, H, T)
    exchange = jnp.concatenate([exchange[:, 0], exchange[:, 1]], axis=2).reshape(3 * H, 2 * T)
    heads = jnp.concatenate([singles, jnp.broadcast_to(occ_energy[:, None], (1, T))], axis=1)
    small = jnp.concatenate([exchange, heads, jnp.zeros((15, 2 * T), BF16)], axis=0)
    total = by_y.reshape(4, 4, 256, 2 * T).astype(F32)
    total = total[0] + total[1] + total[2] + total[3]
    to_share = [jnp.concatenate([total[d].astype(BF16), small], axis=0) for d in (1, 2, 3)]
    shares = [
        lax.ppermute(to_share[d - 1], "trip", shift_route(n_trip, -d)) for d in (1, 2, 3)
    ]
    by_owner, _ = lax.optimization_barrier((by_owner, to_share))
    second_sums = over_y(combine(triples, second_half[0], *by_owner))

    chunk = finish(triples, total[0], shares, second_sums)
    parts = over_y(chunk)
    extra_a, extra_b, inverse = tables(triples, [small, *shares], virt_energy.reshape(1, T))

    mine = energy_of(triples, parts, extra_a, extra_b, inverse)
    other = lax.ppermute(mine, "virt", CORE_ROUTE)
    first = lax.rem(lax.axis_index("virt"), 2) == 0
    return jnp.where(
        first, jnp.concatenate([mine, other], axis=0), jnp.concatenate([other, mine], axis=0)
    )


def solution(mesh):
    placed = (
        P("trip", "virt", None),
        P("trip", None, None, None, "virt"),
        P("trip", "virt", None),
        P("trip", None, "virt", None),
        P("trip", None, None),
        P("trip", None),
        P("trip"),
        P(),
        P("trip", None),
    )
    return jax.shard_map(
        local, mesh=mesh, in_specs=placed, out_specs=P("trip", None), check_vma=False
    )
```

time: 131 us -> 118 us (0.901)
  the two profiles are of different devices: /device:TPU:417 before, /device:TPU:389 now
where the time goes in v3:
time: 118 us; the launch traced here: 117 us
  starting transfers between devices  64.9 us (55%)
  Pallas kernels  36.2 us (31%)
  local copies, waits for them, and re-layouts  7.28 us (6%)
  waiting for transfers between devices  6.27 us (5%)
    ppermute x3, starting transfers between devices, local(): lax.ppermute(second_half[d], 'trip', shift_route(n_trip, -d))  14.2 us
    ppermute x3, starting transfers between devices, local(): lax.ppermute(to_share[d - 1], 'trip', shift_route(n_trip, -d))  14.1 us
    pallas_call x2, Pallas kernels, terms(): pl.pallas_call(functools.partial(terms_kernel, rel), out_shape=jax.ShapeD...  11.4 us
    unnamed x22, local copies, waits for them, and re-layouts  7.13 us
    pallas_call x1, Pallas kernels, tables(): pl.pallas_call(tables_kernel, out_shape=(table, table, table), in_specs=[...  6.09 us
    ppermute x1, starting transfers between devices, local(): other = lax.ppermute(mine, 'virt', CORE_ROUTE)  5.89 us
    pallas_call x1, Pallas kernels, energy_of(): pl.pallas_call(energy_kernel, out_shape=jax.ShapeDtypeStruct((1, T), F32)...  5.52 us
    all_to_all x1, waiting for transfers between devices, local(): second_sums = over_y(combine(triples, second_half[0], *by_owner))  5.44 us
  transfers between devices with their start and end apart: 16, of which 2 were waited for; matrix products, arithmetic and copies ran while one was open for 1% of the time, Pallas kernels for 18%

profile of v3, /device:TPU:389, one launch (start us, length us, event | category | flops | bytes accessed | tf_op | source)
XLA Modules:
  0.0 116.8 jit_solution(654667590507439996)
XLA Ops:
  0.0 0.0 copy-start.4
  0.0 0.9 copy-done.4
  0.9 0.0 copy-start.5
  0.9 0.8 copy-done.5
  1.7 0.0 copy-start.6
  1.7 0.7 copy-done.6
  2.4 1.1 prep.1
  3.5 2.2 %collective-permute-start = (bf16[2,144,256]{2,1,0:T(8,128)(2,1)S(1)}, bf16[2,144,256]{2,1,0:T(8,128)(2,1)S(1)}, u32[]{:S(2)}, u32[]{:S(2)}) collective-permute-start(bf16[2,144,256]{2,1,0:T(8,128)(2,1)S(1)} %get-tuple-element.21), channel_id=1, source_target_pairs={{8,0},{16,8},{24,16},{32,24},{40,32},{48,40},{56,48},{64,56},{72,6... | collective-permute-start | bytes 442376 | tf_op jit(solution)/shard_map/ppermute | solution.py:548
  5.6 3.1 %collective-permute-start.2 = (bf16[2,144,256]{2,1,0:T(8,128)(2,1)S(1)}, bf16[2,144,256]{2,1,0:T(8,128)(2,1)S(1)}, u32[]{:S(2)}, u32[]{:S(2)}) collective-permute-start(bf16[2,144,256]{2,1,0:T(8,128)(2,1)S(1)} %get-tuple-element.23), channel_id=1, source_target_pairs={{0,8},{8,16},{16,24},{24,32},{32,40},{40,48},{48,56},{56,64},{64,7... | collective-permute-start | bytes 442376 | tf_op jit(solution)/shard_map/ppermute | solution.py:549
  8.8 4.1 %collective-permute-start.3 = (bf16[2,144,256]{2,1,0:T(8,128)(2,1)S(1)}, bf16[2,144,256]{2,1,0:T(8,128)(2,1)S(1)}, u32[]{:S(2)}, u32[]{:S(2)}) collective-permute-start(bf16[2,144,256]{2,1,0:T(8,128)(2,1)S(1)} %get-tuple-element.24), channel_id=1, source_target_pairs={{0,16},{8,24},{16,32},{24,40},{32,48},{40,56},{48,64},{56,72},{64,... | collective-permute-start | bytes 442376 | tf_op jit(solution)/shard_map/ppermute | solution.py:547
  12.8 4.4 %collective-permute-start.4 = (bf16[2,144,256]{2,1,0:T(8,128)(2,1)S(1)}, bf16[2,144,256]{2,1,0:T(8,128)(2,1)S(1)}, u32[]{:S(2)}, u32[]{:S(2)}) collective-permute-start(bf16[2,144,256]{2,1,0:T(8,128)(2,1)S(1)} %get-tuple-element.25), channel_id=1, source_target_pairs={{0,24},{8,32},{16,40},{24,48},{32,56},{40,64},{48,72},{56,80},{64,... | collective-permute-start | bytes 442376 | tf_op jit(solution)/shard_map/ppermute | solution.py:550
  17.3 2.1 %collective-permute-start.1 = (bf16[144,256]{1,0:T(8,128)(2,1)S(1)}, bf16[144,256]{1,0:T(8,128)(2,1)S(1)}, u32[]{:S(2)}, u32[]{:S(2)}) collective-permute-start(bf16[144,256]{1,0:T(8,128)(2,1)S(1)} %get-tuple-element.22), channel_id=1, source_target_pairs={{16,0},{24,8},{32,16},{40,24},{48,32},{56,40},{64,48},{72,56},{80,... | collective-permute-start | bytes 221192 | tf_op jit(solution)/shard_map/ppermute | solution.py:546
  19.4 0.0 copy-start
  19.4 1.6 %copy-done = bf16[1,256,4096]{2,1,0:T(8,128)(2,1)S(1)} copy-done((bf16[1,256,4096]{2,1,0:T(8,128)(2,1)S(1)}, bf16[1,256,4096]{2,1,0:T(8,128)(2,1)}, u32[]{:S(2)}) %copy-start) | copy-done | bytes 2097176
  20.9 0.0 copy-start.3
  21.0 1.0 copy-done.3
  21.9 5.2 %panels.1 = bf16[4096,384]{1,0:T(8,128)(2,1)S(1)} custom-call(bf16[256,4096]{1,0:T(8,128)(2,1)S(1)} %bitcast.21, bf16[38,4096]{1,0:T(8,128)(2,1)S(1)} %bitcast.22), custom_call_target="tpu_custom_call" | custom-call | flops 268435456 | bytes 5242880 | tf_op jit(solution)/shard_map/panels/pallas_call | solution.py:149
  27.1 0.0 collective-permute-done.1.got_two
  27.1 0.0 collective-permute-done.got_one
  27.1 0.0 collective-permute-done.2.in1
  27.2 0.0 collective-permute-done.3.in2
  27.2 0.0 collective-permute-done.4.in3
  27.2 0.0 copy-done.7
  27.2 5.7 %terms.3 = bf16[2,16,256,128]{3,2,1,0:T(8,128)(2,1)S(1)} custom-call(s32[2,3]{1,0:T(2,128)S(1)} %copy-done.7, bf16[2,144,256]{2,1,0:T(8,128)(2,1)S(1)} %collective-permute-done.got_one, bf16[144,256]{1,0:T(8,128)(2,1)S(1)} %collective-permute-done.1.got_two, bf16[2,144,256]{2,1,0:T(8,128)(2,1)S(1)} %collective-permute-done.2.in1, ...), custom_call_target="tpu_custom_call" | custom-call | flops 2147483648 | bytes 5242880 | tf_op jit(solution)/shard_map/terms/pallas_call | solution.py:236
  32.9 3.7 %collective-permute-start.5 = (bf16[2,16,256,128]{3,2,1,0:T(8,128)(2,1)S(1)}, bf16[2,16,256,128]{3,2,1,0:T(8,128)(2,1)S(1)}, u32[]{:S(2)}, u32[]{:S(2)}) collective-permute-start(bf16[2,16,256,128]{3,2,1,0:T(8,128)(2,1)S(1)} %terms.3), channel_id=1, source_target_pairs={{0,1},{1,0},{2,3},{3,2},{4,5},{5,4},{6,7},{7,6},{8,9},{9,8},{10,11... | collective-permute-start | bytes 6291464 | tf_op jit(solution)/shard_map/ppermute | solution.py:558
  36.6 5.7 %terms.2.keep = bf16[2,16,256,128]{3,2,1,0:T(8,128)(2,1)S(1)} custom-call(s32[2,3]{1,0:T(2,128)S(1)} %copy-done.7, bf16[2,144,256]{2,1,0:T(8,128)(2,1)S(1)} %collective-permute-done.got_one, bf16[144,256]{1,0:T(8,128)(2,1)S(1)} %collective-permute-done.1.got_two, bf16[2,144,256]{2,1,0:T(8,128)(2,1)S(1)} %collective-permute-done.2.in1, ...), custom_call_target="tpu_custom_call" | custom-call | flops 2147483648 | bytes 5242880 | tf_op jit(solution)/shard_map/terms/pallas_call | solution.py:236
  42.3 0.0 collective-permute-done.5.got
  42.3 1.6 %add.27 = (bf16[16,256,128]{2,1,0:T(8,128)(2,1)}, bf16[4,256,128]{2,1,0:T(8,128)(2,1)S(1)}, bf16[4,256,128]{2,1,0:T(8,128)(2,1)S(1)}, bf16[4,256,128]{2,1,0:T(8,128)(2,1)S(1)}, bf16[4,256,128]{2,1,0:T(8,128)(2,1)S(1)}) custom-call(bf16[2,16,256,128]{3,2,1,0:T(8,128)(2,1)S(1)} %terms.2.keep, bf16[2,16,256,128]{3,2,1,0:T(8,128)(2,1)S(1)} %collective-permute-done.5.got), custom_call_target="tpu_custom_call" | custom-call | tf_op jit(solution)/shard_map/add/pallas_call | solution.py:266
  43.9 4.3 %all-to-all-start = ((bf16[16,256,128]{2,1,0:T(8,128)(2,1)}), bf16[16,256,128]{2,1,0:T(8,128)(2,1)S(1)}, u32[]{:S(2)}, u32[]{:S(2)}) async-start(bf16[16,256,128]{2,1,0:T(8,128)(2,1)} %get-tuple-element.26), calls=%async_computation | async-start | bytes 2097152 | tf_op jit(solution)/shard_map/all_to_all | solution.py:569
  48.9 0.0 copy-done.9
  48.9 0.1 reshape.44
  49.0 0.0 copy-done.10
  49.0 4.0 %collective-permute-start.9 = (bf16[4,256,128]{2,1,0:T(8,128)(2,1)S(1)}, bf16[4,256,128]{2,1,0:T(8,128)(2,1)S(1)}, u32[]{:S(2)}, u32[]{:S(2)}) collective-permute-start(bf16[4,256,128]{2,1,0:T(8,128)(2,1)S(1)} %get-tuple-element.28), channel_id=1, source_target_pairs={{8,0},{16,8},{24,16},{32,24},{40,32},{48,40},{56,48},{64,56},{72,6... | collective-permute-start | bytes 786440 | tf_op jit(solution)/shard_map/ppermute | solution.py:571
  53.0 5.7 %collective-permute-start.10 = (bf16[4,256,128]{2,1,0:T(8,128)(2,1)S(1)}, bf16[4,256,128]{2,1,0:T(8,128)(2,1)S(1)}, u32[]{:S(2)}, u32[]{:S(2)}) collective-permute-start(bf16[4,256,128]{2,1,0:T(8,128)(2,1)S(1)} %get-tuple-element.29), channel_id=1, source_target_pairs={{16,0},{24,8},{32,16},{40,24},{48,32},{56,40},{64,48},{72,56},{80,... | collective-permute-start | bytes 786440 | tf_op jit(solution)/shard_map/ppermute | solution.py:571
  58.7 4.5 %collective-permute-start.11 = (bf16[4,256,128]{2,1,0:T(8,128)(2,1)S(1)}, bf16[4,256,128]{2,1,0:T(8,128)(2,1)S(1)}, u32[]{:S(2)}, u32[]{:S(2)}) collective-permute-start(bf16[4,256,128]{2,1,0:T(8,128)(2,1)S(1)} %get-tuple-element.30), channel_id=1, source_target_pairs={{24,0},{32,8},{40,16},{48,24},{56,32},{64,40},{72,48},{80,56},{88,... | collective-permute-start | bytes 786440 | tf_op jit(solution)/shard_map/ppermute | solution.py:571
  63.3 0.0 all-to-all-done
  63.3 0.2 convert_element_type.16
  63.5 0.1 fusion
  63.6 0.1 pad_maximum_fusion
  63.7 3.9 %collective-permute-start.6 = (bf16[368,128]{1,0:T(8,128)(2,1)S(1)}, bf16[368,128]{1,0:T(8,128)(2,1)S(1)}, u32[]{:S(2)}, u32[]{:S(2)}) collective-permute-start(bf16[368,128]{1,0:T(8,128)(2,1)S(1)} %get-tuple-element.44), channel_id=1, source_target_pairs={{8,0},{16,8},{24,16},{32,24},{40,32},{48,40},{56,48},{64,56},{72,6... | collective-permute-start | bytes 282632 | tf_op jit(solution)/shard_map/ppermute | solution.py:582
  67.6 5.7 %collective-permute-start.7 = (bf16[368,128]{1,0:T(8,128)(2,1)S(1)}, bf16[368,128]{1,0:T(8,128)(2,1)S(1)}, u32[]{:S(2)}, u32[]{:S(2)}) collective-permute-start(bf16[368,128]{1,0:T(8,128)(2,1)S(1)} %get-tuple-element.43), channel_id=1, source_target_pairs={{16,0},{24,8},{32,16},{40,24},{48,32},{56,40},{64,48},{72,56},{80,... | collective-permute-start | bytes 282632 | tf_op jit(solution)/shard_map/ppermute | solution.py:582
  73.3 0.0 collective-permute-done.9.one
  73.3 4.5 %collective-permute-start.8 = (bf16[368,128]{1,0:T(8,128)(2,1)S(1)}, bf16[368,128]{1,0:T(8,128)(2,1)S(1)}, u32[]{:S(2)}, u32[]{:S(2)}) collective-permute-start(bf16[368,128]{1,0:T(8,128)(2,1)S(1)} %get-tuple-element.42), channel_id=1, source_target_pairs={{24,0},{32,8},{40,16},{48,24},{56,32},{64,40},{72,48},{80,56},{88,... | collective-permute-start | bytes 282632 | tf_op jit(solution)/shard_map/ppermute | solution.py:582
  77.9 0.0 collective-permute-done.10.two
  77.9 0.0 collective-permute-done.11.three
  77.9 0.0 copy-start.8
  77.9 3.6 %combine.1 = bf16[4,256,128]{2,1,0:T(8,128)(2,1)} custom-call(s32[2,3]{1,0:T(2,128)S(1)} %copy-done.7, bf16[4,256,128]{2,1,0:T(8,128)(2,1)S(1)} %get-tuple-element.27.own, bf16[4,256,128]{2,1,0:T(8,128)(2,1)S(1)} %collective-permute-done.9.one, bf16[4,256,128]{2,1,0:T(8,128)(2,1)S(1)} %collective-permute-done.10.two, ...), custom_call_target="tpu_custom_call" | custom-call | tf_op jit(solution)/shard_map/combine/pallas_call | solution.py:318
  81.5 3.4 %all-to-all-start.1 = ((bf16[4,256,128]{2,1,0:T(8,128)(2,1)}), bf16[4,256,128]{2,1,0:T(8,128)(2,1)S(1)}, u32[]{:S(2)}, u32[]{:S(2)}) async-start(bf16[4,256,128]{2,1,0:T(8,128)(2,1)} %combine.1), calls=%async_computation.1 | async-start | bytes 524288 | tf_op jit(solution)/shard_map/all_to_all | solution.py:585
  85.0 0.0 collective-permute-done.6.one
  85.0 0.0 collective-permute-done.7.two
  85.0 0.0 collective-permute-done.8.three
  85.0 5.4 %all-to-all-done.1.others = bf16[4,256,128]{2,1,0:T(8,128)(2,1)S(1)} async-done(((bf16[4,256,128]{2,1,0:T(8,128)(2,1)}), bf16[4,256,128]{2,1,0:T(8,128)(2,1)S(1)}, u32[]{:S(2)}, u32[]{:S(2)}) %all-to-all-start.1) | async-done | bytes 262176 | tf_op jit(solution)/shard_map/all_to_all | solution.py:585
  90.4 1.7 %finish.1 = bf16[4,512,128]{2,1,0:T(8,128)(2,1)} custom-call(s32[2,3]{1,0:T(2,128)S(1)} %copy-done.7, f32[256,128]{1,0:T(8,128)S(1)} %slice_bitcast_fusion.own, bf16[368,128]{1,0:T(8,128)(2,1)S(1)} %collective-permute-done.6.one, bf16[368,128]{1,0:T(8,128)(2,1)S(1)} %collective-permute-done.7.two, bf16[368,128]{1,0:T(8,128)(2,1)S(1)} %collective-permute-done.8.three, ...), custom_call_target="tpu_custom_call" | custom-call | tf_op jit(solution)/shard_map/finish/pallas_call | solution.py:342
  92.1 3.5 %all-to-all-start.2 = ((bf16[4,512,128]{2,1,0:T(8,128)(2,1)}), bf16[4,512,128]{2,1,0:T(8,128)(2,1)S(1)}, u32[]{:S(2)}, u32[]{:S(2)}) async-start(bf16[4,512,128]{2,1,0:T(8,128)(2,1)} %finish.1), calls=%async_computation.2 | async-start | bytes 1048576 | tf_op jit(solution)/shard_map/all_to_all | solution.py:588
  95.6 0.1 pad_maximum_fusion.7.own
  95.7 0.0 copy-done.8
  95.7 6.1 %tables.1 = (f32[2048,128]{1,0:T(8,128)S(1)}, f32[2048,128]{1,0:T(8,128)S(1)}, f32[2048,128]{1,0:T(8,128)S(1)}) custom-call(s32[2,3]{1,0:T(2,128)S(1)} %copy-done.7, bf16[112,128]{1,0:T(8,128)(2,1)S(1)} %pad_maximum_fusion.7.own, bf16[368,128]{1,0:T(8,128)(2,1)S(1)} %collective-permute-done.6.one, bf16[368,128]{1,0:T(8,128)(2,1)S(1)} %collective-permute-done.7.two, ...), custom_call_target="tpu_custom_call" | custom-call | flops 268435456 | bytes 3145728 | tf_op jit(solution)/shard_map/tables/pallas_call | solution.py:514
  101.8 1.0 copy-done.1
  102.8 0.0 all-to-all-done.2.parts
  102.8 1.2 %copy-done.2 = f32[2048,128]{1,0:T(8,128)S(1)} copy-done((f32[2048,128]{1,0:T(8,128)S(1)}, f32[2048,128]{1,0:T(8,128)}, u32[]{:S(2)}) %copy-start.2) | copy-done | bytes 1048600
  104.0 5.5 %energy.1 = f32[1,64]{1,0:T(1,128)S(1)} custom-call(s32[2,3]{1,0:T(2,128)S(1)} %copy-done.7, bf16[4,512,128]{2,1,0:T(8,128)(2,1)S(1)} %all-to-all-done.2.parts, f32[2048,128]{1,0:T(8,128)S(1)} %get-tuple-element.34.extra_a, f32[2048,128]{1,0:T(8,128)S(1)} %get-tuple-element.35.extra_b, f32[2048,128]{1,0:T(8,128)S(1)} %copy-done.2), custom_call_target="tpu_custom_call" | custom-call | tf_op jit(solution)/shard_map/energy/pallas_call | solution.py:416
  109.5 5.9 %collective-permute-start.12 = (f32[1,64]{1,0:T(1,128)S(1)}, f32[1,64]{1,0:T(1,128)S(1)}, u32[]{:S(2)}, u32[]{:S(2)}) collective-permute-start(f32[1,64]{1,0:T(1,128)S(1)} %energy.1), channel_id=1, source_target_pairs={{0,1},{1,0},{2,3},{3,2},{4,5},{5,4},{6,7},{7,6},{8,9},{9,8},{10,11... | collective-permute-start | bytes 776 | tf_op jit(solution)/shard_map/ppermute | solution.py:592
  115.4 0.8 collective-permute-done.12
  116.2 0.6 maximum_select_fusion
  (10 shorter events, 0.1 us)
Async XLA Ops:
  0.0 0.9 copy-start.4
  0.9 0.8 copy-start.5
  1.7 0.7 copy-start.6
  3.5 23.7 %collective-permute-start = (bf16[2,144,256]{2,1,0:T(8,128)(2,1)S(1)}, bf16[2,144,256]{2,1,0:T(8,128)(2,1)S(1)}, u32[]{:S(2)}, u32[]{:S(2)}) collective-permute-start(bf16[2,144,256]{2,1,0:T(8,128)(2,1)S(1)} %get-tuple-element.21), channel_id=1, source_target_pairs={{8,0},{16,8},{24,16},{32,24},{40,32},{48,40},{56,48},{64,56},{72,6... | collective-permute-start | bytes 442376 | tf_op jit(solution)/shard_map/ppermute | solution.py:548
  5.6 21.5 %collective-permute-start.2 = (bf16[2,144,256]{2,1,0:T(8,128)(2,1)S(1)}, bf16[2,144,256]{2,1,0:T(8,128)(2,1)S(1)}, u32[]{:S(2)}, u32[]{:S(2)}) collective-permute-start(bf16[2,144,256]{2,1,0:T(8,128)(2,1)S(1)} %get-tuple-element.23), channel_id=1, source_target_pairs={{0,8},{8,16},{16,24},{24,32},{32,40},{40,48},{48,56},{56,64},{64,7... | collective-permute-start | bytes 442376 | tf_op jit(solution)/shard_map/ppermute | solution.py:549
  8.8 18.4 %collective-permute-start.3 = (bf16[2,144,256]{2,1,0:T(8,128)(2,1)S(1)}, bf16[2,144,256]{2,1,0:T(8,128)(2,1)S(1)}, u32[]{:S(2)}, u32[]{:S(2)}) collective-permute-start(bf16[2,144,256]{2,1,0:T(8,128)(2,1)S(1)} %get-tuple-element.24), channel_id=1, source_target_pairs={{0,16},{8,24},{16,32},{24,40},{32,48},{40,56},{48,64},{56,72},{64,... | collective-permute-start | bytes 442376 | tf_op jit(solution)/shard_map/ppermute | solution.py:547
  12.8 14.3 %collective-permute-start.4 = (bf16[2,144,256]{2,1,0:T(8,128)(2,1)S(1)}, bf16[2,144,256]{2,1,0:T(8,128)(2,1)S(1)}, u32[]{:S(2)}, u32[]{:S(2)}) collective-permute-start(bf16[2,144,256]{2,1,0:T(8,128)(2,1)S(1)} %get-tuple-element.25), channel_id=1, source_target_pairs={{0,24},{8,32},{16,40},{24,48},{32,56},{40,64},{48,72},{56,80},{64,... | collective-permute-start | bytes 442376 | tf_op jit(solution)/shard_map/ppermute | solution.py:550
  17.3 9.8 %collective-permute-start.1 = (bf16[144,256]{1,0:T(8,128)(2,1)S(1)}, bf16[144,256]{1,0:T(8,128)(2,1)S(1)}, u32[]{:S(2)}, u32[]{:S(2)}) collective-permute-start(bf16[144,256]{1,0:T(8,128)(2,1)S(1)} %get-tuple-element.22), channel_id=1, source_target_pairs={{16,0},{24,8},{32,16},{40,24},{48,32},{56,40},{64,48},{72,56},{80,... | collective-permute-start | bytes 221192 | tf_op jit(solution)/shard_map/ppermute | solution.py:546
  19.4 1.6 %copy-start = (bf16[1,256,4096]{2,1,0:T(8,128)(2,1)S(1)}, bf16[1,256,4096]{2,1,0:T(8,128)(2,1)}, u32[]{:S(2)}) copy-start(bf16[1,256,4096]{2,1,0:T(8,128)(2,1)} %param.9) | copy-start | bytes 6291460
  20.9 1.0 copy-start.3
  21.9 5.3 %copy-start.7 = (s32[2,3]{1,0:T(2,128)S(1)}, s32[2,3]{1,0:T(2,128)}, u32[]{:S(2)}) copy-start(s32[2,3]{1,0:T(2,128)} %triples.13) | copy-start | bytes 76
  32.9 9.4 %collective-permute-start.5 = (bf16[2,16,256,128]{3,2,1,0:T(8,128)(2,1)S(1)}, bf16[2,16,256,128]{3,2,1,0:T(8,128)(2,1)S(1)}, u32[]{:S(2)}, u32[]{:S(2)}) collective-permute-start(bf16[2,16,256,128]{3,2,1,0:T(8,128)(2,1)S(1)} %terms.3), channel_id=1, source_target_pairs={{0,1},{1,0},{2,3},{3,2},{4,5},{5,4},{6,7},{7,6},{8,9},{9,8},{10,11... | collective-permute-start | bytes 6291464 | tf_op jit(solution)/shard_map/ppermute | solution.py:558
  43.9 5.0 %copy-start.9 = (bf16[1,3,4096]{2,1,0:T(4,128)(2,1)S(1)}, bf16[1,3,4096]{2,1,0:T(4,128)(2,1)}, u32[]{:S(2)}) copy-start(bf16[1,3,4096]{2,1,0:T(4,128)(2,1)} %param.13) | copy-start | bytes 73732
  43.9 5.1 %copy-start.10 = (bf16[1,64]{1,0:T(2,128)(2,1)S(1)}, bf16[1,64]{1,0:T(2,128)(2,1)}, u32[]{:S(2)}) copy-start(bf16[1,64]{1,0:T(2,128)(2,1)} %param.14) | copy-start | bytes 388
  43.9 19.3 %all-to-all-start = ((bf16[16,256,128]{2,1,0:T(8,128)(2,1)}), bf16[16,256,128]{2,1,0:T(8,128)(2,1)S(1)}, u32[]{:S(2)}, u32[]{:S(2)}) async-start(bf16[16,256,128]{2,1,0:T(8,128)(2,1)} %get-tuple-element.26), calls=%async_computation | async-start | bytes 2097152 | tf_op jit(solution)/shard_map/all_to_all | solution.py:569
  49.0 24.3 %collective-permute-start.9 = (bf16[4,256,128]{2,1,0:T(8,128)(2,1)S(1)}, bf16[4,256,128]{2,1,0:T(8,128)(2,1)S(1)}, u32[]{:S(2)}, u32[]{:S(2)}) collective-permute-start(bf16[4,256,128]{2,1,0:T(8,128)(2,1)S(1)} %get-tuple-element.28), channel_id=1, source_target_pairs={{8,0},{16,8},{24,16},{32,24},{40,32},{48,40},{56,48},{64,56},{72,6... | collective-permute-start | bytes 786440 | tf_op jit(solution)/shard_map/ppermute | solution.py:571
  53.0 24.8 %collective-permute-start.10 = (bf16[4,256,128]{2,1,0:T(8,128)(2,1)S(1)}, bf16[4,256,128]{2,1,0:T(8,128)(2,1)S(1)}, u32[]{:S(2)}, u32[]{:S(2)}) collective-permute-start(bf16[4,256,128]{2,1,0:T(8,128)(2,1)S(1)} %get-tuple-element.29), channel_id=1, source_target_pairs={{16,0},{24,8},{32,16},{40,24},{48,32},{56,40},{64,48},{72,56},{80,... | collective-permute-start | bytes 786440 | tf_op jit(solution)/shard_map/ppermute | solution.py:571
  58.7 19.2 %collective-permute-start.11 = (bf16[4,256,128]{2,1,0:T(8,128)(2,1)S(1)}, bf16[4,256,128]{2,1,0:T(8,128)(2,1)S(1)}, u32[]{:S(2)}, u32[]{:S(2)}) collective-permute-start(bf16[4,256,128]{2,1,0:T(8,128)(2,1)S(1)} %get-tuple-element.30), channel_id=1, source_target_pairs={{24,0},{32,8},{40,16},{48,24},{56,32},{64,40},{72,48},{80,56},{88,... | collective-permute-start | bytes 786440 | tf_op jit(solution)/shard_map/ppermute | solution.py:571
  63.7 21.2 %collective-permute-start.6 = (bf16[368,128]{1,0:T(8,128)(2,1)S(1)}, bf16[368,128]{1,0:T(8,128)(2,1)S(1)}, u32[]{:S(2)}, u32[]{:S(2)}) collective-permute-start(bf16[368,128]{1,0:T(8,128)(2,1)S(1)} %get-tuple-element.44), channel_id=1, source_target_pairs={{8,0},{16,8},{24,16},{32,24},{40,32},{48,40},{56,48},{64,56},{72,6... | collective-permute-start | bytes 282632 | tf_op jit(solution)/shard_map/ppermute | solution.py:582
  67.6 17.3 %collective-permute-start.7 = (bf16[368,128]{1,0:T(8,128)(2,1)S(1)}, bf16[368,128]{1,0:T(8,128)(2,1)S(1)}, u32[]{:S(2)}, u32[]{:S(2)}) collective-permute-start(bf16[368,128]{1,0:T(8,128)(2,1)S(1)} %get-tuple-element.43), channel_id=1, source_target_pairs={{16,0},{24,8},{32,16},{40,24},{48,32},{56,40},{64,48},{72,56},{80,... | collective-permute-start | bytes 282632 | tf_op jit(solution)/shard_map/ppermute | solution.py:582
  73.3 11.7 %collective-permute-start.8 = (bf16[368,128]{1,0:T(8,128)(2,1)S(1)}, bf16[368,128]{1,0:T(8,128)(2,1)S(1)}, u32[]{:S(2)}, u32[]{:S(2)}) collective-permute-start(bf16[368,128]{1,0:T(8,128)(2,1)S(1)} %get-tuple-element.42), channel_id=1, source_target_pairs={{24,0},{32,8},{40,16},{48,24},{56,32},{64,40},{72,48},{80,56},{88,... | collective-permute-start | bytes 282632 | tf_op jit(solution)/shard_map/ppermute | solution.py:582
  77.9 17.8 %copy-start.8 = (f32[64]{0:T(128)S(1)}, f32[64]{0:T(128)}, u32[]{:S(2)}) copy-start(f32[64]{0:T(128)} %param.16) | copy-start | bytes 772
  81.5 8.9 %all-to-all-start.1 = ((bf16[4,256,128]{2,1,0:T(8,128)(2,1)}), bf16[4,256,128]{2,1,0:T(8,128)(2,1)S(1)}, u32[]{:S(2)}, u32[]{:S(2)}) async-start(bf16[4,256,128]{2,1,0:T(8,128)(2,1)} %combine.1), calls=%async_computation.1 | async-start | bytes 524288 | tf_op jit(solution)/shard_map/all_to_all | solution.py:585
  92.1 10.6 %all-to-all-start.2 = ((bf16[4,512,128]{2,1,0:T(8,128)(2,1)}), bf16[4,512,128]{2,1,0:T(8,128)(2,1)S(1)}, u32[]{:S(2)}, u32[]{:S(2)}) async-start(bf16[4,512,128]{2,1,0:T(8,128)(2,1)} %finish.1), calls=%async_computation.2 | async-start | bytes 1048576 | tf_op jit(solution)/shard_map/all_to_all | solution.py:588
  101.8 1.0 copy-start.1
  102.8 1.2 %copy-start.2 = (f32[2048,128]{1,0:T(8,128)S(1)}, f32[2048,128]{1,0:T(8,128)}, u32[]{:S(2)}) copy-start(f32[2048,128]{1,0:T(8,128)} %copy-done.1) | copy-start | bytes 3145732
  109.5 6.7 %collective-permute-start.12 = (f32[1,64]{1,0:T(1,128)S(1)}, f32[1,64]{1,0:T(1,128)S(1)}, u32[]{:S(2)}, u32[]{:S(2)}) collective-permute-start(f32[1,64]{1,0:T(1,128)S(1)} %energy.1), channel_id=1, source_target_pairs={{0,1},{1,0},{2,3},{3,2},{4,5},{5,4},{6,7},{7,6},{8,9},{9,8},{10,11... | collective-permute-start | bytes 776 | tf_op jit(solution)/shard_map/ppermute | solution.py:592

commit v4 on v3

--- a/solution.py
+++ b/solution.py
@@ -24,6 +24,10 @@
 CORE_ROUTE = [(i, i ^ 1) for i in range(8)]
 
 
+def in_hbm(array):
+    return pltpu.with_memory_space_constraint(array, pltpu.HBM)
+
+
 def lane_low(rows):
     return lax.broadcasted_iota(jnp.int32, (rows, 2 * T), 1) < T
 
@@ -48,15 +52,7 @@
     return off_i, off_j, live
 
 
-def prep_kernel(triples, amps_in, coulomb_in, out1, out2, out3, up1, up2, blocks, amps, coulomb, sems):
-    copies = [
-        pltpu.make_async_copy(amps_in, amps, sems.at[0]),
-        pltpu.make_async_copy(coulomb_in, coulomb, sems.at[1]),
-    ]
-    for copy in copies:
-        copy.start()
-    for copy in copies:
-        copy.wait()
+def prep_kernel(triples, amps, coulomb, out1, out2, out3, up1, up2, blocks):
     owner, core = lax.axis_index("trip"), lax.rem(lax.axis_index("virt"), 2)
     occ_rows = coulomb.shape[1]
     for s in range(3):
@@ -90,76 +86,77 @@
     return pl.pallas_call(
         prep_kernel,
         out_shape=(two, two, two, two, one),
-        in_specs=[
-            pl.BlockSpec(memory_space=pltpu.SMEM),
-            pl.BlockSpec(memory_space=pltpu.HBM),
-            pl.BlockSpec(memory_space=pltpu.HBM),
-        ],
+        in_specs=[pl.BlockSpec(memory_space=pltpu.SMEM), pl.BlockSpec(), pl.BlockSpec()],
         out_specs=[vmem] * 5,
         scratch_shapes=[
             pltpu.VMEM((3, BLOCK_ROWS, 4 * T), BF16),
-            pltpu.VMEM(amps.shape, BF16),
-            pltpu.VMEM(coulomb.shape, BF16),
-            pltpu.SemaphoreType.DMA((2,)),
         ],
         compiler_params=pltpu.CompilerParams(vmem_limit_bytes=VMEM_LIMIT),
         name="prep",
-    )(triples, amps, coulomb)
+    )(triples, in_hbm(amps), in_hbm(coulomb))
 
 
 STEPS = 8
 DEPTH = 6 * T
-
-
-def panels_kernel(integrals, holes, out, spread_a, spread_b):
+PITCH = 2 * T + 8
+WHOLE_PITCH = T + 8
+FLIP_PITCH = H + 8
+
+
+def panels_kernel(integrals_in, holes, out, spread_a, spread_b, integrals, sems):
     occ_rows = holes.shape[0]
-    step = pl.program_id(0)
     per_step = H // STEPS
-
-    for inner in range(per_step):
-        chunk = step * per_step + inner
-        columns = slice(inner * 2 * T, (inner + 1) * 2 * T)
-        turned = integrals[:, columns].astype(F32).T
-        hole = holes[:, columns].astype(F32)
+    width = per_step * 2 * T
+    copies = []
+    for step in range(STEPS):
+        span = pl.ds(step * width, width)
+        copies.append(
+            pltpu.make_async_copy(integrals_in.at[:, span], integrals.at[:, span], sems.at[step])
+        )
+    for copy in copies:
+        copy.start()
+    for step in range(STEPS):
+        copies[step].wait()
+        for chunk in range(step * per_step, (step + 1) * per_step):
+            columns = slice(chunk * 2 * T, (chunk + 1) * 2 * T)
+            turned = integrals[:, columns].astype(F32).T
+            for part in range(4):
+                at = pl.ds((part % 2) * T + chunk * 2 + part // 2, H, stride=PITCH)
+                spread_a[at, :] = turned[part * H : (part + 1) * H, : 2 * T]
+                spread_b[at, :] = turned[part * H : (part + 1) * H, 2 * T :]
+    for chunk in range(H):
+        hole = holes[:, chunk * 2 * T : (chunk + 1) * 2 * T].astype(F32)
         hole = jnp.concatenate([hole, jnp.zeros((2 * T - occ_rows, 2 * T), F32)], axis=0).T
-        for part in range(4):
-            at = pl.ds((part % 2) * T + chunk * 2 + part // 2, H, stride=2 * T)
-            spread_a[at, :] = turned[part * H : (part + 1) * H, : 2 * T]
-            spread_b[at, :] = turned[part * H : (part + 1) * H, 2 * T :]
         for w in range(2):
             third = chunk * 2 + w
-            at = lax.rem(third, H) * 2 * T + (third // H) * T
-            rows = pl.ds(pl.multiple_of(at, T), T)
-            out[rows, 4 * T :] = hole[w * T : (w + 1) * T].astype(BF16)
-
-    @pl.when(step == STEPS - 1)
-    def _():
-        def settle(step, _):
-            rows = pl.ds(pl.multiple_of(step * 2 * T, 2 * T), 2 * T)
-            out[rows, : 2 * T] = spread_a[rows, :].astype(BF16)
-            out[rows, 2 * T : 4 * T] = spread_b[rows, :].astype(BF16)
-            return 0
-
-        lax.fori_loop(0, H, settle, 0, unroll=2)
+            at = third % H * 2 * T + third // H * T
+            out[at : at + T, 4 * T :] = hole[w * T : (w + 1) * T].astype(BF16)
+
+    def settle(step, _):
+        rows = pl.ds(pl.multiple_of(step * 2 * T, 2 * T), 2 * T)
+        source = pl.ds(pl.multiple_of(step * PITCH, 8), 2 * T)
+        out[rows, : 2 * T] = spread_a[source, :].astype(BF16)
+        out[rows, 2 * T : 4 * T] = spread_b[source, :].astype(BF16)
+        return 0
+
+    lax.fori_loop(0, H, settle, 0, unroll=32)
 
 
 def panels_of(integrals, holes):
-    vmem = pl.BlockSpec(memory_space=pltpu.VMEM)
-    columns = T * T // STEPS
     return pl.pallas_call(
         panels_kernel,
-        grid=(STEPS,),
         out_shape=jax.ShapeDtypeStruct((T * T, DEPTH), BF16),
-        in_specs=[
-            pl.BlockSpec((4 * T, columns), lambda step: (0, step)),
-            pl.BlockSpec((holes.shape[0], columns), lambda step: (0, step)),
+        in_specs=[pl.BlockSpec(memory_space=pltpu.HBM), pl.BlockSpec()],
+        out_specs=pl.BlockSpec(memory_space=pltpu.VMEM),
+        scratch_shapes=[pltpu.VMEM((H * PITCH, 2 * T), F32)] * 2
+        + [
+            pltpu.VMEM(integrals.shape, BF16),
+            pltpu.SemaphoreType.DMA((STEPS,)),
         ],
-        out_specs=vmem,
-        scratch_shapes=[pltpu.VMEM((T * T, 2 * T), F32)] * 2,
         compiler_params=pltpu.CompilerParams(vmem_limit_bytes=VMEM_LIMIT),
         cost_estimate=pl.CostEstimate(flops=1 << 28, bytes_accessed=5 << 20, transcendentals=0),
         name="panels",
-    )(integrals, holes)
+    )(in_hbm(integrals), in_hbm(holes))
 
 
 def terms_kernel(rel, triples, got_one, got_two, in1, in2, in3, panels, out, chosen):
@@ -188,13 +185,13 @@
         lead.append(jnp.concatenate([block[:T], coulomb], axis=1))
         second.append(jnp.concatenate([block[T : 2 * T], coulomb], axis=1))
     lead = jnp.concatenate(lead, axis=0)
-    second = jnp.concatenate(second, axis=0)
+    second = jnp.concatenate(second, axis=0).astype(F32).T.astype(BF16)
     low = lane_low(T)
     contract = (((1,), (1,)), ((), ()))
 
     def group(step, _):
         panel = panels[pl.ds(pl.multiple_of(step * 8 * T, 8 * T), 8 * T), :]
-        by_rows = lax.dot_general(panel, second, contract, preferred_element_type=F32)
+        by_rows = jnp.dot(panel, second, preferred_element_type=F32)
         by_cols = lax.dot_general(lead, panel, contract, preferred_element_type=F32)
 
         def tiles_of(pair, duo):
@@ -228,7 +225,7 @@
                             out[half, index, at, :] = rows16
         return 0
 
-    lax.fori_loop(0, 8, group, 0)
+    lax.fori_loop(0, 8, group, 0, unroll=8)
 
 
 def terms(rel, triples, blocks, panels):
@@ -256,7 +253,7 @@
                 out[index] = total.astype(BF16)
                 return 0
 
-            lax.fori_loop(0, per_out, one, 0)
+            lax.fori_loop(0, per_out, one, 0, unroll=4)
 
 
 def add(keep, got):
@@ -358,9 +355,10 @@
         for q in range(4):
             first = parts[quarter, q * T : (q + 1) * T, :].astype(F32)
             second = parts[quarter, 256 + q * T : 256 + (q + 1) * T, :].astype(F32)
-            at = (quarter * 8 + 2 * q) * T
+            at = (quarter * 8 + 2 * q) * WHOLE_PITCH
             whole[at : at + T, :] = jnp.where(low, first, swap_halves(second))
-            whole[at + T : at + 2 * T, :] = jnp.where(low, swap_halves(first), second)
+            at += WHOLE_PITCH
+            whole[at : at + T, :] = jnp.where(low, swap_halves(first), second)
 
     low32 = lax.broadcasted_iota(jnp.int32, (H, 2 * T), 1) % T < H
     low_half = lane_low(H)
@@ -368,7 +366,7 @@
     def flip(step, _):
         b = step * 4
         across = jnp.concatenate(
-            [whole[pl.ds(b + at, H, stride=T), :] for at in range(4)], axis=0
+            [whole[pl.ds(b + at, H, stride=WHOLE_PITCH), :] for at in range(4)], axis=0
         ).T
         first = [across[at * H : (at + 1) * H] for at in (0, 2, 1, 3)]
         mid = [None] * 4
@@ -382,21 +380,21 @@
                 (0, jnp.where(low32, x, pltpu.roll(z, H, 1))),
                 (1, jnp.where(low32, pltpu.roll(x, 3 * H, 1), z)),
             ):
-                rows = pl.ds(pl.multiple_of((b + at + inner) * H, H), H)
+                rows = pl.ds(pl.multiple_of((b + at + inner) * FLIP_PITCH, 8), H)
                 flipped[rows, :] = value
         return 0
 
-    lax.fori_loop(0, T // 4, flip, 0, unroll=2)
+    lax.fori_loop(0, T // 4, flip, 0, unroll=8)
     acc[...] = jnp.zeros_like(acc)
 
     def pair(bp, _):
-        from_flipped = pack_rows(flipped[pl.ds(bp, T, stride=H), :])
-        from_whole = pack_rows(whole[pl.ds(pl.multiple_of(bp * T, T), T), :])
+        from_flipped = pack_rows(flipped[pl.ds(bp, T, stride=FLIP_PITCH), :])
+        from_whole = pack_rows(whole[pl.ds(pl.multiple_of(bp * WHOLE_PITCH, 8), T), :])
         for half in range(2):
             b = bp + H * half
             at = pl.ds(pl.multiple_of(b * H, H), H)
-            plain = whole[pl.ds(b, H, stride=T), :]
-            turned = flipped[at, :]
+            plain = whole[pl.ds(b, H, stride=WHOLE_PITCH), :]
+            turned = flipped[pl.ds(pl.multiple_of(b * FLIP_PITCH, 8), H), :]
             inv = inverse[at, :]
             first = (4.0 * plain + from_flipped[half]) * (plain - turned + extra_a[at, :]) * inv
             second = plain * (from_flipped[half] - from_whole[half] + extra_b[at, :]) * inv
@@ -404,7 +402,7 @@
             rows_b[pl.ds(b, 1), :] = jnp.sum(second, axis=0, keepdims=True)
         return 0
 
-    lax.fori_loop(0, H, pair, 0, unroll=2)
+    lax.fori_loop(0, H, pair, 0, unroll=8)
     by_a = jnp.sum(acc[...], axis=0, keepdims=True)
     by_a = by_a[:, :T] + by_a[:, T:]
     by_b = jnp.sum(rows_b[...].T, axis=0, keepdims=True)
@@ -419,8 +417,8 @@
         in_specs=[pl.BlockSpec(memory_space=pltpu.SMEM)] + [vmem] * 4,
         out_specs=vmem,
         scratch_shapes=[
-            pltpu.VMEM((H * T, 2 * T), F32),
-            pltpu.VMEM((H * T, 2 * T), F32),
+            pltpu.VMEM((H * WHOLE_PITCH, 2 * T), F32),
+            pltpu.VMEM((T * FLIP_PITCH, 2 * T), F32),
             pltpu.VMEM((H, 2 * T), F32),
             pltpu.VMEM((T, 2 * T), F32),
         ],
@@ -505,7 +503,7 @@
         inverse[at, :] = 1.0 / (base - e_b)
         return 0
 
-    lax.fori_loop(0, T, one_b, 0, unroll=2)
+    lax.fori_loop(0, T, one_b, 0, unroll=8)
 
 
 def tables(triples, small, virt_energy):

time: 118 us -> 107 us (0.907)
  the two profiles are of different devices: /device:TPU:389 before, /device:TPU:227 now
where the time goes in v4:
time: 107 us; the launch traced here: 106 us
  starting transfers between devices  61 us (57%)
  Pallas kernels  24.5 us (23%)
  waiting for transfers between devices  15.9 us (15%)
  local copies, waits for them, and re-layouts  3.04 us (3%)
    ppermute x3, starting transfers between devices, local(): lax.ppermute(to_share[d - 1], 'trip', shift_route(n_trip, -d))  9.78 us
    ppermute x3, starting transfers between devices, local(): lax.ppermute(second_half[d], 'trip', shift_route(n_trip, -d))  9.78 us
    ppermute x1, starting transfers between devices, local(): other = lax.ppermute(mine, 'virt', CORE_ROUTE)  7.78 us
    ppermute x1, starting transfers between devices, local(): in2 = lax.ppermute(out2, 'trip', shift_route(n_trip, 2))  7.07 us
    pallas_call x2, Pallas kernels, terms(): pl.pallas_call(functools.partial(terms_kernel, rel), out_shape=jax.ShapeD...  6.54 us
    all_to_all x1, waiting for transfers between devices, local(): second_sums = over_y(combine(triples, second_half[0], *by_owner))  5.49 us
    all_to_all x1, starting transfers between devices, local(): by_y = over_y(first_half)  4.31 us
    ppermute x1, starting transfers between devices, local(): got = lax.ppermute(send, 'virt', CORE_ROUTE)  4.22 us
  transfers between devices with their start and end apart: 16, of which 7 were waited for; matrix products, arithmetic and copies ran while one was open for 1% of the time, Pallas kernels for 13%

profile of v4, /device:TPU:227, one launch (start us, length us, event | category | flops | bytes accessed | tf_op | source)
XLA Modules:
  0.0 106.4 jit_solution(18170814196219995051)
XLA Ops:
  0.0 0.0 copy-start.2
  0.0 0.7 copy-done.2
  0.7 1.2 %prep.1 = (bf16[2,144,256]{2,1,0:T(8,128)(2,1)S(1)}, bf16[2,144,256]{2,1,0:T(8,128)(2,1)S(1)}, bf16[2,144,256]{2,1,0:T(8,128)(2,1)S(1)}, bf16[2,144,256]{2,1,0:T(8,128)(2,1)S(1)}, bf16[144,256]{1,0:T(8,128)(2,1)S(1)}) custom-call(s32[2,3]{1,0:T(2,128)S(1)} %copy-done.2, bf16[3,128,256]{2,1,0:T(8,128)(2,1)} %bitcast.28, bf16[3,38,64]{2,1,0:T(8,128)(2,1)} %bitcast.29), custom_call_target="tpu_custom_call" | custom-call | tf_op jit(solution)/shard_map/prep/pallas_call | solution.py:86
  1.9 2.2 %collective-permute-start = (bf16[2,144,256]{2,1,0:T(8,128)(2,1)S(1)}, bf16[2,144,256]{2,1,0:T(8,128)(2,1)S(1)}, u32[]{:S(2)}, u32[]{:S(2)}) collective-permute-start(bf16[2,144,256]{2,1,0:T(8,128)(2,1)S(1)} %get-tuple-element.21), channel_id=1, source_target_pairs={{8,0},{16,8},{24,16},{32,24},{40,32},{48,40},{56,48},{64,56},{72,6... | collective-permute-start | bytes 442376 | tf_op jit(solution)/shard_map/ppermute | solution.py:546
  4.0 3.1 %collective-permute-start.2 = (bf16[2,144,256]{2,1,0:T(8,128)(2,1)S(1)}, bf16[2,144,256]{2,1,0:T(8,128)(2,1)S(1)}, u32[]{:S(2)}, u32[]{:S(2)}) collective-permute-start(bf16[2,144,256]{2,1,0:T(8,128)(2,1)S(1)} %get-tuple-element.23), channel_id=1, source_target_pairs={{0,8},{8,16},{16,24},{24,32},{32,40},{40,48},{48,56},{56,64},{64,7... | collective-permute-start | bytes 442376 | tf_op jit(solution)/shard_map/ppermute | solution.py:547
  7.2 7.1 %collective-permute-start.3 = (bf16[2,144,256]{2,1,0:T(8,128)(2,1)S(1)}, bf16[2,144,256]{2,1,0:T(8,128)(2,1)S(1)}, u32[]{:S(2)}, u32[]{:S(2)}) collective-permute-start(bf16[2,144,256]{2,1,0:T(8,128)(2,1)S(1)} %get-tuple-element.24), channel_id=1, source_target_pairs={{0,16},{8,24},{16,32},{24,40},{32,48},{40,56},{48,64},{56,72},{64,... | collective-permute-start | bytes 442376 | tf_op jit(solution)/shard_map/ppermute | solution.py:545
  14.2 2.3 %collective-permute-start.4 = (bf16[2,144,256]{2,1,0:T(8,128)(2,1)S(1)}, bf16[2,144,256]{2,1,0:T(8,128)(2,1)S(1)}, u32[]{:S(2)}, u32[]{:S(2)}) collective-permute-start(bf16[2,144,256]{2,1,0:T(8,128)(2,1)S(1)} %get-tuple-element.25), channel_id=1, source_target_pairs={{0,24},{8,32},{16,40},{24,48},{32,56},{40,64},{48,72},{56,80},{64,... | collective-permute-start | bytes 442376 | tf_op jit(solution)/shard_map/ppermute | solution.py:548
  16.6 3.0 %collective-permute-start.1 = (bf16[144,256]{1,0:T(8,128)(2,1)S(1)}, bf16[144,256]{1,0:T(8,128)(2,1)S(1)}, u32[]{:S(2)}, u32[]{:S(2)}) collective-permute-start(bf16[144,256]{1,0:T(8,128)(2,1)S(1)} %get-tuple-element.22), channel_id=1, source_target_pairs={{16,0},{24,8},{32,16},{40,24},{48,32},{56,40},{64,48},{72,56},{80,... | collective-permute-start | bytes 221192 | tf_op jit(solution)/shard_map/ppermute | solution.py:544
  19.6 3.8 %panels.1 = bf16[4096,384]{1,0:T(8,128)(2,1)S(1)} custom-call(bf16[256,4096]{1,0:T(8,128)(2,1)} %bitcast.22, bf16[38,4096]{1,0:T(8,128)(2,1)} %bitcast.23), custom_call_target="tpu_custom_call" | custom-call | flops 268435456 | bytes 5242880 | tf_op jit(solution)/shard_map/panels/pallas_call | solution.py:146
  23.3 0.5 collective-permute-done.1.got_two
  23.8 0.0 collective-permute-done.got_one
  23.8 0.0 collective-permute-done.2.in1
  23.8 0.0 collective-permute-done.3.in2
  23.8 0.0 collective-permute-done.4.in3
  23.8 3.3 %terms.3 = bf16[2,16,256,128]{3,2,1,0:T(8,128)(2,1)S(1)} custom-call(s32[2,3]{1,0:T(2,128)S(1)} %copy-done.2, bf16[2,144,256]{2,1,0:T(8,128)(2,1)S(1)} %collective-permute-done.got_one, bf16[144,256]{1,0:T(8,128)(2,1)S(1)} %collective-permute-done.1.got_two, bf16[2,144,256]{2,1,0:T(8,128)(2,1)S(1)} %collective-permute-done.2.in1, ...), custom_call_target="tpu_custom_call" | custom-call | flops 2147483648 | bytes 5242880 | tf_op jit(solution)/shard_map/terms/pallas_call | solution.py:233
  27.1 4.2 %collective-permute-start.5 = (bf16[2,16,256,128]{3,2,1,0:T(8,128)(2,1)S(1)}, bf16[2,16,256,128]{3,2,1,0:T(8,128)(2,1)S(1)}, u32[]{:S(2)}, u32[]{:S(2)}) collective-permute-start(bf16[2,16,256,128]{3,2,1,0:T(8,128)(2,1)S(1)} %terms.3), channel_id=1, source_target_pairs={{0,1},{1,0},{2,3},{3,2},{4,5},{5,4},{6,7},{7,6},{8,9},{9,8},{10,11... | collective-permute-start | bytes 6291464 | tf_op jit(solution)/shard_map/ppermute | solution.py:556
  31.3 3.3 %terms.2.keep = bf16[2,16,256,128]{3,2,1,0:T(8,128)(2,1)S(1)} custom-call(s32[2,3]{1,0:T(2,128)S(1)} %copy-done.2, bf16[2,144,256]{2,1,0:T(8,128)(2,1)S(1)} %collective-permute-done.got_one, bf16[144,256]{1,0:T(8,128)(2,1)S(1)} %collective-permute-done.1.got_two, bf16[2,144,256]{2,1,0:T(8,128)(2,1)S(1)} %collective-permute-done.2.in1, ...), custom_call_target="tpu_custom_call" | custom-call | flops 2147483648 | bytes 5242880 | tf_op jit(solution)/shard_map/terms/pallas_call | solution.py:233
  34.6 0.5 collective-permute-done.5.got
  35.1 1.4 %add.27 = (bf16[16,256,128]{2,1,0:T(8,128)(2,1)}, bf16[4,256,128]{2,1,0:T(8,128)(2,1)S(1)}, bf16[4,256,128]{2,1,0:T(8,128)(2,1)S(1)}, bf16[4,256,128]{2,1,0:T(8,128)(2,1)S(1)}, bf16[4,256,128]{2,1,0:T(8,128)(2,1)S(1)}) custom-call(bf16[2,16,256,128]{3,2,1,0:T(8,128)(2,1)S(1)} %terms.2.keep, bf16[2,16,256,128]{3,2,1,0:T(8,128)(2,1)S(1)} %collective-permute-done.5.got), custom_call_target="tpu_custom_call" | custom-call | tf_op jit(solution)/shard_map/add/pallas_call | solution.py:263
  36.5 0.0 copy-start.5
  36.5 0.0 copy-start.6
  36.5 4.3 %all-to-all-start = ((bf16[16,256,128]{2,1,0:T(8,128)(2,1)}), bf16[16,256,128]{2,1,0:T(8,128)(2,1)S(1)}, u32[]{:S(2)}, u32[]{:S(2)}) async-start(bf16[16,256,128]{2,1,0:T(8,128)(2,1)} %get-tuple-element.26), calls=%async_computation | async-start | bytes 2097152 | tf_op jit(solution)/shard_map/all_to_all | solution.py:567
  41.5 0.0 copy-done.5
  41.5 0.1 reshape.44
  41.6 0.0 copy-done.6
  41.6 3.9 %collective-permute-start.9 = (bf16[4,256,128]{2,1,0:T(8,128)(2,1)S(1)}, bf16[4,256,128]{2,1,0:T(8,128)(2,1)S(1)}, u32[]{:S(2)}, u32[]{:S(2)}) collective-permute-start(bf16[4,256,128]{2,1,0:T(8,128)(2,1)S(1)} %get-tuple-element.28), channel_id=1, source_target_pairs={{8,0},{16,8},{24,16},{32,24},{40,32},{48,40},{56,48},{64,56},{72,6... | collective-permute-start | bytes 786440 | tf_op jit(solution)/shard_map/ppermute | solution.py:569
  45.5 4.0 %collective-permute-start.10 = (bf16[4,256,128]{2,1,0:T(8,128)(2,1)S(1)}, bf16[4,256,128]{2,1,0:T(8,128)(2,1)S(1)}, u32[]{:S(2)}, u32[]{:S(2)}) collective-permute-start(bf16[4,256,128]{2,1,0:T(8,128)(2,1)S(1)} %get-tuple-element.29), channel_id=1, source_target_pairs={{16,0},{24,8},{32,16},{40,24},{48,32},{56,40},{64,48},{72,56},{80,... | collective-permute-start | bytes 786440 | tf_op jit(solution)/shard_map/ppermute | solution.py:569
  49.5 1.9 %collective-permute-start.11 = (bf16[4,256,128]{2,1,0:T(8,128)(2,1)S(1)}, bf16[4,256,128]{2,1,0:T(8,128)(2,1)S(1)}, u32[]{:S(2)}, u32[]{:S(2)}) collective-permute-start(bf16[4,256,128]{2,1,0:T(8,128)(2,1)S(1)} %get-tuple-element.30), channel_id=1, source_target_pairs={{24,0},{32,8},{40,16},{48,24},{56,32},{64,40},{72,48},{80,56},{88,... | collective-permute-start | bytes 786440 | tf_op jit(solution)/shard_map/ppermute | solution.py:569
  51.4 3.9 %all-to-all-done = bf16[16,256,128]{2,1,0:T(8,128)(2,1)S(1)} async-done(((bf16[16,256,128]{2,1,0:T(8,128)(2,1)}), bf16[16,256,128]{2,1,0:T(8,128)(2,1)S(1)}, u32[]{:S(2)}, u32[]{:S(2)}) %all-to-all-start) | async-done | bytes 1048608 | tf_op jit(solution)/shard_map/all_to_all | solution.py:567
  55.3 0.2 convert_element_type.16
  55.5 0.0 copy-start.3
  55.5 0.1 fusion
  55.7 0.1 pad_maximum_fusion
  55.8 3.9 %collective-permute-start.6 = (bf16[368,128]{1,0:T(8,128)(2,1)S(1)}, bf16[368,128]{1,0:T(8,128)(2,1)S(1)}, u32[]{:S(2)}, u32[]{:S(2)}) collective-permute-start(bf16[368,128]{1,0:T(8,128)(2,1)S(1)} %get-tuple-element.44), channel_id=1, source_target_pairs={{8,0},{16,8},{24,16},{32,24},{40,32},{48,40},{56,48},{64,56},{72,6... | collective-permute-start | bytes 282632 | tf_op jit(solution)/shard_map/ppermute | solution.py:580
  59.7 4.0 %collective-permute-start.7 = (bf16[368,128]{1,0:T(8,128)(2,1)S(1)}, bf16[368,128]{1,0:T(8,128)(2,1)S(1)}, u32[]{:S(2)}, u32[]{:S(2)}) collective-permute-start(bf16[368,128]{1,0:T(8,128)(2,1)S(1)} %get-tuple-element.43), channel_id=1, source_target_pairs={{16,0},{24,8},{32,16},{40,24},{48,32},{56,40},{64,48},{72,56},{80,... | collective-permute-start | bytes 282632 | tf_op jit(solution)/shard_map/ppermute | solution.py:580
  63.7 0.0 collective-permute-done.9.one
  63.7 1.9 %collective-permute-start.8 = (bf16[368,128]{1,0:T(8,128)(2,1)S(1)}, bf16[368,128]{1,0:T(8,128)(2,1)S(1)}, u32[]{:S(2)}, u32[]{:S(2)}) collective-permute-start(bf16[368,128]{1,0:T(8,128)(2,1)S(1)} %get-tuple-element.42), channel_id=1, source_target_pairs={{24,0},{32,8},{40,16},{48,24},{56,32},{64,40},{72,48},{80,56},{88,... | collective-permute-start | bytes 282632 | tf_op jit(solution)/shard_map/ppermute | solution.py:580
  65.6 0.0 collective-permute-done.10.two
  65.6 1.6 %collective-permute-done.11.three = bf16[4,256,128]{2,1,0:T(8,128)(2,1)S(1)} collective-permute-done((bf16[4,256,128]{2,1,0:T(8,128)(2,1)S(1)}, bf16[4,256,128]{2,1,0:T(8,128)(2,1)S(1)}, u32[]{:S(2)}, u32[]{:S(2)}) %collective-permute-start.11) | collective-permute-done | bytes 262176 | tf_op jit(solution)/shard_map/ppermute | solution.py:569
  67.2 0.0 copy-done.3
  67.2 0.0 copy-start.4
  67.2 3.6 %combine.1 = bf16[4,256,128]{2,1,0:T(8,128)(2,1)} custom-call(s32[2,3]{1,0:T(2,128)S(1)} %copy-done.3, bf16[4,256,128]{2,1,0:T(8,128)(2,1)S(1)} %get-tuple-element.27.own, bf16[4,256,128]{2,1,0:T(8,128)(2,1)S(1)} %collective-permute-done.9.one, bf16[4,256,128]{2,1,0:T(8,128)(2,1)S(1)} %collective-permute-done.10.two, ...), custom_call_target="tpu_custom_call" | custom-call | tf_op jit(solution)/shard_map/combine/pallas_call | solution.py:315
  70.8 4.0 %all-to-all-start.1 = ((bf16[4,256,128]{2,1,0:T(8,128)(2,1)}), bf16[4,256,128]{2,1,0:T(8,128)(2,1)S(1)}, u32[]{:S(2)}, u32[]{:S(2)}) async-start(bf16[4,256,128]{2,1,0:T(8,128)(2,1)} %combine.1), calls=%async_computation.1 | async-start | bytes 524288 | tf_op jit(solution)/shard_map/all_to_all | solution.py:583
  74.8 0.0 collective-permute-done.6.one
  74.8 0.0 collective-permute-done.7.two
  74.8 0.0 collective-permute-done.8.three
  74.8 5.5 %all-to-all-done.1.others = bf16[4,256,128]{2,1,0:T(8,128)(2,1)S(1)} async-done(((bf16[4,256,128]{2,1,0:T(8,128)(2,1)}), bf16[4,256,128]{2,1,0:T(8,128)(2,1)S(1)}, u32[]{:S(2)}, u32[]{:S(2)}) %all-to-all-start.1) | async-done | bytes 262176 | tf_op jit(solution)/shard_map/all_to_all | solution.py:583
  80.3 1.7 %finish.1 = bf16[4,512,128]{2,1,0:T(8,128)(2,1)} custom-call(s32[2,3]{1,0:T(2,128)S(1)} %copy-done.3, f32[256,128]{1,0:T(8,128)S(1)} %slice_bitcast_fusion.own, bf16[368,128]{1,0:T(8,128)(2,1)S(1)} %collective-permute-done.6.one, bf16[368,128]{1,0:T(8,128)(2,1)S(1)} %collective-permute-done.7.two, bf16[368,128]{1,0:T(8,128)(2,1)S(1)} %collective-permute-done.8.three, ...), custom_call_target="tpu_custom_call" | custom-call | tf_op jit(solution)/shard_map/finish/pallas_call | solution.py:339
  82.0 3.5 %all-to-all-start.2 = ((bf16[4,512,128]{2,1,0:T(8,128)(2,1)}), bf16[4,512,128]{2,1,0:T(8,128)(2,1)S(1)}, u32[]{:S(2)}, u32[]{:S(2)}) async-start(bf16[4,512,128]{2,1,0:T(8,128)(2,1)} %finish.1), calls=%async_computation.2 | async-start | bytes 1048576 | tf_op jit(solution)/shard_map/all_to_all | solution.py:586
  85.5 0.1 pad_maximum_fusion.7.own
  85.6 0.0 copy-done.4
  85.6 2.7 %tables.1 = (f32[2048,128]{1,0:T(8,128)S(1)}, f32[2048,128]{1,0:T(8,128)S(1)}, f32[2048,128]{1,0:T(8,128)S(1)}) custom-call(s32[2,3]{1,0:T(2,128)S(1)} %copy-done.3, bf16[112,128]{1,0:T(8,128)(2,1)S(1)} %pad_maximum_fusion.7.own, bf16[368,128]{1,0:T(8,128)(2,1)S(1)} %collective-permute-done.6.one, bf16[368,128]{1,0:T(8,128)(2,1)S(1)} %collective-permute-done.7.two, ...), custom_call_target="tpu_custom_call" | custom-call | flops 268435456 | bytes 3145728 | tf_op jit(solution)/shard_map/tables/pallas_call | solution.py:512
  88.3 0.0 copy-start
  88.3 1.0 copy-done
  89.3 3.1 %all-to-all-done.2.parts = bf16[4,512,128]{2,1,0:T(8,128)(2,1)S(1)} async-done(((bf16[4,512,128]{2,1,0:T(8,128)(2,1)}), bf16[4,512,128]{2,1,0:T(8,128)(2,1)S(1)}, u32[]{:S(2)}, u32[]{:S(2)}) %all-to-all-start.2) | async-done | bytes 524320 | tf_op jit(solution)/shard_map/all_to_all | solution.py:586
  92.4 0.0 copy-start.1
  92.4 1.2 %copy-done.1 = f32[2048,128]{1,0:T(8,128)S(1)} copy-done((f32[2048,128]{1,0:T(8,128)S(1)}, f32[2048,128]{1,0:T(8,128)}, u32[]{:S(2)}) %copy-start.1) | copy-done | bytes 1048600
  93.6 3.6 %energy.1 = f32[1,64]{1,0:T(1,128)S(1)} custom-call(s32[2,3]{1,0:T(2,128)S(1)} %copy-done.3, bf16[4,512,128]{2,1,0:T(8,128)(2,1)S(1)} %all-to-all-done.2.parts, f32[2048,128]{1,0:T(8,128)S(1)} %get-tuple-element.34.extra_a, f32[2048,128]{1,0:T(8,128)S(1)} %get-tuple-element.35.extra_b, f32[2048,128]{1,0:T(8,128)S(1)} %copy-done.1), custom_call_target="tpu_custom_call" | custom-call | tf_op jit(solution)/shard_map/energy/pallas_call | solution.py:414
  97.3 7.8 %collective-permute-start.12 = (f32[1,64]{1,0:T(1,128)S(1)}, f32[1,64]{1,0:T(1,128)S(1)}, u32[]{:S(2)}, u32[]{:S(2)}) collective-permute-start(f32[1,64]{1,0:T(1,128)S(1)} %energy.1), channel_id=1, source_target_pairs={{0,1},{1,0},{2,3},{3,2},{4,5},{5,4},{6,7},{7,6},{8,9},{9,8},{10,11... | collective-permute-start | bytes 776 | tf_op jit(solution)/shard_map/ppermute | solution.py:590
  105.1 0.8 collective-permute-done.12
  105.9 0.6 maximum_select_fusion
  (5 shorter events, 0.0 us)
Async XLA Ops:
  0.0 0.7 copy-start.2
  1.9 21.9 %collective-permute-start = (bf16[2,144,256]{2,1,0:T(8,128)(2,1)S(1)}, bf16[2,144,256]{2,1,0:T(8,128)(2,1)S(1)}, u32[]{:S(2)}, u32[]{:S(2)}) collective-permute-start(bf16[2,144,256]{2,1,0:T(8,128)(2,1)S(1)} %get-tuple-element.21), channel_id=1, source_target_pairs={{8,0},{16,8},{24,16},{32,24},{40,32},{48,40},{56,48},{64,56},{72,6... | collective-permute-start | bytes 442376 | tf_op jit(solution)/shard_map/ppermute | solution.py:546
  4.0 19.8 %collective-permute-start.2 = (bf16[2,144,256]{2,1,0:T(8,128)(2,1)S(1)}, bf16[2,144,256]{2,1,0:T(8,128)(2,1)S(1)}, u32[]{:S(2)}, u32[]{:S(2)}) collective-permute-start(bf16[2,144,256]{2,1,0:T(8,128)(2,1)S(1)} %get-tuple-element.23), channel_id=1, source_target_pairs={{0,8},{8,16},{16,24},{24,32},{32,40},{40,48},{48,56},{56,64},{64,7... | collective-permute-start | bytes 442376 | tf_op jit(solution)/shard_map/ppermute | solution.py:547
  7.2 16.6 %collective-permute-start.3 = (bf16[2,144,256]{2,1,0:T(8,128)(2,1)S(1)}, bf16[2,144,256]{2,1,0:T(8,128)(2,1)S(1)}, u32[]{:S(2)}, u32[]{:S(2)}) collective-permute-start(bf16[2,144,256]{2,1,0:T(8,128)(2,1)S(1)} %get-tuple-element.24), channel_id=1, source_target_pairs={{0,16},{8,24},{16,32},{24,40},{32,48},{40,56},{48,64},{56,72},{64,... | collective-permute-start | bytes 442376 | tf_op jit(solution)/shard_map/ppermute | solution.py:545
  14.2 9.6 %collective-permute-start.4 = (bf16[2,144,256]{2,1,0:T(8,128)(2,1)S(1)}, bf16[2,144,256]{2,1,0:T(8,128)(2,1)S(1)}, u32[]{:S(2)}, u32[]{:S(2)}) collective-permute-start(bf16[2,144,256]{2,1,0:T(8,128)(2,1)S(1)} %get-tuple-element.25), channel_id=1, source_target_pairs={{0,24},{8,32},{16,40},{24,48},{32,56},{40,64},{48,72},{56,80},{64,... | collective-permute-start | bytes 442376 | tf_op jit(solution)/shard_map/ppermute | solution.py:548
  16.6 7.2 %collective-permute-start.1 = (bf16[144,256]{1,0:T(8,128)(2,1)S(1)}, bf16[144,256]{1,0:T(8,128)(2,1)S(1)}, u32[]{:S(2)}, u32[]{:S(2)}) collective-permute-start(bf16[144,256]{1,0:T(8,128)(2,1)S(1)} %get-tuple-element.22), channel_id=1, source_target_pairs={{16,0},{24,8},{32,16},{40,24},{48,32},{56,40},{64,48},{72,56},{80,... | collective-permute-start | bytes 221192 | tf_op jit(solution)/shard_map/ppermute | solution.py:544
  27.1 8.0 %collective-permute-start.5 = (bf16[2,16,256,128]{3,2,1,0:T(8,128)(2,1)S(1)}, bf16[2,16,256,128]{3,2,1,0:T(8,128)(2,1)S(1)}, u32[]{:S(2)}, u32[]{:S(2)}) collective-permute-start(bf16[2,16,256,128]{3,2,1,0:T(8,128)(2,1)S(1)} %terms.3), channel_id=1, source_target_pairs={{0,1},{1,0},{2,3},{3,2},{4,5},{5,4},{6,7},{7,6},{8,9},{9,8},{10,11... | collective-permute-start | bytes 6291464 | tf_op jit(solution)/shard_map/ppermute | solution.py:556
  36.5 5.0 %copy-start.5 = (bf16[1,3,4096]{2,1,0:T(4,128)(2,1)S(1)}, bf16[1,3,4096]{2,1,0:T(4,128)(2,1)}, u32[]{:S(2)}) copy-start(bf16[1,3,4096]{2,1,0:T(4,128)(2,1)} %param.13) | copy-start | bytes 73732
  36.5 5.1 %copy-start.6 = (bf16[1,64]{1,0:T(2,128)(2,1)S(1)}, bf16[1,64]{1,0:T(2,128)(2,1)}, u32[]{:S(2)}) copy-start(bf16[1,64]{1,0:T(2,128)(2,1)} %param.14) | copy-start | bytes 388
  36.5 18.8 %all-to-all-start = ((bf16[16,256,128]{2,1,0:T(8,128)(2,1)}), bf16[16,256,128]{2,1,0:T(8,128)(2,1)S(1)}, u32[]{:S(2)}, u32[]{:S(2)}) async-start(bf16[16,256,128]{2,1,0:T(8,128)(2,1)} %get-tuple-element.26), calls=%async_computation | async-start | bytes 2097152 | tf_op jit(solution)/shard_map/all_to_all | solution.py:567
  41.6 22.1 %collective-permute-start.9 = (bf16[4,256,128]{2,1,0:T(8,128)(2,1)S(1)}, bf16[4,256,128]{2,1,0:T(8,128)(2,1)S(1)}, u32[]{:S(2)}, u32[]{:S(2)}) collective-permute-start(bf16[4,256,128]{2,1,0:T(8,128)(2,1)S(1)} %get-tuple-element.28), channel_id=1, source_target_pairs={{8,0},{16,8},{24,16},{32,24},{40,32},{48,40},{56,48},{64,56},{72,6... | collective-permute-start | bytes 786440 | tf_op jit(solution)/shard_map/ppermute | solution.py:569
  45.5 20.1 %collective-permute-start.10 = (bf16[4,256,128]{2,1,0:T(8,128)(2,1)S(1)}, bf16[4,256,128]{2,1,0:T(8,128)(2,1)S(1)}, u32[]{:S(2)}, u32[]{:S(2)}) collective-permute-start(bf16[4,256,128]{2,1,0:T(8,128)(2,1)S(1)} %get-tuple-element.29), channel_id=1, source_target_pairs={{16,0},{24,8},{32,16},{40,24},{48,32},{56,40},{64,48},{72,56},{80,... | collective-permute-start | bytes 786440 | tf_op jit(solution)/shard_map/ppermute | solution.py:569
  49.5 17.7 %collective-permute-start.11 = (bf16[4,256,128]{2,1,0:T(8,128)(2,1)S(1)}, bf16[4,256,128]{2,1,0:T(8,128)(2,1)S(1)}, u32[]{:S(2)}, u32[]{:S(2)}) collective-permute-start(bf16[4,256,128]{2,1,0:T(8,128)(2,1)S(1)} %get-tuple-element.30), channel_id=1, source_target_pairs={{24,0},{32,8},{40,16},{48,24},{56,32},{64,40},{72,48},{80,56},{88,... | collective-permute-start | bytes 786440 | tf_op jit(solution)/shard_map/ppermute | solution.py:569
  55.5 11.7 %copy-start.3 = (s32[2,3]{1,0:T(2,128)S(1)}, s32[2,3]{1,0:T(2,128)}, u32[]{:S(2)}) copy-start(s32[2,3]{1,0:T(2,128)} %triples.13) | copy-start | bytes 76
  55.8 19.0 %collective-permute-start.6 = (bf16[368,128]{1,0:T(8,128)(2,1)S(1)}, bf16[368,128]{1,0:T(8,128)(2,1)S(1)}, u32[]{:S(2)}, u32[]{:S(2)}) collective-permute-start(bf16[368,128]{1,0:T(8,128)(2,1)S(1)} %get-tuple-element.44), channel_id=1, source_target_pairs={{8,0},{16,8},{24,16},{32,24},{40,32},{48,40},{56,48},{64,56},{72,6... | collective-permute-start | bytes 282632 | tf_op jit(solution)/shard_map/ppermute | solution.py:580
  59.7 15.1 %collective-permute-start.7 = (bf16[368,128]{1,0:T(8,128)(2,1)S(1)}, bf16[368,128]{1,0:T(8,128)(2,1)S(1)}, u32[]{:S(2)}, u32[]{:S(2)}) collective-permute-start(bf16[368,128]{1,0:T(8,128)(2,1)S(1)} %get-tuple-element.43), channel_id=1, source_target_pairs={{16,0},{24,8},{32,16},{40,24},{48,32},{56,40},{64,48},{72,56},{80,... | collective-permute-start | bytes 282632 | tf_op jit(solution)/shard_map/ppermute | solution.py:580
  63.7 11.2 %collective-permute-start.8 = (bf16[368,128]{1,0:T(8,128)(2,1)S(1)}, bf16[368,128]{1,0:T(8,128)(2,1)S(1)}, u32[]{:S(2)}, u32[]{:S(2)}) collective-permute-start(bf16[368,128]{1,0:T(8,128)(2,1)S(1)} %get-tuple-element.42), channel_id=1, source_target_pairs={{24,0},{32,8},{40,16},{48,24},{56,32},{64,40},{72,48},{80,56},{88,... | collective-permute-start | bytes 282632 | tf_op jit(solution)/shard_map/ppermute | solution.py:580
  67.2 18.4 %copy-start.4 = (f32[64]{0:T(128)S(1)}, f32[64]{0:T(128)}, u32[]{:S(2)}) copy-start(f32[64]{0:T(128)} %param.16) | copy-start | bytes 772
  70.8 9.5 %all-to-all-start.1 = ((bf16[4,256,128]{2,1,0:T(8,128)(2,1)}), bf16[4,256,128]{2,1,0:T(8,128)(2,1)S(1)}, u32[]{:S(2)}, u32[]{:S(2)}) async-start(bf16[4,256,128]{2,1,0:T(8,128)(2,1)} %combine.1), calls=%async_computation.1 | async-start | bytes 524288 | tf_op jit(solution)/shard_map/all_to_all | solution.py:583
  82.0 10.4 %all-to-all-start.2 = ((bf16[4,512,128]{2,1,0:T(8,128)(2,1)}), bf16[4,512,128]{2,1,0:T(8,128)(2,1)S(1)}, u32[]{:S(2)}, u32[]{:S(2)}) async-start(bf16[4,512,128]{2,1,0:T(8,128)(2,1)} %finish.1), calls=%async_computation.2 | async-start | bytes 1048576 | tf_op jit(solution)/shard_map/all_to_all | solution.py:586
  88.3 1.0 copy-start
  92.4 1.2 %copy-start.1 = (f32[2048,128]{1,0:T(8,128)S(1)}, f32[2048,128]{1,0:T(8,128)}, u32[]{:S(2)}) copy-start(f32[2048,128]{1,0:T(8,128)} %copy-done) | copy-start | bytes 3145732
  97.3 8.6 %collective-permute-start.12 = (f32[1,64]{1,0:T(1,128)S(1)}, f32[1,64]{1,0:T(1,128)S(1)}, u32[]{:S(2)}, u32[]{:S(2)}) collective-permute-start(f32[1,64]{1,0:T(1,128)S(1)} %energy.1), channel_id=1, source_target_pairs={{0,1},{1,0},{2,3},{3,2},{4,5},{5,4},{6,7},{7,6},{8,9},{9,8},{10,11... | collective-permute-start | bytes 776 | tf_op jit(solution)/shard_map/ppermute | solution.py:590

commit v5 on v4

v5 whole, which is shorter than its diff:
```python
import functools

import jax
import jax.numpy as jnp
from jax import lax
from jax.experimental import pallas as pl
from jax.experimental.pallas import tpu as pltpu
from jax.sharding import PartitionSpec as P

T = 64
H = 32
F32 = jnp.float32
BF16 = jnp.bfloat16
CROWS = 16
BLOCK_ROWS = 2 * T + CROWS
SMALL_ROWS = 3 * H + 16
VMEM_LIMIT = 12 * 1024 * 1024


def shift_route(size, distance):
    return [(i, i + distance) for i in range(size) if 0 <= i + distance < size]


CORE_ROUTE = [(i, i ^ 1) for i in range(8)]


def in_hbm(array):
    return pltpu.with_memory_space_constraint(array, pltpu.HBM)


def lane_low(rows):
    return lax.broadcasted_iota(jnp.int32, (rows, 2 * T), 1) < T


def swap_halves(x):
    return pltpu.roll(x, T, 1)


def row_of(triples, owner, core, rel):
    s = jnp.where(core == 0, rel, 1 - rel)
    live = triples[s, 0] >= 0
    off_i = jnp.where(live, triples[s, 0] - owner, 2)
    off_j = jnp.where(live, triples[s, 1] - owner, 1)
    return off_i, off_j, live


def prep_kernel(triples, amps, coulomb, out1, out2, out3, up1, up2, blocks):
    owner, core = lax.axis_index("trip"), lax.rem(lax.axis_index("virt"), 2)
    occ_rows = coulomb.shape[1]
    for s in range(3):
        blocks[s, : 2 * T, :] = amps[s]
        turned = jnp.concatenate(
            [coulomb[s].astype(F32), jnp.zeros((T - occ_rows, T), F32)], axis=0
        ).T
        packed = jnp.concatenate([-turned[g * CROWS : (g + 1) * CROWS] for g in range(4)], axis=1)
        blocks[s, 2 * T :, :] = packed.astype(BF16)
    up1[...] = blocks[0:2]
    up2[...] = blocks[0]
    for rel in range(2):
        off_i, off_j, live = row_of(triples, owner, core, rel)
        for d, out in ((1, out1), (2, out2), (3, out3)):
            takes_part = live & ((off_i == d) | (off_j == d))
            other = jnp.clip(off_i + off_j - d - 1, 0, 2)

            @pl.when(takes_part)
            def _():
                out[rel] = blocks[other]

            @pl.when(jnp.logical_not(takes_part))
            def _():
                out[rel] = jnp.zeros((BLOCK_ROWS, 4 * T), BF16)


def prep(triples, amps, coulomb):
    vmem = pl.BlockSpec(memory_space=pltpu.VMEM)
    two = jax.ShapeDtypeStruct((2, BLOCK_ROWS, 4 * T), BF16)
    one = jax.ShapeDtypeStruct((BLOCK_ROWS, 4 * T), BF16)
    return pl.pallas_call(
        prep_kernel,
        out_shape=(two, two, two, two, one),
        in_specs=[pl.BlockSpec(memory_space=pltpu.SMEM), pl.BlockSpec(), pl.BlockSpec()],
        out_specs=[vmem] * 5,
        scratch_shapes=[
            pltpu.VMEM((3, BLOCK_ROWS, 4 * T), BF16),
        ],
        compiler_params=pltpu.CompilerParams(vmem_limit_bytes=VMEM_LIMIT),
        name="prep",
    )(triples, in_hbm(amps), in_hbm(coulomb))


STEPS = 8
DEPTH = 6 * T
PITCH = 2 * T + 8


def panels_kernel(integrals_in, holes, out, spread_a, spread_b, integrals, sems):
    occ_rows = holes.shape[0]
    per_step = H // STEPS
    width = per_step * 2 * T
    copies = []
    for step in range(STEPS):
        span = pl.ds(step * width, width)
        copies.append(
            pltpu.make_async_copy(integrals_in.at[:, span], integrals.at[:, span], sems.at[step])
        )
    for copy in copies:
        copy.start()
    for step in range(STEPS):
        copies[step].wait()
        for chunk in range(step * per_step, (step + 1) * per_step):
            columns = slice(chunk * 2 * T, (chunk + 1) * 2 * T)
            turned = integrals[:, columns].astype(F32).T
            for part in range(4):
                at = pl.ds((part % 2) * T + chunk * 2 + part // 2, H, stride=PITCH)
                spread_a[at, :] = turned[part * H : (part + 1) * H, : 2 * T]
                spread_b[at, :] = turned[part * H : (part + 1) * H, 2 * T :]
    for chunk in range(H):
        hole = holes[:, chunk * 2 * T : (chunk + 1) * 2 * T].astype(F32)
        hole = jnp.concatenate([hole, jnp.zeros((2 * T - occ_rows, 2 * T), F32)], axis=0).T
        for w in range(2):
            third = chunk * 2 + w
            at = third % H * 2 * T + third // H * T
            out[at : at + T, 4 * T :] = hole[w * T : (w + 1) * T].astype(BF16)

    def settle(step, _):
        rows = pl.ds(pl.multiple_of(step * 2 * T, 2 * T), 2 * T)
        source = pl.ds(pl.multiple_of(step * PITCH, 8), 2 * T)
        out[rows, : 2 * T] = spread_a[source, :].astype(BF16)
        out[rows, 2 * T : 4 * T] = spread_b[source, :].astype(BF16)
        return 0

    lax.fori_loop(0, H, settle, 0, unroll=32)


def panels_of(integrals, holes):
    return pl.pallas_call(
        panels_kernel,
        out_shape=jax.ShapeDtypeStruct((T * T, DEPTH), BF16),
        in_specs=[pl.BlockSpec(memory_space=pltpu.HBM), pl.BlockSpec()],
        out_specs=pl.BlockSpec(memory_space=pltpu.VMEM),
        scratch_shapes=[pltpu.VMEM((H * PITCH, 2 * T), F32)] * 2
        + [
            pltpu.VMEM(integrals.shape, BF16),
            pltpu.SemaphoreType.DMA((STEPS,)),
        ],
        compiler_params=pltpu.CompilerParams(vmem_limit_bytes=VMEM_LIMIT),
        cost_estimate=pl.CostEstimate(flops=1 << 28, bytes_accessed=5 << 20, transcendentals=0),
        name="panels",
    )(in_hbm(integrals), in_hbm(holes))


def terms_kernel(rel, triples, got_one, got_two, in1, in2, in3, panels, out, chosen):
    core = lax.rem(lax.axis_index("virt"), 2)
    off_i, off_j, live = row_of(triples, lax.axis_index("trip"), core, rel)
    which = jnp.where(live, off_i + off_j - 3, 3)
    for at, option in enumerate((got_one.at[0], got_one.at[1], got_two)):

        @pl.when(which == at)
        def _():
            chosen[...] = option[...]

    @pl.when(which == 3)
    def _():
        chosen[...] = jnp.zeros_like(chosen)

    blocks = (chosen, in1.at[rel], in2.at[rel], in3.at[rel])
    lead, second = [], []
    for d in range(4):
        block = blocks[d][...]
        packed = block[2 * T :]
        coulomb = jnp.concatenate(
            [packed[:, g * T : (g + 1) * T] for g in range(4)], axis=0
        )
        coulomb = jnp.concatenate([coulomb, jnp.zeros_like(coulomb)], axis=1)
        lead.append(jnp.concatenate([block[:T], coulomb], axis=1))
        second.append(jnp.concatenate([block[T : 2 * T], coulomb], axis=1))
    lead = jnp.concatenate(lead, axis=0)
    second = jnp.concatenate(second, axis=0).astype(F32).T.astype(BF16)
    low = lane_low(T)
    contract = (((1,), (1,)), ((), ()))

    eighth = lax.broadcasted_iota(jnp.int32, (8, 2 * T), 1) // 8
    odd_eighth = jnp.bitwise_and(eighth, 1) == 1
    high_eighth = jnp.bitwise_and(eighth, 2) == 2

    def skewed(tile):
        result = []
        for half in range(2):
            rows = [tile[half * H + 8 * at : half * H + 8 * at + 8] for at in range(4)]
            rows = [jnp.where(odd_eighth, rows[(j - 1) % 4], rows[j]) for j in range(4)]
            result.append([jnp.where(high_eighth, rows[(j - 2) % 4], rows[j]) for j in range(4)])
        return result

    def group(step, _):
        panel = panels[pl.ds(pl.multiple_of(step * 8 * T, 8 * T), 8 * T), :]
        by_rows = jnp.dot(panel, second, preferred_element_type=F32)
        by_cols = lax.dot_general(lead, panel, contract, preferred_element_type=F32)

        def tiles_of(pair, duo):
            row = pair * 2 * T
            lanes = slice(duo * 2 * T, (duo + 1) * 2 * T)
            upper, lower = by_rows[row : row + T, lanes], by_rows[row + T : row + 2 * T, lanes]
            first = jnp.where(low, upper, swap_halves(lower))
            other = jnp.where(low, swap_halves(upper), lower)
            at = 2 * duo * T
            return (
                first + by_cols[at : at + T, row : row + 2 * T],
                other + by_cols[at + T : at + 2 * T, row : row + 2 * T],
            )

        for two in range(2):
            evens = tiles_of(2 * two, 0) + tiles_of(2 * two, 1)
            odds = tiles_of(2 * two + 1, 0) + tiles_of(2 * two + 1, 1)
            at = pl.ds(pl.multiple_of((step * 4 + 2 * two) * 8, 16), 16)
            for d, (even, odd) in enumerate(zip(evens, odds)):
                if d == 0:
                    tiles = [
                        skewed(jnp.where(low, even, swap_halves(odd))),
                        skewed(jnp.where(low, swap_halves(even), odd)),
                    ]
                else:
                    first, second_tile = skewed(even), skewed(odd)
                    tiles = [(first[half], second_tile[half]) for half in range(2)]
                for half in range(2):
                    for j in range(4):
                        part = lax.rem(step // 2 + j, 4)
                        index = part * 4 + d if half == 0 else d * 4 + part
                        rows16 = jnp.concatenate([tiles[half][0][j], tiles[half][1][j]], axis=0)
                        out[half, index, at, :] = rows16.astype(BF16)
        return 0

    lax.fori_loop(0, 8, group, 0, unroll=8)


def terms(rel, triples, blocks, panels):
    vmem = pl.BlockSpec(memory_space=pltpu.VMEM)
    return pl.pallas_call(
        functools.partial(terms_kernel, rel),
        out_shape=jax.ShapeDtypeStruct((2, 16, 256, 2 * T), BF16),
        in_specs=[pl.BlockSpec(memory_space=pltpu.SMEM)] + [vmem] * 6,
        out_specs=vmem,
        scratch_shapes=[pltpu.VMEM((BLOCK_ROWS, 4 * T), BF16)],
        compiler_params=pltpu.CompilerParams(vmem_limit_bytes=VMEM_LIMIT),
        cost_estimate=pl.CostEstimate(flops=1 << 31, bytes_accessed=5 << 20, transcendentals=0),
        name="terms",
    )(triples, *blocks, panels)


def add_kernel(keep, got, small, first, *second):
    for half, outs in ((0, [first]), (1, second)):
        per_out = 16 // len(outs)
        for at, out in enumerate(outs):

            def one(index, _):
                source = at * per_out + index
                total = keep[half, source].astype(F32) + got[half, source].astype(F32)
                out[pl.ds(pl.multiple_of(index * 256, 256), 256), :] = total.astype(BF16)
                return 0

            lax.fori_loop(0, per_out, one, 0, unroll=4)
    for out in second[1:]:
        out[1024:, :] = small[...]


def add(keep, got, small):
    vmem = pl.BlockSpec(memory_space=pltpu.VMEM)

    def rows(count):
        return jax.ShapeDtypeStruct((count, 2 * T), BF16)

    return pl.pallas_call(
        add_kernel,
        out_shape=(rows(4096), rows(1024)) + (rows(1024 + SMALL_ROWS),) * 3,
        in_specs=[vmem] * 3,
        out_specs=[vmem] * 5,
        compiler_params=pltpu.CompilerParams(vmem_limit_bytes=VMEM_LIMIT),
        name="add",
    )(keep, got, small)


def gather_terms(mid_is_j, one, two, three, by_j, by_i):
    middle = two.astype(F32)
    by_j[...] = one.astype(F32) + jnp.where(mid_is_j, middle, 0.0)
    by_i[...] = three.astype(F32) + jnp.where(mid_is_j, 0.0, middle)


def lane_key(part, rows, lanes):
    quarter = lax.broadcasted_iota(jnp.int32, (rows, lanes), 1) // 8
    return jnp.bitwise_and(part + 4 * 64 - quarter, 3)


def by_key(key, options, shift):
    value = options[(3 - shift) % 4]
    for k in (2, 1, 0):
        value = jnp.where(key == k, options[(k - shift) % 4], value)
    return value


def own_tile(load, key, q):
    groups = []
    pairs = [load((c_quarter * 4 + q) * 16).astype(F32) for c_quarter in range(4)]
    for half in range(2):
        options = [x[half * 8 : half * 8 + 8] for x in pairs]
        groups += [by_key(key, options, b_quarter) for b_quarter in range(4)]
    return jnp.concatenate(groups, axis=0)


def turned_sum(own, by_j, by_i, base, q):
    low = lane_low(H)

    def as_rows(table):
        even = table[pl.ds(base + 2 * q, H, stride=8), :]
        odd = table[pl.ds(base + 2 * q + 1, H, stride=8), :]
        top = jnp.where(low, even, swap_halves(odd))
        bottom = jnp.where(low, swap_halves(even), odd)
        return jnp.concatenate([top, bottom], axis=0)

    flat = as_rows(by_i).T
    return own + as_rows(by_j) + jnp.concatenate([flat[:T], flat[T:]], axis=1)


def middle_is_j(triples):
    core = lax.rem(lax.axis_index("virt"), 2)
    _, off_j, _ = row_of(triples, lax.axis_index("trip"), core, 0)
    return off_j == 2


def combine_kernel(triples, own, one, two, three, out, by_j, by_i):
    rows = pl.ds(0, 1024)
    gather_terms(middle_is_j(triples), one[rows, :], two[rows, :], three[rows, :], by_j, by_i)
    for part in range(4):
        key = lane_key(part, 8, 2 * T)
        for q in range(4):
            tile = own_tile(lambda at: own[part * 256 + at : part * 256 + at + 16, :], key, q)
            total = turned_sum(tile, by_j, by_i, part * 256, q)
            out[part, q * T : (q + 1) * T, :] = total.astype(BF16)


def combine(triples, own, one, two, three):
    vmem = pl.BlockSpec(memory_space=pltpu.VMEM)
    return pl.pallas_call(
        combine_kernel,
        out_shape=jax.ShapeDtypeStruct((4, 256, 2 * T), BF16),
        in_specs=[pl.BlockSpec(memory_space=pltpu.SMEM)] + [vmem] * 4,
        out_specs=vmem,
        scratch_shapes=[pltpu.VMEM((1024, 2 * T), F32)] * 2,
        compiler_params=pltpu.CompilerParams(vmem_limit_bytes=VMEM_LIMIT),
        name="combine",
    )(triples, own, one, two, three)


PART_PITCH = T + 8
PART_ROWS = 16 * PART_PITCH


def energy_kernel(
    triples, own, one, two, three, others, extra_b, extra_a, inverse, out, by_j, by_i, plain, turned
):
    virt = lax.axis_index("virt")
    _, _, live = row_of(triples, lax.axis_index("trip"), lax.rem(virt, 2), 0)
    gather_terms(middle_is_j(triples), one[...], two[...], three[...], by_j, by_i)
    wide_key = lane_key(virt // 2, 8, 2 * T)
    key = lane_key(virt // 2, 8, T)
    for q in range(4):
        at = slice(q * T, (q + 1) * T)
        tile = own_tile(lambda at: own[at : at + 16, :], wide_key, q)
        first = turned_sum(tile, by_j, by_i, 0, q)
        second = sum(others[source, at, :].astype(F32) for source in range(4))
        for half, tile in ((0, first), (1, second)):
            base = (half * 8 + 2 * q) * PART_PITCH
            flat = tile.T
            plain[base : base + T, :] = tile[:, :T]
            turned[base : base + T, :] = flat[:T]
            base += PART_PITCH
            plain[base : base + T, :] = swap_halves(tile)[:, :T]
            turned[base : base + T, :] = flat[T:]

    def exchanged(table, half, c_low):
        groups = []
        for b_half in range(2):
            options = [
                table[
                    pl.ds(b_half * 8 * PART_PITCH + half * H + 8 * at + c_low, 8, stride=PART_PITCH), :
                ]
                for at in range(4)
            ]
            groups += [by_key(key, options, b_quarter) for b_quarter in range(4)]
        return jnp.concatenate(groups, axis=0)

    sum_b = jnp.zeros((T, T), F32)
    sum_a = jnp.zeros((T, T), F32)
    for half in range(2):
        for c_low in range(8):
            index = half * 8 + c_low
            at = slice(index * T, (index + 1) * T)
            acb = exchanged(plain, half, c_low)
            cab = exchanged(turned, half, c_low)
            bac = turned[index * PART_PITCH : index * PART_PITCH + T, :]
            inv = inverse[at, :]
            sum_b += (4.0 * bac + acb) * (bac - cab + extra_b[at, :]) * inv
            sum_a += bac * (acb - acb.T + extra_a[at, :]) * inv
    total = jnp.sum(sum_a + sum_b.T, axis=0, keepdims=True)
    total = jnp.where(live, total, 0.0)
    total = jnp.concatenate([total, jnp.zeros_like(total)], axis=1)
    out[...] = jnp.broadcast_to(total[None], out.shape)


def energy_of(triples, own, shares, others, extra_b, extra_a, inverse):
    vmem = pl.BlockSpec(memory_space=pltpu.VMEM)
    return pl.pallas_call(
        energy_kernel,
        out_shape=jax.ShapeDtypeStruct((8, 8, 2 * T), F32),
        in_specs=[pl.BlockSpec(memory_space=pltpu.SMEM)] + [vmem] * 8,
        out_specs=vmem,
        scratch_shapes=[pltpu.VMEM((256, 2 * T), F32)] * 2 + [pltpu.VMEM((PART_ROWS, T), F32)] * 2,
        compiler_params=pltpu.CompilerParams(vmem_limit_bytes=VMEM_LIMIT),
        name="energy",
    )(triples, own, *shares, others, extra_b, extra_a, inverse)


def tables_kernel(
    triples, own, one, two, three, virt_energy, extra_b, extra_a, inverse, columns, rows, matrices
):
    virt = lax.axis_index("virt")
    off_i, off_j, _ = row_of(triples, lax.axis_index("trip"), lax.rem(virt, 2), 0)
    part = virt // 2

    def small_of(table):
        return table[table.shape[0] - SMALL_ROWS :, :]

    def exch(slot, table, index):
        flat = small_of(table)[index * H : (index + 1) * H, :].astype(F32)
        matrices[pl.ds(slot * T, H, stride=2), :] = flat[:, :T]
        matrices[pl.ds(slot * T + 1, H, stride=2), :] = swap_halves(flat)[:, :T]
        return matrices[slot * T : (slot + 1) * T, :]

    def pick(options, index):
        result = options[-1]
        for at in range(len(options) - 1):
            result = jnp.where(index == at, options[at], result)
        return result

    own_exch = [exch(slot, own, slot) for slot in range(3)]
    kj = pick(own_exch[:2], off_j - 1)
    ki = pick(own_exch[1:], off_i - 2)
    ji = pick([exch(3, one, 0), exch(4, one, 1), exch(5, two, 0)], off_i + off_j - 3)
    kj_t, ki_t, ji_t = kj.T, ki.T, ji.T
    heads = [small_of(x)[3 * H :, :].astype(F32) for x in (own, one, two, three)]
    head_i = pick([heads[2], heads[3]], off_i - 2)
    head_j = pick([heads[1], heads[2]], off_j - 1)
    head_k = heads[0]
    occ = head_i[0:1, T:] + head_j[0:1, T:] + head_k[0:1, T:]
    s_i, s_j, s_k = (x[0:1, :T] for x in (head_i, head_j, head_k))
    e_a = virt_energy[...]
    s_ib, s_jb, s_kb, e_b = (jnp.broadcast_to(v, (T, T)).T for v in (s_i, s_j, s_k, e_a))
    for at, m in enumerate((kj, ji_t, ji, kj_t, s_ib, s_jb, s_kb, e_b)):
        rows[at * T : (at + 1) * T, :] = m
    for at, m in enumerate((kj, ji_t, ki_t, ki)):
        for half in range(2):
            for quarter in range(4):
                base = quarter * T + at * 16 + half * 8
                source = half * H + quarter * 8
                columns[base : base + 8, :] = m[source : source + 8]
    key = lane_key(part, 1, T)
    key_rows = lane_key(part, T, T)
    c_of_row = lax.broadcasted_iota(jnp.int32, (T, T), 0)
    ki_diff = ki - ki_t

    def one(index, _):
        half, c_low = index // 8, lax.rem(index, 8)
        first_c = half * H + c_low
        looked_up = [
            [rows[pl.ds(at * T + first_c + 8 * quarter, 1), :] for quarter in range(4)]
            for at in range(8)
        ]
        for quarter in range(4):
            wanted = first_c + 8 * jnp.bitwise_and(key_rows - quarter, 3)
            choice = jnp.where(c_of_row == wanted, 1.0, 0.0).astype(BF16)
            source = columns[quarter * T : (quarter + 1) * T, :].astype(BF16)
            over_bc = jnp.dot(source, choice, preferred_element_type=F32)
            kj_ca, ji_ac, ji_ca, kj_ac, si_c, sj_c, sk_c, e_c = (
                by_key(key, options, quarter) for options in looked_up
            )
            for b_half in range(2):
                at = b_half * H + quarter * 8
                b = slice(at, at + 8)
                kj_bc, ji_cb, ki_cb, ki_bc = (
                    over_bc[g * 16 + b_half * 8 : g * 16 + b_half * 8 + 8] for g in range(4)
                )
                target = pl.ds(pl.multiple_of(index * T + at, 8), 8)
                extra_b[target, :] = (
                    s_ib[b] * kj_ca
                    - s_kb[b] * ji_ac
                    + s_j * (ki_cb - ki_bc)
                    + sk_c * ji_t[b]
                    - si_c * kj[b]
                )
                extra_a[target, :] = (
                    s_kb[b] * ji_ca
                    - s_ib[b] * kj_ac
                    + s_i * kj_bc
                    - s_k * ji_cb
                    + sj_c * ki_diff[b]
                )
                inverse[target, :] = 1.0 / (occ - e_a - e_b[b] - e_c)
        return 0

    lax.fori_loop(0, 16, one, 0, unroll=2)


def tables(triples, small, virt_energy):
    vmem = pl.BlockSpec(memory_space=pltpu.VMEM)
    table = jax.ShapeDtypeStruct((16 * T, T), F32)
    return pl.pallas_call(
        tables_kernel,
        out_shape=(table, table, table),
        in_specs=[pl.BlockSpec(memory_space=pltpu.SMEM)] + [vmem] * 5,
        out_specs=[vmem] * 3,
        scratch_shapes=[pltpu.VMEM((rows * T, T), F32) for rows in (4, 8, 6)],
        compiler_params=pltpu.CompilerParams(vmem_limit_bytes=VMEM_LIMIT),
        cost_estimate=pl.CostEstimate(flops=1 << 28, bytes_accessed=3 << 20, transcendentals=0),
        name="tables",
    )(triples, *small, virt_energy)


def local(
    virt_integrals,
    pair_amps,
    hole_amps,
    coulomb_ints,
    exchange_ints,
    singles,
    occ_energy,
    virt_energy,
    triples,
):
    n_trip = lax.axis_size("trip")

    out1, out2, out3, up1, up2 = prep(
        triples, pair_amps.reshape(3, 2 * T, 4 * T), coulomb_ints.reshape(coulomb_ints.shape[1:])
    )
    got_two = lax.ppermute(up2, "trip", shift_route(n_trip, -2))
    in2 = lax.ppermute(out2, "trip", shift_route(n_trip, 2))
    got_one = lax.ppermute(up1, "trip", shift_route(n_trip, -1))
    in1 = lax.ppermute(out1, "trip", shift_route(n_trip, 1))
    in3 = lax.ppermute(out3, "trip", shift_route(n_trip, 3))
    blocks = (got_one, got_two, in1, in2, in3)

    panels = panels_of(
        virt_integrals.reshape(4 * T, T * T), hole_amps.reshape(hole_amps.shape[1:])
    )

    heads = jnp.concatenate([singles, jnp.broadcast_to(occ_energy[:, None], (1, T))], axis=1)
    small = jnp.concatenate(
        [exchange_ints.reshape(3 * H, 2 * T), heads, jnp.zeros((15, 2 * T), BF16)], axis=0
    )
    panels, small = lax.optimization_barrier((panels, small))

    send = terms(1, triples, blocks, panels)
    got = lax.ppermute(send, "virt", CORE_ROUTE)
    keep = terms(0, triples, blocks, panels)
    first_half, *second_half = add(keep, got, small)
    over_y = functools.partial(
        lax.all_to_all,
        axis_name="virt",
        split_axis=0,
        concat_axis=0,
        axis_index_groups=[[0, 2, 4, 6], [1, 3, 5, 7]],
        tiled=True,
    )
    by_y = over_y(first_half.reshape(16, 256, 2 * T))
    by_owner = [
        lax.ppermute(second_half[d], "trip", shift_route(n_trip, -d)) for d in (1, 2, 3)
    ]

    total = by_y.reshape(4, 4, 256, 2 * T).astype(F32)
    total = total[0] + total[1] + total[2] + total[3]
    to_share = [total[d].astype(BF16) for d in (1, 2, 3)]
    shares = [
        lax.ppermute(to_share[d - 1], "trip", shift_route(n_trip, -d)) for d in (1, 2, 3)
    ]
    by_owner, _ = lax.optimization_barrier((by_owner, to_share))
    others = over_y(combine(triples, second_half[0], *by_owner))
    extras = tables(triples, [small, *by_owner], virt_energy.reshape(1, T))

    mine = energy_of(triples, total[0], shares, others, *extras)
    everyone = lax.all_to_all(mine, "virt", 0, 0, tiled=True)
    return jnp.sum(everyone[:, 0, :T].reshape(4, 2, T), axis=0)


def solution(mesh):
    placed = (
        P("trip", "virt", None),
        P("trip", None, None, None, "virt"),
        P("trip", "virt", None),
        P("trip", None, "virt", None),
        P("trip", None, None),
        P("trip", None),
        P("trip"),
        P(),
        P("trip", None),
    )
    return jax.shard_map(
        local, mesh=mesh, in_specs=placed, out_specs=P("trip", None), check_vma=False
    )
```

time: 107 us -> 98.2 us (0.918)
  the two profiles are of different devices: /device:TPU:227 before, /device:TPU:384 now
where the time goes in v5:
time: 98.2 us; the launch traced here: 97.4 us
  starting transfers between devices  55.6 us (57%)
  Pallas kernels  20.9 us (21%)
  blocking collectives  7.82 us (8%)
  waiting for transfers between devices  7.61 us (8%)
  other arithmetic  2.85 us (3%)
  local copies, waits for them, and re-layouts  1.61 us (2%)
    ppermute x3, starting transfers between devices, local(): lax.ppermute(to_share[d - 1], 'trip', shift_route(n_trip, -d))  14.1 us
    ppermute x3, starting transfers between devices, local(): lax.ppermute(second_half[d], 'trip', shift_route(n_trip, -d))  12.9 us
    all_to_all x1, blocking collectives, local(): everyone = lax.all_to_all(mine, 'virt', 0, 0, tiled=True)  7.82 us
    ppermute x1, starting transfers between devices, local(): got_two = lax.ppermute(up2, 'trip', shift_route(n_trip, -2))  6.59 us
    pallas_call x2, Pallas kernels, terms(): pl.pallas_call(functools.partial(terms_kernel, rel), out_shape=jax.ShapeD...  6.55 us
    all_to_all x1, starting transfers between devices, local(): by_y = over_y(first_half.reshape(16, 256, 2 * T))  4.46 us
    all_to_all x1, waiting for transfers between devices, local(): others = over_y(combine(triples, second_half[0], *by_owner))  4.16 us
    ppermute x1, starting transfers between devices, local(): in3 = lax.ppermute(out3, 'trip', shift_route(n_trip, 3))  3.77 us
  transfers between devices with their start and end apart: 14, of which 3 were waited for; matrix products, arithmetic and copies ran while one was open for 3% of the time, Pallas kernels for 13%

profile of v5, /device:TPU:384, one launch (start us, length us, event | category | flops | bytes accessed | tf_op | source)
XLA Modules:
  0.0 97.4 jit_solution(17675953505966432336)
XLA Ops:
  0.0 0.0 copy-start
  0.0 0.7 copy-done
  0.7 1.2 %prep.1 = (bf16[2,144,256]{2,1,0:T(8,128)(2,1)S(1)}, bf16[2,144,256]{2,1,0:T(8,128)(2,1)S(1)}, bf16[2,144,256]{2,1,0:T(8,128)(2,1)S(1)}, bf16[2,144,256]{2,1,0:T(8,128)(2,1)S(1)}, bf16[144,256]{1,0:T(8,128)(2,1)S(1)}) custom-call(s32[2,3]{1,0:T(2,128)S(1)} %copy-done, bf16[3,128,256]{2,1,0:T(8,128)(2,1)} %bitcast.20, bf16[3,38,64]{2,1,0:T(8,128)(2,1)} %bitcast.21), custom_call_target="tpu_custom_call" | custom-call | tf_op jit(solution)/shard_map/prep/pallas_call | solution.py:78
  1.9 6.6 %collective-permute-start.1 = (bf16[144,256]{1,0:T(8,128)(2,1)S(1)}, bf16[144,256]{1,0:T(8,128)(2,1)S(1)}, u32[]{:S(2)}, u32[]{:S(2)}) collective-permute-start(bf16[144,256]{1,0:T(8,128)(2,1)S(1)} %get-tuple-element.24), channel_id=1, source_target_pairs={{16,0},{24,8},{32,16},{40,24},{48,32},{56,40},{64,48},{72,56},{80,... | collective-permute-start | bytes 221192 | tf_op jit(solution)/shard_map/ppermute | solution.py:542
  8.5 3.0 %collective-permute-start = (bf16[2,144,256]{2,1,0:T(8,128)(2,1)S(1)}, bf16[2,144,256]{2,1,0:T(8,128)(2,1)S(1)}, u32[]{:S(2)}, u32[]{:S(2)}) collective-permute-start(bf16[2,144,256]{2,1,0:T(8,128)(2,1)S(1)} %get-tuple-element.23), channel_id=1, source_target_pairs={{8,0},{16,8},{24,16},{32,24},{40,32},{48,40},{56,48},{64,56},{72,6... | collective-permute-start | bytes 442376 | tf_op jit(solution)/shard_map/ppermute | solution.py:544
  11.5 2.8 %collective-permute-start.2 = (bf16[2,144,256]{2,1,0:T(8,128)(2,1)S(1)}, bf16[2,144,256]{2,1,0:T(8,128)(2,1)S(1)}, u32[]{:S(2)}, u32[]{:S(2)}) collective-permute-start(bf16[2,144,256]{2,1,0:T(8,128)(2,1)S(1)} %get-tuple-element.25), channel_id=1, source_target_pairs={{0,8},{8,16},{16,24},{24,32},{32,40},{40,48},{48,56},{56,64},{64,7... | collective-permute-start | bytes 442376 | tf_op jit(solution)/shard_map/ppermute | solution.py:545
  14.3 2.5 %collective-permute-start.3 = (bf16[2,144,256]{2,1,0:T(8,128)(2,1)S(1)}, bf16[2,144,256]{2,1,0:T(8,128)(2,1)S(1)}, u32[]{:S(2)}, u32[]{:S(2)}) collective-permute-start(bf16[2,144,256]{2,1,0:T(8,128)(2,1)S(1)} %get-tuple-element.26), channel_id=1, source_target_pairs={{0,16},{8,24},{16,32},{24,40},{32,48},{40,56},{48,64},{56,72},{64,... | collective-permute-start | bytes 442376 | tf_op jit(solution)/shard_map/ppermute | solution.py:543
  16.9 3.8 %collective-permute-start.4 = (bf16[2,144,256]{2,1,0:T(8,128)(2,1)S(1)}, bf16[2,144,256]{2,1,0:T(8,128)(2,1)S(1)}, u32[]{:S(2)}, u32[]{:S(2)}) collective-permute-start(bf16[2,144,256]{2,1,0:T(8,128)(2,1)S(1)} %get-tuple-element.27), channel_id=1, source_target_pairs={{0,24},{8,32},{16,40},{24,48},{32,56},{40,64},{48,72},{56,80},{64,... | collective-permute-start | bytes 442376 | tf_op jit(solution)/shard_map/ppermute | solution.py:546
  21.3 0.8 reshape.42
  22.1 0.1 pad.3.clone
  22.2 0.7 fusion.3.small.own
  22.9 0.0 copy-start.1
  23.0 3.8 %panels.1 = bf16[4096,384]{1,0:T(8,128)(2,1)S(1)} custom-call(bf16[256,4096]{1,0:T(8,128)(2,1)} %bitcast.18, bf16[38,4096]{1,0:T(8,128)(2,1)} %bitcast.19), custom_call_target="tpu_custom_call" | custom-call | flops 268435456 | bytes 5242880 | tf_op jit(solution)/shard_map/panels/pallas_call | solution.py:136
  26.7 0.0 collective-permute-done.1.got_two
  26.7 0.0 collective-permute-done.got_one
  26.7 0.0 collective-permute-done.2.in1
  26.8 0.0 collective-permute-done.3.in2
  26.8 0.0 collective-permute-done.4.in3
  26.8 0.0 copy-done.1
  26.8 3.3 %terms.3 = bf16[2,16,256,128]{3,2,1,0:T(8,128)(2,1)S(1)} custom-call(s32[2,3]{1,0:T(2,128)S(1)} %copy-done.1, bf16[2,144,256]{2,1,0:T(8,128)(2,1)S(1)} %collective-permute-done.got_one, bf16[144,256]{1,0:T(8,128)(2,1)S(1)} %collective-permute-done.1.got_two, bf16[2,144,256]{2,1,0:T(8,128)(2,1)S(1)} %collective-permute-done.2.in1, ...), custom_call_target="tpu_custom_call" | custom-call | flops 2147483648 | bytes 5242880 | tf_op jit(solution)/shard_map/terms/pallas_call | solution.py:237
  30.1 1.9 %collective-permute-start.5 = (bf16[2,16,256,128]{3,2,1,0:T(8,128)(2,1)S(1)}, bf16[2,16,256,128]{3,2,1,0:T(8,128)(2,1)S(1)}, u32[]{:S(2)}, u32[]{:S(2)}) collective-permute-start(bf16[2,16,256,128]{3,2,1,0:T(8,128)(2,1)S(1)} %terms.3), channel_id=1, source_target_pairs={{0,1},{1,0},{2,3},{3,2},{4,5},{5,4},{6,7},{7,6},{8,9},{9,8},{10,11... | collective-permute-start | bytes 6291464 | tf_op jit(solution)/shard_map/ppermute | solution.py:560
  32.0 3.3 %terms.2.keep = bf16[2,16,256,128]{3,2,1,0:T(8,128)(2,1)S(1)} custom-call(s32[2,3]{1,0:T(2,128)S(1)} %copy-done.1, bf16[2,144,256]{2,1,0:T(8,128)(2,1)S(1)} %collective-permute-done.got_one, bf16[144,256]{1,0:T(8,128)(2,1)S(1)} %collective-permute-done.1.got_two, bf16[2,144,256]{2,1,0:T(8,128)(2,1)S(1)} %collective-permute-done.2.in1, ...), custom_call_target="tpu_custom_call" | custom-call | flops 2147483648 | bytes 5242880 | tf_op jit(solution)/shard_map/terms/pallas_call | solution.py:237
  35.3 0.8 collective-permute-done.5.got
  36.1 1.4 %add.27 = (bf16[4096,128]{1,0:T(8,128)(2,1)}, bf16[1024,128]{1,0:T(8,128)(2,1)S(1)}, bf16[1136,128]{1,0:T(8,128)(2,1)S(1)}, bf16[1136,128]{1,0:T(8,128)(2,1)S(1)}, bf16[1136,128]{1,0:T(8,128)(2,1)S(1)}) custom-call(bf16[2,16,256,128]{3,2,1,0:T(8,128)(2,1)S(1)} %terms.2.keep, bf16[2,16,256,128]{3,2,1,0:T(8,128)(2,1)S(1)} %collective-permute-done.5.got, ...), custom_call_target="tpu_custom_call" | custom-call | tf_op jit(solution)/shard_map/add/pallas_call | solution.py:271
  37.5 4.5 %all-to-all-start = ((bf16[16,256,128]{2,1,0:T(8,128)(2,1)}), bf16[16,256,128]{2,1,0:T(8,128)(2,1)}, u32[]{:S(2)}, u32[]{:S(2)}) async-start(bf16[16,256,128]{2,1,0:T(8,128)(2,1)} %bitcast.5), calls=%async_computation | async-start | bytes 2097152 | tf_op jit(solution)/shard_map/all_to_all | solution.py:571
  42.0 6.6 %collective-permute-start.9 = (bf16[1136,128]{1,0:T(8,128)(2,1)S(1)}, bf16[1136,128]{1,0:T(8,128)(2,1)S(1)}, u32[]{:S(2)}, u32[]{:S(2)}) collective-permute-start(bf16[1136,128]{1,0:T(8,128)(2,1)S(1)} %get-tuple-element.32), channel_id=1, source_target_pairs={{8,0},{16,8},{24,16},{32,24},{40,32},{48,40},{56,48},{64,56},{72,6... | collective-permute-start | bytes 872456 | tf_op jit(solution)/shard_map/ppermute | solution.py:573
  48.6 2.1 %collective-permute-start.10 = (bf16[1136,128]{1,0:T(8,128)(2,1)S(1)}, bf16[1136,128]{1,0:T(8,128)(2,1)S(1)}, u32[]{:S(2)}, u32[]{:S(2)}) collective-permute-start(bf16[1136,128]{1,0:T(8,128)(2,1)S(1)} %get-tuple-element.33), channel_id=1, source_target_pairs={{16,0},{24,8},{32,16},{40,24},{48,32},{56,40},{64,48},{72,56},{80,... | collective-permute-start | bytes 872456 | tf_op jit(solution)/shard_map/ppermute | solution.py:573
  50.7 4.2 %collective-permute-start.11 = (bf16[1136,128]{1,0:T(8,128)(2,1)S(1)}, bf16[1136,128]{1,0:T(8,128)(2,1)S(1)}, u32[]{:S(2)}, u32[]{:S(2)}) collective-permute-start(bf16[1136,128]{1,0:T(8,128)(2,1)S(1)} %get-tuple-element.34), channel_id=1, source_target_pairs={{24,0},{32,8},{40,16},{48,24},{56,32},{64,40},{72,48},{80,56},{88,... | collective-permute-start | bytes 872456 | tf_op jit(solution)/shard_map/ppermute | solution.py:573
  54.9 2.6 %all-to-all-done = bf16[16,256,128]{2,1,0:T(8,128)(2,1)} async-done(((bf16[16,256,128]{2,1,0:T(8,128)(2,1)}), bf16[16,256,128]{2,1,0:T(8,128)(2,1)}, u32[]{:S(2)}, u32[]{:S(2)}) %all-to-all-start) | async-done | bytes 1048608 | tf_op jit(solution)/shard_map/all_to_all | solution.py:571
  57.5 1.4 %convert_element_type.16 = f32[16,256,128]{2,1,0:T(8,128)S(1)} convert(bf16[16,256,128]{2,1,0:T(8,128)(2,1)} %all-to-all-done) | non-fusion elementwise | flops 524288 | bytes 3145728 | tf_op jit(solution)/shard_map/convert_element_type | solution.py:576
  58.9 0.0 copy-start.2
  59.0 0.1 fusion.4
  59.1 4.7 %collective-permute-start.8 = (bf16[256,128]{1,0:T(8,128)(2,1)S(1)}, bf16[256,128]{1,0:T(8,128)(2,1)S(1)}, u32[]{:S(2)}, u32[]{:S(2)}) collective-permute-start(bf16[256,128]{1,0:T(8,128)(2,1)S(1)} %get-tuple-element.43), channel_id=1, source_target_pairs={{24,0},{32,8},{40,16},{48,24},{56,32},{64,40},{72,48},{80,56},{88,... | collective-permute-start | bytes 196616 | tf_op jit(solution)/shard_map/ppermute | solution.py:580
  63.8 5.1 %collective-permute-start.7 = (bf16[256,128]{1,0:T(8,128)(2,1)S(1)}, bf16[256,128]{1,0:T(8,128)(2,1)S(1)}, u32[]{:S(2)}, u32[]{:S(2)}) collective-permute-start(bf16[256,128]{1,0:T(8,128)(2,1)S(1)} %get-tuple-element.44), channel_id=1, source_target_pairs={{16,0},{24,8},{32,16},{40,24},{48,32},{56,40},{64,48},{72,56},{80,... | collective-permute-start | bytes 196616 | tf_op jit(solution)/shard_map/ppermute | solution.py:580
  69.0 0.0 collective-permute-done.9.one
  69.0 4.3 %collective-permute-start.6 = (bf16[256,128]{1,0:T(8,128)(2,1)S(1)}, bf16[256,128]{1,0:T(8,128)(2,1)S(1)}, u32[]{:S(2)}, u32[]{:S(2)}) collective-permute-start(bf16[256,128]{1,0:T(8,128)(2,1)S(1)} %get-tuple-element.45), channel_id=1, source_target_pairs={{8,0},{16,8},{24,16},{32,24},{40,32},{48,40},{56,48},{64,56},{72,6... | collective-permute-start | bytes 196616 | tf_op jit(solution)/shard_map/ppermute | solution.py:580
  73.3 0.0 collective-permute-done.10.two
  73.3 0.0 collective-permute-done.11.three
  73.3 3.6 %combine.1 = bf16[4,256,128]{2,1,0:T(8,128)(2,1)} custom-call(s32[2,3]{1,0:T(2,128)S(1)} %copy-done.1, bf16[1024,128]{1,0:T(8,128)(2,1)S(1)} %get-tuple-element.31.own, bf16[1136,128]{1,0:T(8,128)(2,1)S(1)} %collective-permute-done.9.one, bf16[1136,128]{1,0:T(8,128)(2,1)S(1)} %collective-permute-done.10.two, bf16[1136,128]{1,0:T(8,128)(2,1)S(1)} %collective-permute-done.11.three), custom_call_target="tpu_custom_call" | custom-call | tf_op jit(solution)/shard_map/combine/pallas_call | solution.py:341
  76.9 3.4 %all-to-all-start.1 = ((bf16[4,256,128]{2,1,0:T(8,128)(2,1)}), bf16[4,256,128]{2,1,0:T(8,128)(2,1)S(1)}, u32[]{:S(2)}, u32[]{:S(2)}) async-start(bf16[4,256,128]{2,1,0:T(8,128)(2,1)} %combine.1), calls=%async_computation.1 | async-start | bytes 524288 | tf_op jit(solution)/shard_map/all_to_all | solution.py:583
  80.4 0.0 copy-done.2
  80.4 2.4 %tables.1 = (f32[1024,64]{1,0:T(8,128)S(1)}, f32[1024,64]{1,0:T(8,128)S(1)}, f32[1024,64]{1,0:T(8,128)S(1)}) custom-call(s32[2,3]{1,0:T(2,128)S(1)} %copy-done.1, bf16[112,128]{1,0:T(8,128)(2,1)S(1)} %fusion.3.small.own, bf16[1136,128]{1,0:T(8,128)(2,1)S(1)} %collective-permute-done.9.one, bf16[1136,128]{1,0:T(8,128)(2,1)S(1)} %collective-permute-done.10.two, ...), custom_call_target="tpu_custom_call" | custom-call | flops 268435456 | bytes 3145728 | tf_op jit(solution)/shard_map/tables/pallas_call | solution.py:514
  82.8 0.0 collective-permute-done.8.three
  82.8 0.0 collective-permute-done.7.two
  82.8 0.0 collective-permute-done.6.one
  82.8 4.2 %all-to-all-done.1.others = bf16[4,256,128]{2,1,0:T(8,128)(2,1)S(1)} async-done(((bf16[4,256,128]{2,1,0:T(8,128)(2,1)}), bf16[4,256,128]{2,1,0:T(8,128)(2,1)S(1)}, u32[]{:S(2)}, u32[]{:S(2)}) %all-to-all-start.1) | async-done | bytes 262176 | tf_op jit(solution)/shard_map/all_to_all | solution.py:583
  87.0 2.0 %energy.1 = f32[8,8,128]{2,1,0:T(8,128)S(1)} custom-call(s32[2,3]{1,0:T(2,128)S(1)} %copy-done.1, f32[256,128]{1,0:T(8,128)S(1)} %slice_bitcast_fusion.own, bf16[256,128]{1,0:T(8,128)(2,1)S(1)} %collective-permute-done.6.one, bf16[256,128]{1,0:T(8,128)(2,1)S(1)} %collective-permute-done.7.two, bf16[256,128]{1,0:T(8,128)(2,1)S(1)} %collective-permute-done.8.three, ...), custom_call_target="tpu_custom_call" | custom-call | tf_op jit(solution)/shard_map/energy/pallas_call | solution.py:410
  89.0 7.8 %all_to_all.15 = f32[8,8,128]{2,1,0:T(8,128)S(1)} all-to-all(f32[8,8,128]{2,1,0:T(8,128)S(1)} %energy.1), channel_id=1, replica_groups=mesh['trip'=64,'virt'=8] {'virt'}, dimensions={0} | all-to-all | bytes 65536 | tf_op jit(solution)/shard_map/all_to_all | solution.py:587
  96.8 0.6 reduce_sum.9
  (4 shorter events, 0.0 us)
Async XLA Ops:
  0.0 0.7 copy-start
  1.9 24.9 %collective-permute-start.1 = (bf16[144,256]{1,0:T(8,128)(2,1)S(1)}, bf16[144,256]{1,0:T(8,128)(2,1)S(1)}, u32[]{:S(2)}, u32[]{:S(2)}) collective-permute-start(bf16[144,256]{1,0:T(8,128)(2,1)S(1)} %get-tuple-element.24), channel_id=1, source_target_pairs={{16,0},{24,8},{32,16},{40,24},{48,32},{56,40},{64,48},{72,56},{80,... | collective-permute-start | bytes 221192 | tf_op jit(solution)/shard_map/ppermute | solution.py:542
  8.5 18.3 %collective-permute-start = (bf16[2,144,256]{2,1,0:T(8,128)(2,1)S(1)}, bf16[2,144,256]{2,1,0:T(8,128)(2,1)S(1)}, u32[]{:S(2)}, u32[]{:S(2)}) collective-permute-start(bf16[2,144,256]{2,1,0:T(8,128)(2,1)S(1)} %get-tuple-element.23), channel_id=1, source_target_pairs={{8,0},{16,8},{24,16},{32,24},{40,32},{48,40},{56,48},{64,56},{72,6... | collective-permute-start | bytes 442376 | tf_op jit(solution)/shard_map/ppermute | solution.py:544
  11.5 15.2 %collective-permute-start.2 = (bf16[2,144,256]{2,1,0:T(8,128)(2,1)S(1)}, bf16[2,144,256]{2,1,0:T(8,128)(2,1)S(1)}, u32[]{:S(2)}, u32[]{:S(2)}) collective-permute-start(bf16[2,144,256]{2,1,0:T(8,128)(2,1)S(1)} %get-tuple-element.25), channel_id=1, source_target_pairs={{0,8},{8,16},{16,24},{24,32},{32,40},{40,48},{48,56},{56,64},{64,7... | collective-permute-start | bytes 442376 | tf_op jit(solution)/shard_map/ppermute | solution.py:545
  14.3 12.4 %collective-permute-start.3 = (bf16[2,144,256]{2,1,0:T(8,128)(2,1)S(1)}, bf16[2,144,256]{2,1,0:T(8,128)(2,1)S(1)}, u32[]{:S(2)}, u32[]{:S(2)}) collective-permute-start(bf16[2,144,256]{2,1,0:T(8,128)(2,1)S(1)} %get-tuple-element.26), channel_id=1, source_target_pairs={{0,16},{8,24},{16,32},{24,40},{32,48},{40,56},{48,64},{56,72},{64,... | collective-permute-start | bytes 442376 | tf_op jit(solution)/shard_map/ppermute | solution.py:543
  16.9 9.9 %collective-permute-start.4 = (bf16[2,144,256]{2,1,0:T(8,128)(2,1)S(1)}, bf16[2,144,256]{2,1,0:T(8,128)(2,1)S(1)}, u32[]{:S(2)}, u32[]{:S(2)}) collective-permute-start(bf16[2,144,256]{2,1,0:T(8,128)(2,1)S(1)} %get-tuple-element.27), channel_id=1, source_target_pairs={{0,24},{8,32},{16,40},{24,48},{32,56},{40,64},{48,72},{56,80},{64,... | collective-permute-start | bytes 442376 | tf_op jit(solution)/shard_map/ppermute | solution.py:546
  22.9 3.8 %copy-start.1 = (s32[2,3]{1,0:T(2,128)S(1)}, s32[2,3]{1,0:T(2,128)}, u32[]{:S(2)}) copy-start(s32[2,3]{1,0:T(2,128)} %triples.11) | copy-start | bytes 76
  30.1 6.1 %collective-permute-start.5 = (bf16[2,16,256,128]{3,2,1,0:T(8,128)(2,1)S(1)}, bf16[2,16,256,128]{3,2,1,0:T(8,128)(2,1)S(1)}, u32[]{:S(2)}, u32[]{:S(2)}) collective-permute-start(bf16[2,16,256,128]{3,2,1,0:T(8,128)(2,1)S(1)} %terms.3), channel_id=1, source_target_pairs={{0,1},{1,0},{2,3},{3,2},{4,5},{5,4},{6,7},{7,6},{8,9},{9,8},{10,11... | collective-permute-start | bytes 6291464 | tf_op jit(solution)/shard_map/ppermute | solution.py:560
  37.5 20.0 %all-to-all-start = ((bf16[16,256,128]{2,1,0:T(8,128)(2,1)}), bf16[16,256,128]{2,1,0:T(8,128)(2,1)}, u32[]{:S(2)}, u32[]{:S(2)}) async-start(bf16[16,256,128]{2,1,0:T(8,128)(2,1)} %bitcast.5), calls=%async_computation | async-start | bytes 2097152 | tf_op jit(solution)/shard_map/all_to_all | solution.py:571
  42.0 27.0 %collective-permute-start.9 = (bf16[1136,128]{1,0:T(8,128)(2,1)S(1)}, bf16[1136,128]{1,0:T(8,128)(2,1)S(1)}, u32[]{:S(2)}, u32[]{:S(2)}) collective-permute-start(bf16[1136,128]{1,0:T(8,128)(2,1)S(1)} %get-tuple-element.32), channel_id=1, source_target_pairs={{8,0},{16,8},{24,16},{32,24},{40,32},{48,40},{56,48},{64,56},{72,6... | collective-permute-start | bytes 872456 | tf_op jit(solution)/shard_map/ppermute | solution.py:573
  48.6 24.7 %collective-permute-start.10 = (bf16[1136,128]{1,0:T(8,128)(2,1)S(1)}, bf16[1136,128]{1,0:T(8,128)(2,1)S(1)}, u32[]{:S(2)}, u32[]{:S(2)}) collective-permute-start(bf16[1136,128]{1,0:T(8,128)(2,1)S(1)} %get-tuple-element.33), channel_id=1, source_target_pairs={{16,0},{24,8},{32,16},{40,24},{48,32},{56,40},{64,48},{72,56},{80,... | collective-permute-start | bytes 872456 | tf_op jit(solution)/shard_map/ppermute | solution.py:573
  50.7 22.6 %collective-permute-start.11 = (bf16[1136,128]{1,0:T(8,128)(2,1)S(1)}, bf16[1136,128]{1,0:T(8,128)(2,1)S(1)}, u32[]{:S(2)}, u32[]{:S(2)}) collective-permute-start(bf16[1136,128]{1,0:T(8,128)(2,1)S(1)} %get-tuple-element.34), channel_id=1, source_target_pairs={{24,0},{32,8},{40,16},{48,24},{56,32},{64,40},{72,48},{80,56},{88,... | collective-permute-start | bytes 872456 | tf_op jit(solution)/shard_map/ppermute | solution.py:573
  58.9 21.4 %copy-start.2 = (f32[64]{0:T(128)S(1)}, f32[64]{0:T(128)}, u32[]{:S(2)}) copy-start(f32[64]{0:T(128)} %param.16) | copy-start | bytes 772
  59.1 23.7 %collective-permute-start.8 = (bf16[256,128]{1,0:T(8,128)(2,1)S(1)}, bf16[256,128]{1,0:T(8,128)(2,1)S(1)}, u32[]{:S(2)}, u32[]{:S(2)}) collective-permute-start(bf16[256,128]{1,0:T(8,128)(2,1)S(1)} %get-tuple-element.43), channel_id=1, source_target_pairs={{24,0},{32,8},{40,16},{48,24},{56,32},{64,40},{72,48},{80,56},{88,... | collective-permute-start | bytes 196616 | tf_op jit(solution)/shard_map/ppermute | solution.py:580
  63.8 19.0 %collective-permute-start.7 = (bf16[256,128]{1,0:T(8,128)(2,1)S(1)}, bf16[256,128]{1,0:T(8,128)(2,1)S(1)}, u32[]{:S(2)}, u32[]{:S(2)}) collective-permute-start(bf16[256,128]{1,0:T(8,128)(2,1)S(1)} %get-tuple-element.44), channel_id=1, source_target_pairs={{16,0},{24,8},{32,16},{40,24},{48,32},{56,40},{64,48},{72,56},{80,... | collective-permute-start | bytes 196616 | tf_op jit(solution)/shard_map/ppermute | solution.py:580
  69.0 13.8 %collective-permute-start.6 = (bf16[256,128]{1,0:T(8,128)(2,1)S(1)}, bf16[256,128]{1,0:T(8,128)(2,1)S(1)}, u32[]{:S(2)}, u32[]{:S(2)}) collective-permute-start(bf16[256,128]{1,0:T(8,128)(2,1)S(1)} %get-tuple-element.45), channel_id=1, source_target_pairs={{8,0},{16,8},{24,16},{32,24},{40,32},{48,40},{56,48},{64,56},{72,6... | collective-permute-start | bytes 196616 | tf_op jit(solution)/shard_map/ppermute | solution.py:580
  76.9 10.1 %all-to-all-start.1 = ((bf16[4,256,128]{2,1,0:T(8,128)(2,1)}), bf16[4,256,128]{2,1,0:T(8,128)(2,1)S(1)}, u32[]{:S(2)}, u32[]{:S(2)}) async-start(bf16[4,256,128]{2,1,0:T(8,128)(2,1)} %combine.1), calls=%async_computation.1 | async-start | bytes 524288 | tf_op jit(solution)/shard_map/all_to_all | solution.py:583

commit v6 on v5

--- a/solution.py
+++ b/solution.py
@@ -246,7 +246,15 @@
     )(triples, *blocks, panels)
 
 
-def add_kernel(keep, got, small, first, *second):
+def add_kernel(keep, got, exchange, singles, occ, first, own, one, two, three, small, table):
+    for s in range(3):
+        for row in range(H):
+            lanes = slice(row * 2 * T, (row + 1) * 2 * T)
+            table[s * H + row : s * H + row + 1, :] = exchange[s : s + 1, lanes].astype(F32)
+    heads = [singles[...].astype(F32), jnp.broadcast_to(occ[...].astype(F32), (1, T))]
+    table[3 * H :, :] = jnp.broadcast_to(jnp.concatenate(heads, axis=1), (16, 2 * T))
+    small[...] = table[...].astype(BF16)
+    second = (own, one, two, three)
     for half, outs in ((0, [first]), (1, second)):
         per_out = 16 // len(outs)
         for at, out in enumerate(outs):
@@ -262,7 +270,7 @@
         out[1024:, :] = small[...]
 
 
-def add(keep, got, small):
+def add(keep, got, exchange, singles, occ):
     vmem = pl.BlockSpec(memory_space=pltpu.VMEM)
 
     def rows(count):
@@ -270,12 +278,32 @@
 
     return pl.pallas_call(
         add_kernel,
-        out_shape=(rows(4096), rows(1024)) + (rows(1024 + SMALL_ROWS),) * 3,
-        in_specs=[vmem] * 3,
-        out_specs=[vmem] * 5,
+        out_shape=(rows(4096), rows(1024))
+        + (rows(1024 + SMALL_ROWS),) * 3
+        + (rows(SMALL_ROWS),),
+        in_specs=[vmem] * 5,
+        out_specs=[vmem] * 6,
+        scratch_shapes=[pltpu.VMEM((SMALL_ROWS, 2 * T), F32)],
         compiler_params=pltpu.CompilerParams(vmem_limit_bytes=VMEM_LIMIT),
         name="add",
-    )(keep, got, small)
+    )(keep, got, exchange, singles, occ)
+
+
+def collect_kernel(by_y, out):
+    for d in range(4):
+        out[d] = sum(by_y[source * 4 + d].astype(F32) for source in range(4))
+
+
+def collect(by_y):
+    vmem = pl.BlockSpec(memory_space=pltpu.VMEM)
+    return pl.pallas_call(
+        collect_kernel,
+        out_shape=jax.ShapeDtypeStruct((4, 256, 2 * T), F32),
+        in_specs=[vmem],
+        out_specs=vmem,
+        compiler_params=pltpu.CompilerParams(vmem_limit_bytes=VMEM_LIMIT),
+        name="collect",
+    )(by_y)
 
 
 def gather_terms(mid_is_j, one, two, three, by_j, by_i):
@@ -305,18 +333,22 @@
     return jnp.concatenate(groups, axis=0)
 
 
-def turned_sum(own, by_j, by_i, base, q):
-    low = lane_low(H)
-
-    def as_rows(table):
+def turned_sums(owns, by_j, by_i, base, q):
+    low, low_rows = lane_low(H), lane_low(T)
+
+    def as_rows(table, q):
         even = table[pl.ds(base + 2 * q, H, stride=8), :]
         odd = table[pl.ds(base + 2 * q + 1, H, stride=8), :]
         top = jnp.where(low, even, swap_halves(odd))
         bottom = jnp.where(low, swap_halves(even), odd)
         return jnp.concatenate([top, bottom], axis=0)
 
-    flat = as_rows(by_i).T
-    return own + as_rows(by_j) + jnp.concatenate([flat[:T], flat[T:]], axis=1)
+    flat = jnp.concatenate([as_rows(by_i, q), as_rows(by_i, q + 1)], axis=0).T
+    first, second = flat[:T], flat[T:]
+    return (
+        owns[0] + as_rows(by_j, q) + jnp.where(low_rows, first, swap_halves(second)),
+        owns[1] + as_rows(by_j, q + 1) + jnp.where(low_rows, swap_halves(first), second),
+    )
 
 
 def middle_is_j(triples):
@@ -330,10 +362,14 @@
     gather_terms(middle_is_j(triples), one[rows, :], two[rows, :], three[rows, :], by_j, by_i)
     for part in range(4):
         key = lane_key(part, 8, 2 * T)
-        for q in range(4):
-            tile = own_tile(lambda at: own[part * 256 + at : part * 256 + at + 16, :], key, q)
-            total = turned_sum(tile, by_j, by_i, part * 256, q)
-            out[part, q * T : (q + 1) * T, :] = total.astype(BF16)
+
+        def load(at):
+            return own[part * 256 + at : part * 256 + at + 16, :]
+
+        for q in (0, 2):
+            owns = [own_tile(load, key, q), own_tile(load, key, q + 1)]
+            for at, total in enumerate(turned_sums(owns, by_j, by_i, part * 256, q)):
+                out[part, (q + at) * T : (q + at + 1) * T, :] = total.astype(BF16)
 
 
 def combine(triples, own, one, two, three):
@@ -362,18 +398,21 @@
     wide_key = lane_key(virt // 2, 8, 2 * T)
     key = lane_key(virt // 2, 8, T)
     for q in range(4):
+        if q % 2 == 0:
+            owns = [own_tile(lambda at: own[at : at + 16, :], wide_key, q + at) for at in range(2)]
+            firsts = turned_sums(owns, by_j, by_i, 0, q)
+        first = firsts[q % 2]
         at = slice(q * T, (q + 1) * T)
-        tile = own_tile(lambda at: own[at : at + 16, :], wide_key, q)
-        first = turned_sum(tile, by_j, by_i, 0, q)
         second = sum(others[source, at, :].astype(F32) for source in range(4))
-        for half, tile in ((0, first), (1, second)):
+        flat = jnp.concatenate([first, second], axis=0).T
+        flat_swapped = swap_halves(flat)
+        for half, tile, across in ((0, first, flat), (1, second, flat_swapped)):
             base = (half * 8 + 2 * q) * PART_PITCH
-            flat = tile.T
             plain[base : base + T, :] = tile[:, :T]
-            turned[base : base + T, :] = flat[:T]
+            turned[base : base + T, :] = across[:T, :T]
             base += PART_PITCH
             plain[base : base + T, :] = swap_halves(tile)[:, :T]
-            turned[base : base + T, :] = flat[T:]
+            turned[base : base + T, :] = across[T:, :T]
 
     def exchanged(table, half, c_low):
         groups = []
@@ -389,16 +428,18 @@
 
     sum_b = jnp.zeros((T, T), F32)
     sum_a = jnp.zeros((T, T), F32)
-    for half in range(2):
-        for c_low in range(8):
+    for c_low in range(8):
+        acbs = [exchanged(plain, half, c_low) for half in range(2)]
+        flat = jnp.concatenate(acbs, axis=1).T
+        for half, acb in enumerate(acbs):
             index = half * 8 + c_low
             at = slice(index * T, (index + 1) * T)
-            acb = exchanged(plain, half, c_low)
             cab = exchanged(turned, half, c_low)
+            bca = flat[half * T : (half + 1) * T]
             bac = turned[index * PART_PITCH : index * PART_PITCH + T, :]
             inv = inverse[at, :]
             sum_b += (4.0 * bac + acb) * (bac - cab + extra_b[at, :]) * inv
-            sum_a += bac * (acb - acb.T + extra_a[at, :]) * inv
+            sum_a += bac * (acb - bca + extra_a[at, :]) * inv
     total = jnp.sum(sum_a + sum_b.T, axis=0, keepdims=True)
     total = jnp.where(live, total, 0.0)
     total = jnp.concatenate([total, jnp.zeros_like(total)], axis=1)
@@ -550,16 +591,12 @@
         virt_integrals.reshape(4 * T, T * T), hole_amps.reshape(hole_amps.shape[1:])
     )
 
-    heads = jnp.concatenate([singles, jnp.broadcast_to(occ_energy[:, None], (1, T))], axis=1)
-    small = jnp.concatenate(
-        [exchange_ints.reshape(3 * H, 2 * T), heads, jnp.zeros((15, 2 * T), BF16)], axis=0
-    )
-    panels, small = lax.optimization_barrier((panels, small))
-
     send = terms(1, triples, blocks, panels)
     got = lax.ppermute(send, "virt", CORE_ROUTE)
     keep = terms(0, triples, blocks, panels)
-    first_half, *second_half = add(keep, got, small)
+    first_half, *second_half, small = add(
+        keep, got, exchange_ints.reshape(3, T * T), singles, occ_energy.reshape(1, 1)
+    )
     over_y = functools.partial(
         lax.all_to_all,
         axis_name="virt",
@@ -573,8 +610,7 @@
         lax.ppermute(second_half[d], "trip", shift_route(n_trip, -d)) for d in (1, 2, 3)
     ]
 
-    total = by_y.reshape(4, 4, 256, 2 * T).astype(F32)
-    total = total[0] + total[1] + total[2] + total[3]
+    total = collect(by_y)
     to_share = [total[d].astype(BF16) for d in (1, 2, 3)]
     shares = [
         lax.ppermute(to_share[d - 1], "trip", shift_route(n_trip, -d)) for d in (1, 2, 3)

time: 98.2 us -> 95.4 us (0.971)
  the two profiles are of different devices: /device:TPU:384 before, /device:TPU:227 now
where the time goes in v6:
time: 95.4 us; the launch traced here: 94.7 us
  starting transfers between devices  49.9 us (52%)
  Pallas kernels  19.9 us (21%)
  blocking collectives  11.3 us (12%)
  waiting for transfers between devices  10.8 us (11%)
  local copies, waits for them, and re-layouts  1.35 us (1%)
    all_to_all x1, blocking collectives, local(): everyone = lax.all_to_all(mine, 'virt', 0, 0, tiled=True)  11.3 us
    ppermute x3, starting transfers between devices, local(): lax.ppermute(to_share[d - 1], 'trip', shift_route(n_trip, -d))  9.78 us
    ppermute x3, starting transfers between devices, local(): lax.ppermute(second_half[d], 'trip', shift_route(n_trip, -d))  9.78 us
    ppermute x1, starting transfers between devices, local(): in2 = lax.ppermute(out2, 'trip', shift_route(n_trip, 2))  7.08 us
    pallas_call x2, Pallas kernels, terms(): pl.pallas_call(functools.partial(terms_kernel, rel), out_shape=jax.ShapeD...  6.6 us
    all_to_all x1, waiting for transfers between devices, local(): by_y = over_y(first_half.reshape(16, 256, 2 * T))  4.97 us
    all_to_all x1, starting transfers between devices, local(): by_y = over_y(first_half.reshape(16, 256, 2 * T))  4.31 us
    ppermute x1, starting transfers between devices, local(): got = lax.ppermute(send, 'virt', CORE_ROUTE)  4.21 us
  transfers between devices with their start and end apart: 14, of which 4 were waited for; matrix products, arithmetic and copies ran while one was open for 1% of the time, Pallas kernels for 13%

profile of v6, /device:TPU:227, one launch (start us, length us, event | category | flops | bytes accessed | tf_op | source)
XLA Modules:
  0.0 94.7 jit_solution(9569252839134205686)
XLA Ops:
  0.0 0.0 copy-start.1
  0.0 0.7 copy-done.1
  0.7 1.2 %prep.1 = (bf16[2,144,256]{2,1,0:T(8,128)(2,1)S(1)}, bf16[2,144,256]{2,1,0:T(8,128)(2,1)S(1)}, bf16[2,144,256]{2,1,0:T(8,128)(2,1)S(1)}, bf16[2,144,256]{2,1,0:T(8,128)(2,1)S(1)}, bf16[144,256]{1,0:T(8,128)(2,1)S(1)}) custom-call(s32[2,3]{1,0:T(2,128)S(1)} %copy-done.1, bf16[3,128,256]{2,1,0:T(8,128)(2,1)} %bitcast.22, bf16[3,38,64]{2,1,0:T(8,128)(2,1)} %bitcast.23), custom_call_target="tpu_custom_call" | custom-call | tf_op jit(solution)/shard_map/prep/pallas_call | solution.py:78
  1.9 2.2 %collective-permute-start = (bf16[2,144,256]{2,1,0:T(8,128)(2,1)S(1)}, bf16[2,144,256]{2,1,0:T(8,128)(2,1)S(1)}, u32[]{:S(2)}, u32[]{:S(2)}) collective-permute-start(bf16[2,144,256]{2,1,0:T(8,128)(2,1)S(1)} %get-tuple-element.22), channel_id=1, source_target_pairs={{8,0},{16,8},{24,16},{32,24},{40,32},{48,40},{56,48},{64,56},{72,6... | collective-permute-start | bytes 442376 | tf_op jit(solution)/shard_map/ppermute | solution.py:585
  4.0 3.1 %collective-permute-start.2 = (bf16[2,144,256]{2,1,0:T(8,128)(2,1)S(1)}, bf16[2,144,256]{2,1,0:T(8,128)(2,1)S(1)}, u32[]{:S(2)}, u32[]{:S(2)}) collective-permute-start(bf16[2,144,256]{2,1,0:T(8,128)(2,1)S(1)} %get-tuple-element.24), channel_id=1, source_target_pairs={{0,8},{8,16},{16,24},{24,32},{32,40},{40,48},{48,56},{56,64},{64,7... | collective-permute-start | bytes 442376 | tf_op jit(solution)/shard_map/ppermute | solution.py:586
  7.2 7.1 %collective-permute-start.3 = (bf16[2,144,256]{2,1,0:T(8,128)(2,1)S(1)}, bf16[2,144,256]{2,1,0:T(8,128)(2,1)S(1)}, u32[]{:S(2)}, u32[]{:S(2)}) collective-permute-start(bf16[2,144,256]{2,1,0:T(8,128)(2,1)S(1)} %get-tuple-element.25), channel_id=1, source_target_pairs={{0,16},{8,24},{16,32},{24,40},{32,48},{40,56},{48,64},{56,72},{64,... | collective-permute-start | bytes 442376 | tf_op jit(solution)/shard_map/ppermute | solution.py:584
  14.2 2.3 %collective-permute-start.4 = (bf16[2,144,256]{2,1,0:T(8,128)(2,1)S(1)}, bf16[2,144,256]{2,1,0:T(8,128)(2,1)S(1)}, u32[]{:S(2)}, u32[]{:S(2)}) collective-permute-start(bf16[2,144,256]{2,1,0:T(8,128)(2,1)S(1)} %get-tuple-element.26), channel_id=1, source_target_pairs={{0,24},{8,32},{16,40},{24,48},{32,56},{40,64},{48,72},{56,80},{64,... | collective-permute-start | bytes 442376 | tf_op jit(solution)/shard_map/ppermute | solution.py:587
  16.6 3.0 %collective-permute-start.1 = (bf16[144,256]{1,0:T(8,128)(2,1)S(1)}, bf16[144,256]{1,0:T(8,128)(2,1)S(1)}, u32[]{:S(2)}, u32[]{:S(2)}) collective-permute-start(bf16[144,256]{1,0:T(8,128)(2,1)S(1)} %get-tuple-element.23), channel_id=1, source_target_pairs={{16,0},{24,8},{32,16},{40,24},{48,32},{56,40},{64,48},{72,56},{80,... | collective-permute-start | bytes 221192 | tf_op jit(solution)/shard_map/ppermute | solution.py:583
  19.6 3.8 %panels.1 = bf16[4096,384]{1,0:T(8,128)(2,1)S(1)} custom-call(bf16[256,4096]{1,0:T(8,128)(2,1)} %bitcast.20, bf16[38,4096]{1,0:T(8,128)(2,1)} %bitcast.21), custom_call_target="tpu_custom_call" | custom-call | flops 268435456 | bytes 5242880 | tf_op jit(solution)/shard_map/panels/pallas_call | solution.py:136
  23.3 0.5 collective-permute-done.1.got_two
  23.8 0.0 collective-permute-done.got_one
  23.8 0.0 collective-permute-done.2.in1
  23.8 0.0 collective-permute-done.3.in2
  23.8 0.0 collective-permute-done.4.in3
  23.8 3.3 %terms.3 = bf16[2,16,256,128]{3,2,1,0:T(8,128)(2,1)S(1)} custom-call(s32[2,3]{1,0:T(2,128)S(1)} %copy-done.1, bf16[2,144,256]{2,1,0:T(8,128)(2,1)S(1)} %collective-permute-done.got_one, bf16[144,256]{1,0:T(8,128)(2,1)S(1)} %collective-permute-done.1.got_two, bf16[2,144,256]{2,1,0:T(8,128)(2,1)S(1)} %collective-permute-done.2.in1, ...), custom_call_target="tpu_custom_call" | custom-call | flops 2147483648 | bytes 5242880 | tf_op jit(solution)/shard_map/terms/pallas_call | solution.py:237
  27.1 4.2 %collective-permute-start.5 = (bf16[2,16,256,128]{3,2,1,0:T(8,128)(2,1)S(1)}, bf16[2,16,256,128]{3,2,1,0:T(8,128)(2,1)S(1)}, u32[]{:S(2)}, u32[]{:S(2)}) collective-permute-start(bf16[2,16,256,128]{3,2,1,0:T(8,128)(2,1)S(1)} %terms.3), channel_id=1, source_target_pairs={{0,1},{1,0},{2,3},{3,2},{4,5},{5,4},{6,7},{7,6},{8,9},{9,8},{10,11... | collective-permute-start | bytes 6291464 | tf_op jit(solution)/shard_map/ppermute | solution.py:595
  32.0 0.0 copy-start
  32.0 0.0 copy-start.3
  32.0 3.3 %terms.2.keep = bf16[2,16,256,128]{3,2,1,0:T(8,128)(2,1)S(1)} custom-call(s32[2,3]{1,0:T(2,128)S(1)} %copy-done.1, bf16[2,144,256]{2,1,0:T(8,128)(2,1)S(1)} %collective-permute-done.got_one, bf16[144,256]{1,0:T(8,128)(2,1)S(1)} %collective-permute-done.1.got_two, bf16[2,144,256]{2,1,0:T(8,128)(2,1)S(1)} %collective-permute-done.2.in1, ...), custom_call_target="tpu_custom_call" | custom-call | flops 2147483648 | bytes 5242880 | tf_op jit(solution)/shard_map/terms/pallas_call | solution.py:237
  35.3 0.0 collective-permute-done.5.got
  35.3 0.0 copy-done
  35.4 0.0 copy-done.3
  35.4 1.6 %add.1 = (bf16[4096,128]{1,0:T(8,128)(2,1)}, bf16[1024,128]{1,0:T(8,128)(2,1)S(1)}, bf16[1136,128]{1,0:T(8,128)(2,1)}, bf16[1136,128]{1,0:T(8,128)(2,1)}, bf16[1...) custom-call(bf16[2,16,256,128]{3,2,1,0:T(8,128)(2,1)S(1)} %terms.2.keep, ...), custom_call_target="tpu_custom_call" | custom-call | tf_op jit(solution)/shard_map/add/pallas_call | solution.py:279
  36.9 0.0 copy-start.2
  36.9 4.3 %all-to-all-start = ((bf16[16,256,128]{2,1,0:T(8,128)(2,1)}), bf16[16,256,128]{2,1,0:T(8,128)(2,1)S(1)}, u32[]{:S(2)}, u32[]{:S(2)}) async-start(bf16[16,256,128]{2,1,0:T(8,128)(2,1)} %bitcast.6), calls=%async_computation | async-start | bytes 2097152 | tf_op jit(solution)/shard_map/all_to_all | solution.py:608
  41.2 3.9 %collective-permute-start.9 = (bf16[1136,128]{1,0:T(8,128)(2,1)}, bf16[1136,128]{1,0:T(8,128)(2,1)S(1)}, u32[]{:S(2)}, u32[]{:S(2)}) collective-permute-start(bf16[1136,128]{1,0:T(8,128)(2,1)} %get-tuple-element.29), channel_id=1, source_target_pairs={{8,0},{16,8},{24,16},{32,24},{40,32},{48,40},{56,48},{64,56},{72,6... | collective-permute-start | bytes 872456 | tf_op jit(solution)/shard_map/ppermute | solution.py:610
  45.1 4.0 %collective-permute-start.10 = (bf16[1136,128]{1,0:T(8,128)(2,1)}, bf16[1136,128]{1,0:T(8,128)(2,1)S(1)}, u32[]{:S(2)}, u32[]{:S(2)}) collective-permute-start(bf16[1136,128]{1,0:T(8,128)(2,1)} %get-tuple-element.30), channel_id=1, source_target_pairs={{16,0},{24,8},{32,16},{40,24},{48,32},{56,40},{64,48},{72,56},{80,... | collective-permute-start | bytes 872456 | tf_op jit(solution)/shard_map/ppermute | solution.py:610
  49.1 0.0 copy-start.4
  49.1 1.9 %collective-permute-start.11 = (bf16[1136,128]{1,0:T(8,128)(2,1)S(1)}, bf16[1136,128]{1,0:T(8,128)(2,1)S(1)}, u32[]{:S(2)}, u32[]{:S(2)}) collective-permute-start(bf16[1136,128]{1,0:T(8,128)(2,1)S(1)} %get-tuple-element.31), channel_id=1, source_target_pairs={{24,0},{32,8},{40,16},{48,24},{56,32},{64,40},{72,48},{80,56},{88,... | collective-permute-start | bytes 872456 | tf_op jit(solution)/shard_map/ppermute | solution.py:610
  51.1 5.0 %all-to-all-done.by_y = bf16[16,256,128]{2,1,0:T(8,128)(2,1)S(1)} async-done(((bf16[16,256,128]{2,1,0:T(8,128)(2,1)}), bf16[16,256,128]{2,1,0:T(8,128)(2,1)S(1)}, u32[]{:S(2)}, u32[]{:S(2)}) %all-to-all-start) | async-done | bytes 1048608 | tf_op jit(solution)/shard_map/all_to_all | solution.py:608
  56.0 0.1 collect.1
  56.2 0.6 slice_bitcast_fusion.1
  56.8 3.9 %collective-permute-start.6 = (bf16[256,128]{1,0:T(8,128)(2,1)}, bf16[256,128]{1,0:T(8,128)(2,1)S(1)}, u32[]{:S(2)}, u32[]{:S(2)}) collective-permute-start(bf16[256,128]{1,0:T(8,128)(2,1)} %get-tuple-element.41), channel_id=1, source_target_pairs={{8,0},{16,8},{24,16},{32,24},{40,32},{48,40},{56,48},{64,56},{72,6... | collective-permute-start | bytes 196616 | tf_op jit(solution)/shard_map/ppermute | solution.py:616
  60.7 4.0 %collective-permute-start.7 = (bf16[256,128]{1,0:T(8,128)(2,1)S(1)}, bf16[256,128]{1,0:T(8,128)(2,1)S(1)}, u32[]{:S(2)}, u32[]{:S(2)}) collective-permute-start(bf16[256,128]{1,0:T(8,128)(2,1)S(1)} %get-tuple-element.40), channel_id=1, source_target_pairs={{16,0},{24,8},{32,16},{40,24},{48,32},{56,40},{64,48},{72,56},{80,... | collective-permute-start | bytes 196616 | tf_op jit(solution)/shard_map/ppermute | solution.py:616
  64.7 0.0 collective-permute-done.9.one
  64.7 1.9 %collective-permute-start.8 = (bf16[256,128]{1,0:T(8,128)(2,1)S(1)}, bf16[256,128]{1,0:T(8,128)(2,1)S(1)}, u32[]{:S(2)}, u32[]{:S(2)}) collective-permute-start(bf16[256,128]{1,0:T(8,128)(2,1)S(1)} %get-tuple-element.39), channel_id=1, source_target_pairs={{24,0},{32,8},{40,16},{48,24},{56,32},{64,40},{72,48},{80,56},{88,... | collective-permute-start | bytes 196616 | tf_op jit(solution)/shard_map/ppermute | solution.py:616
  66.6 0.0 collective-permute-done.10.two
  66.7 2.2 %collective-permute-done.11.three = bf16[1136,128]{1,0:T(8,128)(2,1)S(1)} collective-permute-done((bf16[1136,128]{1,0:T(8,128)(2,1)S(1)}, bf16[1136,128]{1,0:T(8,128)(2,1)S(1)}, u32[]{:S(2)}, u32[]{:S(2)}) %collective-permute-start.11) | collective-permute-done | bytes 290848 | tf_op jit(solution)/shard_map/ppermute | solution.py:610
  68.9 0.0 copy-done.2
  68.9 2.5 %combine.1 = bf16[4,256,128]{2,1,0:T(8,128)(2,1)} custom-call(s32[2,3]{1,0:T(2,128)S(1)} %copy-done.2, bf16[1024,128]{1,0:T(8,128)(2,1)S(1)} %get-tuple-element.28.own, bf16[1136,128]{1,0:T(8,128)(2,1)S(1)} %collective-permute-done.9.one, bf16[1136,128]{1,0:T(8,128)(2,1)S(1)} %collective-permute-done.10.two, bf16[1136,128]{1,0:T(8,128)(2,1)S(1)} %collective-permute-done.11.three), custom_call_target="tpu_custom_call" | custom-call | tf_op jit(solution)/shard_map/combine/pallas_call | solution.py:377
  71.4 4.1 %all-to-all-start.1 = ((bf16[4,256,128]{2,1,0:T(8,128)(2,1)}), bf16[4,256,128]{2,1,0:T(8,128)(2,1)S(1)}, u32[]{:S(2)}, u32[]{:S(2)}) async-start(bf16[4,256,128]{2,1,0:T(8,128)(2,1)} %combine.1), calls=%async_computation.1 | async-start | bytes 524288 | tf_op jit(solution)/shard_map/all_to_all | solution.py:619
  75.6 0.0 copy-done.4
  75.6 2.4 %tables.1 = (f32[1024,64]{1,0:T(8,128)S(1)}, f32[1024,64]{1,0:T(8,128)S(1)}, f32[1024,64]{1,0:T(8,128)S(1)}) custom-call(s32[2,3]{1,0:T(2,128)S(1)} %copy-done.2, bf16[112,128]{1,0:T(8,128)(2,1)S(1)} %get-tuple-element.35.own, bf16[1136,128]{1,0:T(8,128)(2,1)S(1)} %collective-permute-done.9.one, bf16[1136,128]{1,0:T(8,128)(2,1)S(1)} %collective-permute-done.10.two, ...), custom_call_target="tpu_custom_call" | custom-call | flops 268435456 | bytes 3145728 | tf_op jit(solution)/shard_map/tables/pallas_call | solution.py:555
  78.0 0.0 collective-permute-done.6.one
  78.0 0.0 collective-permute-done.7.two
  78.0 0.0 collective-permute-done.8.three
  78.0 3.1 %all-to-all-done.1.others = bf16[4,256,128]{2,1,0:T(8,128)(2,1)S(1)} async-done(((bf16[4,256,128]{2,1,0:T(8,128)(2,1)}), bf16[4,256,128]{2,1,0:T(8,128)(2,1)S(1)}, u32[]{:S(2)}, u32[]{:S(2)}) %all-to-all-start.1) | async-done | bytes 262176 | tf_op jit(solution)/shard_map/all_to_all | solution.py:619
  81.1 1.7 %energy.1 = f32[8,8,128]{2,1,0:T(8,128)S(1)} custom-call(s32[2,3]{1,0:T(2,128)S(1)} %copy-done.2, f32[256,128]{1,0:T(8,128)S(1)} %slice_bitcast_fusion.own, bf16[256,128]{1,0:T(8,128)(2,1)S(1)} %collective-permute-done.6.one, bf16[256,128]{1,0:T(8,128)(2,1)S(1)} %collective-permute-done.7.two, bf16[256,128]{1,0:T(8,128)(2,1)S(1)} %collective-permute-done.8.three, ...), custom_call_target="tpu_custom_call" | custom-call | tf_op jit(solution)/shard_map/energy/pallas_call | solution.py:451
  82.8 11.3 %all_to_all.15 = f32[8,8,128]{2,1,0:T(8,128)S(1)} all-to-all(f32[8,8,128]{2,1,0:T(8,128)S(1)} %energy.1), channel_id=1, replica_groups=mesh['trip'=64,'virt'=8] {'virt'}, dimensions={0} | all-to-all | bytes 65536 | tf_op jit(solution)/shard_map/all_to_all | solution.py:623
  94.1 0.6 reduce_sum.9
  (3 shorter events, 0.1 us)
Async XLA Ops:
  0.0 0.7 copy-start.1
  1.9 21.9 %collective-permute-start = (bf16[2,144,256]{2,1,0:T(8,128)(2,1)S(1)}, bf16[2,144,256]{2,1,0:T(8,128)(2,1)S(1)}, u32[]{:S(2)}, u32[]{:S(2)}) collective-permute-start(bf16[2,144,256]{2,1,0:T(8,128)(2,1)S(1)} %get-tuple-element.22), channel_id=1, source_target_pairs={{8,0},{16,8},{24,16},{32,24},{40,32},{48,40},{56,48},{64,56},{72,6... | collective-permute-start | bytes 442376 | tf_op jit(solution)/shard_map/ppermute | solution.py:585
  4.0 19.8 %collective-permute-start.2 = (bf16[2,144,256]{2,1,0:T(8,128)(2,1)S(1)}, bf16[2,144,256]{2,1,0:T(8,128)(2,1)S(1)}, u32[]{:S(2)}, u32[]{:S(2)}) collective-permute-start(bf16[2,144,256]{2,1,0:T(8,128)(2,1)S(1)} %get-tuple-element.24), channel_id=1, source_target_pairs={{0,8},{8,16},{16,24},{24,32},{32,40},{40,48},{48,56},{56,64},{64,7... | collective-permute-start | bytes 442376 | tf_op jit(solution)/shard_map/ppermute | solution.py:586
  7.2 16.6 %collective-permute-start.3 = (bf16[2,144,256]{2,1,0:T(8,128)(2,1)S(1)}, bf16[2,144,256]{2,1,0:T(8,128)(2,1)S(1)}, u32[]{:S(2)}, u32[]{:S(2)}) collective-permute-start(bf16[2,144,256]{2,1,0:T(8,128)(2,1)S(1)} %get-tuple-element.25), channel_id=1, source_target_pairs={{0,16},{8,24},{16,32},{24,40},{32,48},{40,56},{48,64},{56,72},{64,... | collective-permute-start | bytes 442376 | tf_op jit(solution)/shard_map/ppermute | solution.py:584
  14.2 9.6 %collective-permute-start.4 = (bf16[2,144,256]{2,1,0:T(8,128)(2,1)S(1)}, bf16[2,144,256]{2,1,0:T(8,128)(2,1)S(1)}, u32[]{:S(2)}, u32[]{:S(2)}) collective-permute-start(bf16[2,144,256]{2,1,0:T(8,128)(2,1)S(1)} %get-tuple-element.26), channel_id=1, source_target_pairs={{0,24},{8,32},{16,40},{24,48},{32,56},{40,64},{48,72},{56,80},{64,... | collective-permute-start | bytes 442376 | tf_op jit(solution)/shard_map/ppermute | solution.py:587
  16.6 7.2 %collective-permute-start.1 = (bf16[144,256]{1,0:T(8,128)(2,1)S(1)}, bf16[144,256]{1,0:T(8,128)(2,1)S(1)}, u32[]{:S(2)}, u32[]{:S(2)}) collective-permute-start(bf16[144,256]{1,0:T(8,128)(2,1)S(1)} %get-tuple-element.23), channel_id=1, source_target_pairs={{16,0},{24,8},{32,16},{40,24},{48,32},{56,40},{64,48},{72,56},{80,... | collective-permute-start | bytes 221192 | tf_op jit(solution)/shard_map/ppermute | solution.py:583
  27.1 8.2 %collective-permute-start.5 = (bf16[2,16,256,128]{3,2,1,0:T(8,128)(2,1)S(1)}, bf16[2,16,256,128]{3,2,1,0:T(8,128)(2,1)S(1)}, u32[]{:S(2)}, u32[]{:S(2)}) collective-permute-start(bf16[2,16,256,128]{3,2,1,0:T(8,128)(2,1)S(1)} %terms.3), channel_id=1, source_target_pairs={{0,1},{1,0},{2,3},{3,2},{4,5},{5,4},{6,7},{7,6},{8,9},{9,8},{10,11... | collective-permute-start | bytes 6291464 | tf_op jit(solution)/shard_map/ppermute | solution.py:595
  32.0 3.3 %copy-start = (bf16[1,3,4096]{2,1,0:T(4,128)(2,1)S(1)}, bf16[1,3,4096]{2,1,0:T(4,128)(2,1)}, u32[]{:S(2)}) copy-start(bf16[1,3,4096]{2,1,0:T(4,128)(2,1)} %param.13) | copy-start | bytes 73732
  32.0 3.3 %copy-start.3 = (bf16[1,64]{1,0:T(2,128)(2,1)S(1)}, bf16[1,64]{1,0:T(2,128)(2,1)}, u32[]{:S(2)}) copy-start(bf16[1,64]{1,0:T(2,128)(2,1)} %singles.1) | copy-start | bytes 388
  36.9 32.0 %copy-start.2 = (s32[2,3]{1,0:T(2,128)S(1)}, s32[2,3]{1,0:T(2,128)}, u32[]{:S(2)}) copy-start(s32[2,3]{1,0:T(2,128)} %triples.11) | copy-start | bytes 76
  36.9 19.1 %all-to-all-start = ((bf16[16,256,128]{2,1,0:T(8,128)(2,1)}), bf16[16,256,128]{2,1,0:T(8,128)(2,1)S(1)}, u32[]{:S(2)}, u32[]{:S(2)}) async-start(bf16[16,256,128]{2,1,0:T(8,128)(2,1)} %bitcast.6), calls=%async_computation | async-start | bytes 2097152 | tf_op jit(solution)/shard_map/all_to_all | solution.py:608
  41.2 23.5 %collective-permute-start.9 = (bf16[1136,128]{1,0:T(8,128)(2,1)}, bf16[1136,128]{1,0:T(8,128)(2,1)S(1)}, u32[]{:S(2)}, u32[]{:S(2)}) collective-permute-start(bf16[1136,128]{1,0:T(8,128)(2,1)} %get-tuple-element.29), channel_id=1, source_target_pairs={{8,0},{16,8},{24,16},{32,24},{40,32},{48,40},{56,48},{64,56},{72,6... | collective-permute-start | bytes 872456 | tf_op jit(solution)/shard_map/ppermute | solution.py:610
  45.1 21.5 %collective-permute-start.10 = (bf16[1136,128]{1,0:T(8,128)(2,1)}, bf16[1136,128]{1,0:T(8,128)(2,1)S(1)}, u32[]{:S(2)}, u32[]{:S(2)}) collective-permute-start(bf16[1136,128]{1,0:T(8,128)(2,1)} %get-tuple-element.30), channel_id=1, source_target_pairs={{16,0},{24,8},{32,16},{40,24},{48,32},{56,40},{64,48},{72,56},{80,... | collective-permute-start | bytes 872456 | tf_op jit(solution)/shard_map/ppermute | solution.py:610
  49.1 26.5 %copy-start.4 = (f32[64]{0:T(128)S(1)}, f32[64]{0:T(128)}, u32[]{:S(2)}) copy-start(f32[64]{0:T(128)} %param.16) | copy-start | bytes 772
  49.1 19.8 %collective-permute-start.11 = (bf16[1136,128]{1,0:T(8,128)(2,1)S(1)}, bf16[1136,128]{1,0:T(8,128)(2,1)S(1)}, u32[]{:S(2)}, u32[]{:S(2)}) collective-permute-start(bf16[1136,128]{1,0:T(8,128)(2,1)S(1)} %get-tuple-element.31), channel_id=1, source_target_pairs={{24,0},{32,8},{40,16},{48,24},{56,32},{64,40},{72,48},{80,56},{88,... | collective-permute-start | bytes 872456 | tf_op jit(solution)/shard_map/ppermute | solution.py:610
  56.8 21.2 %collective-permute-start.6 = (bf16[256,128]{1,0:T(8,128)(2,1)}, bf16[256,128]{1,0:T(8,128)(2,1)S(1)}, u32[]{:S(2)}, u32[]{:S(2)}) collective-permute-start(bf16[256,128]{1,0:T(8,128)(2,1)} %get-tuple-element.41), channel_id=1, source_target_pairs={{8,0},{16,8},{24,16},{32,24},{40,32},{48,40},{56,48},{64,56},{72,6... | collective-permute-start | bytes 196616 | tf_op jit(solution)/shard_map/ppermute | solution.py:616
  60.7 17.3 %collective-permute-start.7 = (bf16[256,128]{1,0:T(8,128)(2,1)S(1)}, bf16[256,128]{1,0:T(8,128)(2,1)S(1)}, u32[]{:S(2)}, u32[]{:S(2)}) collective-permute-start(bf16[256,128]{1,0:T(8,128)(2,1)S(1)} %get-tuple-element.40), channel_id=1, source_target_pairs={{16,0},{24,8},{32,16},{40,24},{48,32},{56,40},{64,48},{72,56},{80,... | collective-permute-start | bytes 196616 | tf_op jit(solution)/shard_map/ppermute | solution.py:616
  64.7 13.3 %collective-permute-start.8 = (bf16[256,128]{1,0:T(8,128)(2,1)S(1)}, bf16[256,128]{1,0:T(8,128)(2,1)S(1)}, u32[]{:S(2)}, u32[]{:S(2)}) collective-permute-start(bf16[256,128]{1,0:T(8,128)(2,1)S(1)} %get-tuple-element.39), channel_id=1, source_target_pairs={{24,0},{32,8},{40,16},{48,24},{56,32},{64,40},{72,48},{80,56},{88,... | collective-permute-start | bytes 196616 | tf_op jit(solution)/shard_map/ppermute | solution.py:616
  71.4 9.7 %all-to-all-start.1 = ((bf16[4,256,128]{2,1,0:T(8,128)(2,1)}), bf16[4,256,128]{2,1,0:T(8,128)(2,1)S(1)}, u32[]{:S(2)}, u32[]{:S(2)}) async-start(bf16[4,256,128]{2,1,0:T(8,128)(2,1)} %combine.1), calls=%async_computation.1 | async-start | bytes 524288 | tf_op jit(solution)/shard_map/all_to_all | solution.py:619

commit v7 on v6

--- a/solution.py
+++ b/solution.py
@@ -138,7 +138,7 @@
         out_shape=jax.ShapeDtypeStruct((T * T, DEPTH), BF16),
         in_specs=[pl.BlockSpec(memory_space=pltpu.HBM), pl.BlockSpec()],
         out_specs=pl.BlockSpec(memory_space=pltpu.VMEM),
-        scratch_shapes=[pltpu.VMEM((H * PITCH, 2 * T), F32)] * 2
+        scratch_shapes=[pltpu.VMEM(((H + 1) * PITCH, 2 * T), F32)] * 2
         + [
             pltpu.VMEM(integrals.shape, BF16),
             pltpu.SemaphoreType.DMA((STEPS,)),
@@ -308,8 +308,9 @@
 
 def gather_terms(mid_is_j, one, two, three, by_j, by_i):
     middle = two.astype(F32)
-    by_j[...] = one.astype(F32) + jnp.where(mid_is_j, middle, 0.0)
-    by_i[...] = three.astype(F32) + jnp.where(mid_is_j, 0.0, middle)
+    rows = slice(0, one.shape[0])
+    by_j[rows, :] = one.astype(F32) + jnp.where(mid_is_j, middle, 0.0)
+    by_i[rows, :] = three.astype(F32) + jnp.where(mid_is_j, 0.0, middle)
 
 
 def lane_key(part, rows, lanes):
@@ -379,14 +380,14 @@
         out_shape=jax.ShapeDtypeStruct((4, 256, 2 * T), BF16),
         in_specs=[pl.BlockSpec(memory_space=pltpu.SMEM)] + [vmem] * 4,
         out_specs=vmem,
-        scratch_shapes=[pltpu.VMEM((1024, 2 * T), F32)] * 2,
+        scratch_shapes=[pltpu.VMEM((1024 + 8, 2 * T), F32)] * 2,
         compiler_params=pltpu.CompilerParams(vmem_limit_bytes=VMEM_LIMIT),
         name="combine",
     )(triples, own, one, two, three)
 
 
 PART_PITCH = T + 8
-PART_ROWS = 16 * PART_PITCH
+PART_ROWS = 17 * PART_PITCH
 
 
 def energy_kernel(
@@ -453,7 +454,7 @@
         out_shape=jax.ShapeDtypeStruct((8, 8, 2 * T), F32),
         in_specs=[pl.BlockSpec(memory_space=pltpu.SMEM)] + [vmem] * 8,
         out_specs=vmem,
-        scratch_shapes=[pltpu.VMEM((256, 2 * T), F32)] * 2 + [pltpu.VMEM((PART_ROWS, T), F32)] * 2,
+        scratch_shapes=[pltpu.VMEM((256 + 8, 2 * T), F32)] * 2 + [pltpu.VMEM((PART_ROWS, T), F32)] * 2,
         compiler_params=pltpu.CompilerParams(vmem_limit_bytes=VMEM_LIMIT),
         name="energy",
     )(triples, own, *shares, others, extra_b, extra_a, inverse)
@@ -557,7 +558,7 @@
         out_shape=(table, table, table),
         in_specs=[pl.BlockSpec(memory_space=pltpu.SMEM)] + [vmem] * 5,
         out_specs=[vmem] * 3,
-        scratch_shapes=[pltpu.VMEM((rows * T, T), F32) for rows in (4, 8, 6)],
+        scratch_shapes=[pltpu.VMEM((rows * T + 8, T), F32) for rows in (4, 8, 6)],
         compiler_params=pltpu.CompilerParams(vmem_limit_bytes=VMEM_LIMIT),
         cost_estimate=pl.CostEstimate(flops=1 << 28, bytes_accessed=3 << 20, transcendentals=0),
         name="tables",

time: 95.4 us -> 95.4 us (level)
  no operation moved by 1% of the time
where the time goes in v7:
time: 95.4 us; the launch traced here: 94.7 us
  starting transfers between devices  49.8 us (52%)
  Pallas kernels  19.9 us (21%)
  blocking collectives  11.3 us (12%)
  waiting for transfers between devices  10.8 us (11%)
  local copies, waits for them, and re-layouts  1.35 us (1%)
    all_to_all x1, blocking collectives, local(): everyone = lax.all_to_all(mine, 'virt', 0, 0, tiled=True)  11.3 us
    ppermute x3, starting transfers between devices, local(): lax.ppermute(to_share[d - 1], 'trip', shift_route(n_trip, -d))  9.77 us
    ppermute x3, starting transfers between devices, local(): lax.ppermute(second_half[d], 'trip', shift_route(n_trip, -d))  9.77 us
    ppermute x1, starting transfers between devices, local(): in2 = lax.ppermute(out2, 'trip', shift_route(n_trip, 2))  7.07 us
    pallas_call x2, Pallas kernels, terms(): pl.pallas_call(functools.partial(terms_kernel, rel), out_shape=jax.ShapeD...  6.6 us
    all_to_all x1, waiting for transfers between devices, local(): by_y = over_y(first_half.reshape(16, 256, 2 * T))  4.98 us
    all_to_all x1, starting transfers between devices, local(): by_y = over_y(first_half.reshape(16, 256, 2 * T))  4.31 us
    ppermute x1, starting transfers between devices, local(): got = lax.ppermute(send, 'virt', CORE_ROUTE)  4.22 us
  transfers between devices with their start and end apart: 14, of which 4 were waited for; matrix products, arithmetic and copies ran while one was open for 1% of the time, Pallas kernels for 13%

profile of v7, /device:TPU:227, one launch (start us, length us, event | category | flops | bytes accessed | tf_op | source)
XLA Modules:
  0.0 94.7 jit_solution(13128511667436186469)
XLA Ops:
  0.0 0.0 copy-start.1
  0.0 0.7 copy-done.1
  0.7 1.2 %prep.1 = (bf16[2,144,256]{2,1,0:T(8,128)(2,1)S(1)}, bf16[2,144,256]{2,1,0:T(8,128)(2,1)S(1)}, bf16[2,144,256]{2,1,0:T(8,128)(2,1)S(1)}, bf16[2,144,256]{2,1,0:T(8,128)(2,1)S(1)}, bf16[144,256]{1,0:T(8,128)(2,1)S(1)}) custom-call(s32[2,3]{1,0:T(2,128)S(1)} %copy-done.1, bf16[3,128,256]{2,1,0:T(8,128)(2,1)} %bitcast.22, bf16[3,38,64]{2,1,0:T(8,128)(2,1)} %bitcast.23), custom_call_target="tpu_custom_call" | custom-call | tf_op jit(solution)/shard_map/prep/pallas_call | solution.py:78
  1.9 2.2 %collective-permute-start = (bf16[2,144,256]{2,1,0:T(8,128)(2,1)S(1)}, bf16[2,144,256]{2,1,0:T(8,128)(2,1)S(1)}, u32[]{:S(2)}, u32[]{:S(2)}) collective-permute-start(bf16[2,144,256]{2,1,0:T(8,128)(2,1)S(1)} %get-tuple-element.22), channel_id=1, source_target_pairs={{8,0},{16,8},{24,16},{32,24},{40,32},{48,40},{56,48},{64,56},{72,6... | collective-permute-start | bytes 442376 | tf_op jit(solution)/shard_map/ppermute | solution.py:586
  4.0 3.1 %collective-permute-start.2 = (bf16[2,144,256]{2,1,0:T(8,128)(2,1)S(1)}, bf16[2,144,256]{2,1,0:T(8,128)(2,1)S(1)}, u32[]{:S(2)}, u32[]{:S(2)}) collective-permute-start(bf16[2,144,256]{2,1,0:T(8,128)(2,1)S(1)} %get-tuple-element.24), channel_id=1, source_target_pairs={{0,8},{8,16},{16,24},{24,32},{32,40},{40,48},{48,56},{56,64},{64,7... | collective-permute-start | bytes 442376 | tf_op jit(solution)/shard_map/ppermute | solution.py:587
  7.2 7.1 %collective-permute-start.3 = (bf16[2,144,256]{2,1,0:T(8,128)(2,1)S(1)}, bf16[2,144,256]{2,1,0:T(8,128)(2,1)S(1)}, u32[]{:S(2)}, u32[]{:S(2)}) collective-permute-start(bf16[2,144,256]{2,1,0:T(8,128)(2,1)S(1)} %get-tuple-element.25), channel_id=1, source_target_pairs={{0,16},{8,24},{16,32},{24,40},{32,48},{40,56},{48,64},{56,72},{64,... | collective-permute-start | bytes 442376 | tf_op jit(solution)/shard_map/ppermute | solution.py:585
  14.2 2.3 %collective-permute-start.4 = (bf16[2,144,256]{2,1,0:T(8,128)(2,1)S(1)}, bf16[2,144,256]{2,1,0:T(8,128)(2,1)S(1)}, u32[]{:S(2)}, u32[]{:S(2)}) collective-permute-start(bf16[2,144,256]{2,1,0:T(8,128)(2,1)S(1)} %get-tuple-element.26), channel_id=1, source_target_pairs={{0,24},{8,32},{16,40},{24,48},{32,56},{40,64},{48,72},{56,80},{64,... | collective-permute-start | bytes 442376 | tf_op jit(solution)/shard_map/ppermute | solution.py:588
  16.6 3.0 %collective-permute-start.1 = (bf16[144,256]{1,0:T(8,128)(2,1)S(1)}, bf16[144,256]{1,0:T(8,128)(2,1)S(1)}, u32[]{:S(2)}, u32[]{:S(2)}) collective-permute-start(bf16[144,256]{1,0:T(8,128)(2,1)S(1)} %get-tuple-element.23), channel_id=1, source_target_pairs={{16,0},{24,8},{32,16},{40,24},{48,32},{56,40},{64,48},{72,56},{80,... | collective-permute-start | bytes 221192 | tf_op jit(solution)/shard_map/ppermute | solution.py:584
  19.6 3.8 %panels.1 = bf16[4096,384]{1,0:T(8,128)(2,1)S(1)} custom-call(bf16[256,4096]{1,0:T(8,128)(2,1)} %bitcast.20, bf16[38,4096]{1,0:T(8,128)(2,1)} %bitcast.21), custom_call_target="tpu_custom_call" | custom-call | flops 268435456 | bytes 5242880 | tf_op jit(solution)/shard_map/panels/pallas_call | solution.py:136
  23.3 0.5 collective-permute-done.1.got_two
  23.8 0.0 collective-permute-done.got_one
  23.8 0.0 collective-permute-done.2.in1
  23.8 0.0 collective-permute-done.3.in2
  23.8 0.0 collective-permute-done.4.in3
  23.8 3.3 %terms.3 = bf16[2,16,256,128]{3,2,1,0:T(8,128)(2,1)S(1)} custom-call(s32[2,3]{1,0:T(2,128)S(1)} %copy-done.1, bf16[2,144,256]{2,1,0:T(8,128)(2,1)S(1)} %collective-permute-done.got_one, bf16[144,256]{1,0:T(8,128)(2,1)S(1)} %collective-permute-done.1.got_two, bf16[2,144,256]{2,1,0:T(8,128)(2,1)S(1)} %collective-permute-done.2.in1, ...), custom_call_target="tpu_custom_call" | custom-call | flops 2147483648 | bytes 5242880 | tf_op jit(solution)/shard_map/terms/pallas_call | solution.py:237
  27.1 4.2 %collective-permute-start.5 = (bf16[2,16,256,128]{3,2,1,0:T(8,128)(2,1)S(1)}, bf16[2,16,256,128]{3,2,1,0:T(8,128)(2,1)S(1)}, u32[]{:S(2)}, u32[]{:S(2)}) collective-permute-start(bf16[2,16,256,128]{3,2,1,0:T(8,128)(2,1)S(1)} %terms.3), channel_id=1, source_target_pairs={{0,1},{1,0},{2,3},{3,2},{4,5},{5,4},{6,7},{7,6},{8,9},{9,8},{10,11... | collective-permute-start | bytes 6291464 | tf_op jit(solution)/shard_map/ppermute | solution.py:596
  32.0 0.0 copy-start
  32.0 0.0 copy-start.3
  32.0 3.3 %terms.2.keep = bf16[2,16,256,128]{3,2,1,0:T(8,128)(2,1)S(1)} custom-call(s32[2,3]{1,0:T(2,128)S(1)} %copy-done.1, bf16[2,144,256]{2,1,0:T(8,128)(2,1)S(1)} %collective-permute-done.got_one, bf16[144,256]{1,0:T(8,128)(2,1)S(1)} %collective-permute-done.1.got_two, bf16[2,144,256]{2,1,0:T(8,128)(2,1)S(1)} %collective-permute-done.2.in1, ...), custom_call_target="tpu_custom_call" | custom-call | flops 2147483648 | bytes 5242880 | tf_op jit(solution)/shard_map/terms/pallas_call | solution.py:237
  35.3 0.0 collective-permute-done.5.got
  35.4 0.0 copy-done
  35.4 0.0 copy-done.3
  35.4 1.6 %add.1 = (bf16[4096,128]{1,0:T(8,128)(2,1)}, bf16[1024,128]{1,0:T(8,128)(2,1)S(1)}, bf16[1136,128]{1,0:T(8,128)(2,1)}, bf16[1136,128]{1,0:T(8,128)(2,1)}, bf16[1...) custom-call(bf16[2,16,256,128]{3,2,1,0:T(8,128)(2,1)S(1)} %terms.2.keep, ...), custom_call_target="tpu_custom_call" | custom-call | tf_op jit(solution)/shard_map/add/pallas_call | solution.py:279
  36.9 0.0 copy-start.2
  36.9 4.3 %all-to-all-start = ((bf16[16,256,128]{2,1,0:T(8,128)(2,1)}), bf16[16,256,128]{2,1,0:T(8,128)(2,1)S(1)}, u32[]{:S(2)}, u32[]{:S(2)}) async-start(bf16[16,256,128]{2,1,0:T(8,128)(2,1)} %bitcast.6), calls=%async_computation | async-start | bytes 2097152 | tf_op jit(solution)/shard_map/all_to_all | solution.py:609
  41.2 3.9 %collective-permute-start.9 = (bf16[1136,128]{1,0:T(8,128)(2,1)}, bf16[1136,128]{1,0:T(8,128)(2,1)S(1)}, u32[]{:S(2)}, u32[]{:S(2)}) collective-permute-start(bf16[1136,128]{1,0:T(8,128)(2,1)} %get-tuple-element.29), channel_id=1, source_target_pairs={{8,0},{16,8},{24,16},{32,24},{40,32},{48,40},{56,48},{64,56},{72,6... | collective-permute-start | bytes 872456 | tf_op jit(solution)/shard_map/ppermute | solution.py:611
  45.1 4.0 %collective-permute-start.10 = (bf16[1136,128]{1,0:T(8,128)(2,1)}, bf16[1136,128]{1,0:T(8,128)(2,1)S(1)}, u32[]{:S(2)}, u32[]{:S(2)}) collective-permute-start(bf16[1136,128]{1,0:T(8,128)(2,1)} %get-tuple-element.30), channel_id=1, source_target_pairs={{16,0},{24,8},{32,16},{40,24},{48,32},{56,40},{64,48},{72,56},{80,... | collective-permute-start | bytes 872456 | tf_op jit(solution)/shard_map/ppermute | solution.py:611
  49.1 0.0 copy-start.4
  49.1 1.9 %collective-permute-start.11 = (bf16[1136,128]{1,0:T(8,128)(2,1)S(1)}, bf16[1136,128]{1,0:T(8,128)(2,1)S(1)}, u32[]{:S(2)}, u32[]{:S(2)}) collective-permute-start(bf16[1136,128]{1,0:T(8,128)(2,1)S(1)} %get-tuple-element.31), channel_id=1, source_target_pairs={{24,0},{32,8},{40,16},{48,24},{56,32},{64,40},{72,48},{80,56},{88,... | collective-permute-start | bytes 872456 | tf_op jit(solution)/shard_map/ppermute | solution.py:611
  51.0 5.0 %all-to-all-done.by_y = bf16[16,256,128]{2,1,0:T(8,128)(2,1)S(1)} async-done(((bf16[16,256,128]{2,1,0:T(8,128)(2,1)}), bf16[16,256,128]{2,1,0:T(8,128)(2,1)S(1)}, u32[]{:S(2)}, u32[]{:S(2)}) %all-to-all-start) | async-done | bytes 1048608 | tf_op jit(solution)/shard_map/all_to_all | solution.py:609
  56.0 0.1 collect.1
  56.2 0.6 slice_bitcast_fusion.1
  56.8 3.9 %collective-permute-start.6 = (bf16[256,128]{1,0:T(8,128)(2,1)}, bf16[256,128]{1,0:T(8,128)(2,1)S(1)}, u32[]{:S(2)}, u32[]{:S(2)}) collective-permute-start(bf16[256,128]{1,0:T(8,128)(2,1)} %get-tuple-element.41), channel_id=1, source_target_pairs={{8,0},{16,8},{24,16},{32,24},{40,32},{48,40},{56,48},{64,56},{72,6... | collective-permute-start | bytes 196616 | tf_op jit(solution)/shard_map/ppermute | solution.py:617
  60.7 4.0 %collective-permute-start.7 = (bf16[256,128]{1,0:T(8,128)(2,1)S(1)}, bf16[256,128]{1,0:T(8,128)(2,1)S(1)}, u32[]{:S(2)}, u32[]{:S(2)}) collective-permute-start(bf16[256,128]{1,0:T(8,128)(2,1)S(1)} %get-tuple-element.40), channel_id=1, source_target_pairs={{16,0},{24,8},{32,16},{40,24},{48,32},{56,40},{64,48},{72,56},{80,... | collective-permute-start | bytes 196616 | tf_op jit(solution)/shard_map/ppermute | solution.py:617
  64.7 0.0 collective-permute-done.9.one
  64.7 1.9 %collective-permute-start.8 = (bf16[256,128]{1,0:T(8,128)(2,1)S(1)}, bf16[256,128]{1,0:T(8,128)(2,1)S(1)}, u32[]{:S(2)}, u32[]{:S(2)}) collective-permute-start(bf16[256,128]{1,0:T(8,128)(2,1)S(1)} %get-tuple-element.39), channel_id=1, source_target_pairs={{24,0},{32,8},{40,16},{48,24},{56,32},{64,40},{72,48},{80,56},{88,... | collective-permute-start | bytes 196616 | tf_op jit(solution)/shard_map/ppermute | solution.py:617
  66.6 0.0 collective-permute-done.10.two
  66.7 2.3 %collective-permute-done.11.three = bf16[1136,128]{1,0:T(8,128)(2,1)S(1)} collective-permute-done((bf16[1136,128]{1,0:T(8,128)(2,1)S(1)}, bf16[1136,128]{1,0:T(8,128)(2,1)S(1)}, u32[]{:S(2)}, u32[]{:S(2)}) %collective-permute-start.11) | collective-permute-done | bytes 290848 | tf_op jit(solution)/shard_map/ppermute | solution.py:611
  68.9 0.0 copy-done.2
  68.9 2.5 %combine.1 = bf16[4,256,128]{2,1,0:T(8,128)(2,1)} custom-call(s32[2,3]{1,0:T(2,128)S(1)} %copy-done.2, bf16[1024,128]{1,0:T(8,128)(2,1)S(1)} %get-tuple-element.28.own, bf16[1136,128]{1,0:T(8,128)(2,1)S(1)} %collective-permute-done.9.one, bf16[1136,128]{1,0:T(8,128)(2,1)S(1)} %collective-permute-done.10.two, bf16[1136,128]{1,0:T(8,128)(2,1)S(1)} %collective-permute-done.11.three), custom_call_target="tpu_custom_call" | custom-call | tf_op jit(solution)/shard_map/combine/pallas_call | solution.py:378
  71.4 4.1 %all-to-all-start.1 = ((bf16[4,256,128]{2,1,0:T(8,128)(2,1)}), bf16[4,256,128]{2,1,0:T(8,128)(2,1)S(1)}, u32[]{:S(2)}, u32[]{:S(2)}) async-start(bf16[4,256,128]{2,1,0:T(8,128)(2,1)} %combine.1), calls=%async_computation.1 | async-start | bytes 524288 | tf_op jit(solution)/shard_map/all_to_all | solution.py:620
  75.6 0.0 copy-done.4
  75.6 2.4 %tables.1 = (f32[1024,64]{1,0:T(8,128)S(1)}, f32[1024,64]{1,0:T(8,128)S(1)}, f32[1024,64]{1,0:T(8,128)S(1)}) custom-call(s32[2,3]{1,0:T(2,128)S(1)} %copy-done.2, bf16[112,128]{1,0:T(8,128)(2,1)S(1)} %get-tuple-element.35.own, bf16[1136,128]{1,0:T(8,128)(2,1)S(1)} %collective-permute-done.9.one, bf16[1136,128]{1,0:T(8,128)(2,1)S(1)} %collective-permute-done.10.two, ...), custom_call_target="tpu_custom_call" | custom-call | flops 268435456 | bytes 3145728 | tf_op jit(solution)/shard_map/tables/pallas_call | solution.py:556
  78.0 0.0 collective-permute-done.6.one
  78.0 0.0 collective-permute-done.7.two
  78.0 0.0 collective-permute-done.8.three
  78.0 3.1 %all-to-all-done.1.others = bf16[4,256,128]{2,1,0:T(8,128)(2,1)S(1)} async-done(((bf16[4,256,128]{2,1,0:T(8,128)(2,1)}), bf16[4,256,128]{2,1,0:T(8,128)(2,1)S(1)}, u32[]{:S(2)}, u32[]{:S(2)}) %all-to-all-start.1) | async-done | bytes 262176 | tf_op jit(solution)/shard_map/all_to_all | solution.py:620
  81.1 1.7 %energy.1 = f32[8,8,128]{2,1,0:T(8,128)S(1)} custom-call(s32[2,3]{1,0:T(2,128)S(1)} %copy-done.2, f32[256,128]{1,0:T(8,128)S(1)} %slice_bitcast_fusion.own, bf16[256,128]{1,0:T(8,128)(2,1)S(1)} %collective-permute-done.6.one, bf16[256,128]{1,0:T(8,128)(2,1)S(1)} %collective-permute-done.7.two, bf16[256,128]{1,0:T(8,128)(2,1)S(1)} %collective-permute-done.8.three, ...), custom_call_target="tpu_custom_call" | custom-call | tf_op jit(solution)/shard_map/energy/pallas_call | solution.py:452
  82.8 11.3 %all_to_all.15 = f32[8,8,128]{2,1,0:T(8,128)S(1)} all-to-all(f32[8,8,128]{2,1,0:T(8,128)S(1)} %energy.1), channel_id=1, replica_groups=mesh['trip'=64,'virt'=8] {'virt'}, dimensions={0} | all-to-all | bytes 65536 | tf_op jit(solution)/shard_map/all_to_all | solution.py:624
  94.1 0.6 reduce_sum.9
  (3 shorter events, 0.1 us)
Async XLA Ops:
  0.0 0.7 copy-start.1
  1.9 21.9 %collective-permute-start = (bf16[2,144,256]{2,1,0:T(8,128)(2,1)S(1)}, bf16[2,144,256]{2,1,0:T(8,128)(2,1)S(1)}, u32[]{:S(2)}, u32[]{:S(2)}) collective-permute-start(bf16[2,144,256]{2,1,0:T(8,128)(2,1)S(1)} %get-tuple-element.22), channel_id=1, source_target_pairs={{8,0},{16,8},{24,16},{32,24},{40,32},{48,40},{56,48},{64,56},{72,6... | collective-permute-start | bytes 442376 | tf_op jit(solution)/shard_map/ppermute | solution.py:586
  4.0 19.8 %collective-permute-start.2 = (bf16[2,144,256]{2,1,0:T(8,128)(2,1)S(1)}, bf16[2,144,256]{2,1,0:T(8,128)(2,1)S(1)}, u32[]{:S(2)}, u32[]{:S(2)}) collective-permute-start(bf16[2,144,256]{2,1,0:T(8,128)(2,1)S(1)} %get-tuple-element.24), channel_id=1, source_target_pairs={{0,8},{8,16},{16,24},{24,32},{32,40},{40,48},{48,56},{56,64},{64,7... | collective-permute-start | bytes 442376 | tf_op jit(solution)/shard_map/ppermute | solution.py:587
  7.2 16.6 %collective-permute-start.3 = (bf16[2,144,256]{2,1,0:T(8,128)(2,1)S(1)}, bf16[2,144,256]{2,1,0:T(8,128)(2,1)S(1)}, u32[]{:S(2)}, u32[]{:S(2)}) collective-permute-start(bf16[2,144,256]{2,1,0:T(8,128)(2,1)S(1)} %get-tuple-element.25), channel_id=1, source_target_pairs={{0,16},{8,24},{16,32},{24,40},{32,48},{40,56},{48,64},{56,72},{64,... | collective-permute-start | bytes 442376 | tf_op jit(solution)/shard_map/ppermute | solution.py:585
  14.2 9.6 %collective-permute-start.4 = (bf16[2,144,256]{2,1,0:T(8,128)(2,1)S(1)}, bf16[2,144,256]{2,1,0:T(8,128)(2,1)S(1)}, u32[]{:S(2)}, u32[]{:S(2)}) collective-permute-start(bf16[2,144,256]{2,1,0:T(8,128)(2,1)S(1)} %get-tuple-element.26), channel_id=1, source_target_pairs={{0,24},{8,32},{16,40},{24,48},{32,56},{40,64},{48,72},{56,80},{64,... | collective-permute-start | bytes 442376 | tf_op jit(solution)/shard_map/ppermute | solution.py:588
  16.6 7.2 %collective-permute-start.1 = (bf16[144,256]{1,0:T(8,128)(2,1)S(1)}, bf16[144,256]{1,0:T(8,128)(2,1)S(1)}, u32[]{:S(2)}, u32[]{:S(2)}) collective-permute-start(bf16[144,256]{1,0:T(8,128)(2,1)S(1)} %get-tuple-element.23), channel_id=1, source_target_pairs={{16,0},{24,8},{32,16},{40,24},{48,32},{56,40},{64,48},{72,56},{80,... | collective-permute-start | bytes 221192 | tf_op jit(solution)/shard_map/ppermute | solution.py:584
  27.1 8.2 %collective-permute-start.5 = (bf16[2,16,256,128]{3,2,1,0:T(8,128)(2,1)S(1)}, bf16[2,16,256,128]{3,2,1,0:T(8,128)(2,1)S(1)}, u32[]{:S(2)}, u32[]{:S(2)}) collective-permute-start(bf16[2,16,256,128]{3,2,1,0:T(8,128)(2,1)S(1)} %terms.3), channel_id=1, source_target_pairs={{0,1},{1,0},{2,3},{3,2},{4,5},{5,4},{6,7},{7,6},{8,9},{9,8},{10,11... | collective-permute-start | bytes 6291464 | tf_op jit(solution)/shard_map/ppermute | solution.py:596
  32.0 3.3 %copy-start = (bf16[1,3,4096]{2,1,0:T(4,128)(2,1)S(1)}, bf16[1,3,4096]{2,1,0:T(4,128)(2,1)}, u32[]{:S(2)}) copy-start(bf16[1,3,4096]{2,1,0:T(4,128)(2,1)} %param.13) | copy-start | bytes 73732
  32.0 3.3 %copy-start.3 = (bf16[1,64]{1,0:T(2,128)(2,1)S(1)}, bf16[1,64]{1,0:T(2,128)(2,1)}, u32[]{:S(2)}) copy-start(bf16[1,64]{1,0:T(2,128)(2,1)} %singles.1) | copy-start | bytes 388
  36.9 32.0 %copy-start.2 = (s32[2,3]{1,0:T(2,128)S(1)}, s32[2,3]{1,0:T(2,128)}, u32[]{:S(2)}) copy-start(s32[2,3]{1,0:T(2,128)} %triples.11) | copy-start | bytes 76
  36.9 19.1 %all-to-all-start = ((bf16[16,256,128]{2,1,0:T(8,128)(2,1)}), bf16[16,256,128]{2,1,0:T(8,128)(2,1)S(1)}, u32[]{:S(2)}, u32[]{:S(2)}) async-start(bf16[16,256,128]{2,1,0:T(8,128)(2,1)} %bitcast.6), calls=%async_computation | async-start | bytes 2097152 | tf_op jit(solution)/shard_map/all_to_all | solution.py:609
  41.2 23.5 %collective-permute-start.9 = (bf16[1136,128]{1,0:T(8,128)(2,1)}, bf16[1136,128]{1,0:T(8,128)(2,1)S(1)}, u32[]{:S(2)}, u32[]{:S(2)}) collective-permute-start(bf16[1136,128]{1,0:T(8,128)(2,1)} %get-tuple-element.29), channel_id=1, source_target_pairs={{8,0},{16,8},{24,16},{32,24},{40,32},{48,40},{56,48},{64,56},{72,6... | collective-permute-start | bytes 872456 | tf_op jit(solution)/shard_map/ppermute | solution.py:611
  45.1 21.5 %collective-permute-start.10 = (bf16[1136,128]{1,0:T(8,128)(2,1)}, bf16[1136,128]{1,0:T(8,128)(2,1)S(1)}, u32[]{:S(2)}, u32[]{:S(2)}) collective-permute-start(bf16[1136,128]{1,0:T(8,128)(2,1)} %get-tuple-element.30), channel_id=1, source_target_pairs={{16,0},{24,8},{32,16},{40,24},{48,32},{56,40},{64,48},{72,56},{80,... | collective-permute-start | bytes 872456 | tf_op jit(solution)/shard_map/ppermute | solution.py:611
  49.1 26.5 %copy-start.4 = (f32[64]{0:T(128)S(1)}, f32[64]{0:T(128)}, u32[]{:S(2)}) copy-start(f32[64]{0:T(128)} %param.16) | copy-start | bytes 772
  49.1 19.8 %collective-permute-start.11 = (bf16[1136,128]{1,0:T(8,128)(2,1)S(1)}, bf16[1136,128]{1,0:T(8,128)(2,1)S(1)}, u32[]{:S(2)}, u32[]{:S(2)}) collective-permute-start(bf16[1136,128]{1,0:T(8,128)(2,1)S(1)} %get-tuple-element.31), channel_id=1, source_target_pairs={{24,0},{32,8},{40,16},{48,24},{56,32},{64,40},{72,48},{80,56},{88,... | collective-permute-start | bytes 872456 | tf_op jit(solution)/shard_map/ppermute | solution.py:611
  56.8 21.2 %collective-permute-start.6 = (bf16[256,128]{1,0:T(8,128)(2,1)}, bf16[256,128]{1,0:T(8,128)(2,1)S(1)}, u32[]{:S(2)}, u32[]{:S(2)}) collective-permute-start(bf16[256,128]{1,0:T(8,128)(2,1)} %get-tuple-element.41), channel_id=1, source_target_pairs={{8,0},{16,8},{24,16},{32,24},{40,32},{48,40},{56,48},{64,56},{72,6... | collective-permute-start | bytes 196616 | tf_op jit(solution)/shard_map/ppermute | solution.py:617
  60.7 17.3 %collective-permute-start.7 = (bf16[256,128]{1,0:T(8,128)(2,1)S(1)}, bf16[256,128]{1,0:T(8,128)(2,1)S(1)}, u32[]{:S(2)}, u32[]{:S(2)}) collective-permute-start(bf16[256,128]{1,0:T(8,128)(2,1)S(1)} %get-tuple-element.40), channel_id=1, source_target_pairs={{16,0},{24,8},{32,16},{40,24},{48,32},{56,40},{64,48},{72,56},{80,... | collective-permute-start | bytes 196616 | tf_op jit(solution)/shard_map/ppermute | solution.py:617
  64.7 13.3 %collective-permute-start.8 = (bf16[256,128]{1,0:T(8,128)(2,1)S(1)}, bf16[256,128]{1,0:T(8,128)(2,1)S(1)}, u32[]{:S(2)}, u32[]{:S(2)}) collective-permute-start(bf16[256,128]{1,0:T(8,128)(2,1)S(1)} %get-tuple-element.39), channel_id=1, source_target_pairs={{24,0},{32,8},{40,16},{48,24},{56,32},{64,40},{72,48},{80,56},{88,... | collective-permute-start | bytes 196616 | tf_op jit(solution)/shard_map/ppermute | solution.py:617
  71.4 9.7 %all-to-all-start.1 = ((bf16[4,256,128]{2,1,0:T(8,128)(2,1)}), bf16[4,256,128]{2,1,0:T(8,128)(2,1)S(1)}, u32[]{:S(2)}, u32[]{:S(2)}) async-start(bf16[4,256,128]{2,1,0:T(8,128)(2,1)} %combine.1), calls=%async_computation.1 | async-start | bytes 524288 | tf_op jit(solution)/shard_map/all_to_all | solution.py:620
